TPU v7x, 32 devices: a whole 2x2x4 slice. The times are simulated.
32 devices in a mesh: dp: 4 (over z), row: 2 (over core), col: 4 (over y, x).
Axes of the slice: x: 2, y: 2, z: 4, core: 2. Of those that a mesh axis runs over, the one named last changes fastest.
Arguments:
- tokens: bfloat16 [8192, 1024], P(('dp', 'row'), 'col'), may hold values from -6 to 6
- segment_ids: int32 [4, 2048], P('dp'), may hold values from 0 to 7, as said below
- cotangent: bfloat16 [8192, 1024], P(('dp', 'row'), 'col'), may hold values from -6 to 6
- qkv_weight: bfloat16 [1024, 3, 16, 64], P('col', None, 'row'), may hold values from -0.1875 to 0.1875
- attn_weight: bfloat16 [16, 64, 1024], P('row', None, 'col'), may hold values from -1 to 1
- in_weight: bfloat16 [1024, 2, 2624], P('col', None, 'row'), may hold values from -0.1875 to 0.1875
- out_weight: bfloat16 [2624, 1024], P('row', 'col'), may hold values from -0.125 to 0.125
- norm_gains: float32 [2, 1024], P(None, 'col'), may hold values from 0.4 to 3
- qkv_master: float32 [1024, 3, 16, 64], P(('col', 'dp'), None, 'row'), may hold values from -0.1875 to 0.1875
- attn_master: float32 [16, 64, 1024], P('row', None, ('col', 'dp')), may hold values from -0.1875 to 0.1875
- in_master: float32 [1024, 2, 2624], P(('col', 'dp'), None, 'row'), may hold values from -0.1875 to 0.1875
- out_master: float32 [2624, 1024], P('row', ('col', 'dp')), may hold values from -0.125 to 0.125
- qkv_first: float32 [1024, 3, 16, 64], P(('col', 'dp'), None, 'row'), may hold values from -0.00048828125 to 0.00048828125
- attn_first: float32 [16, 64, 1024], P('row', None, ('col', 'dp')), may hold values from -0.00048828125 to 0.00048828125
- in_first: float32 [1024, 2, 2624], P(('col', 'dp'), None, 'row'), may hold values from -0.00048828125 to 0.00048828125
- out_first: float32 [2624, 1024], P('row', ('col', 'dp')), may hold values from -0.00048828125 to 0.00048828125
- qkv_second: float32 [1024, 3, 16, 64], P(('col', 'dp'), None, 'row'), may hold values from 8.1584167e-10 to 1.3053467e-08
- attn_second: float32 [16, 64, 1024], P('row', None, ('col', 'dp')), may hold values from 3.2633668e-10 to 3.2633667e-09
- in_second: float32 [1024, 2, 2624], P(('col', 'dp'), None, 'row'), may hold values from 8.1584167e-10 to 1.3053467e-08
- out_second: float32 [2624, 1024], P('row', ('col', 'dp')), may hold values from 8.1584167e-10 to 1.3053467e-08
- gains_first: float32 [2, 1024], P(None, 'col'), may hold values from -0.00048828125 to 0.00048828125
- gains_second: float32 [2, 1024], P(None, 'col'), may hold values from 8.1584167e-10 to 1.3053467e-08
Outputs:
- layer_out: bfloat16 [8192, 1024], P(('dp', 'row'), 'col')
- input_grad: float32 [8192, 1024], P(('dp', 'row'), 'col')
- grad_norm: float32 [], replicated
- new_qkv_first: float32 [1024, 3, 16, 64], P(('col', 'dp'), None, 'row')
- new_attn_first: float32 [16, 64, 1024], P('row', None, ('col', 'dp'))
- new_in_first: float32 [1024, 2, 2624], P(('col', 'dp'), None, 'row')
- new_out_first: float32 [2624, 1024], P('row', ('col', 'dp'))
- new_qkv_second: float32 [1024, 3, 16, 64], P(('col', 'dp'), None, 'row')
- new_attn_second: float32 [16, 64, 1024], P('row', None, ('col', 'dp'))
- new_in_second: float32 [1024, 2, 2624], P(('col', 'dp'), None, 'row')
- new_out_second: float32 [2624, 1024], P('row', ('col', 'dp'))
- new_qkv_master: float32 [1024, 3, 16, 64], P(('col', 'dp'), None, 'row')
- new_attn_master: float32 [16, 64, 1024], P('row', None, ('col', 'dp'))
- new_in_master: float32 [1024, 2, 2624], P(('col', 'dp'), None, 'row')
- new_out_master: float32 [2624, 1024], P('row', ('col', 'dp'))
- new_qkv_copy: bfloat16 [1024, 3, 16, 64], P(('col', 'dp'), None, 'row')
- new_attn_copy: bfloat16 [16, 64, 1024], P('row', None, ('col', 'dp'))
- new_in_copy: bfloat16 [1024, 2, 2624], P(('col', 'dp'), None, 'row')
- new_out_copy: bfloat16 [2624, 1024], P('row', ('col', 'dp'))
- new_gains_first: float32 [2, 1024], P(None, 'col')
- new_gains_second: float32 [2, 1024], P(None, 'col')
- new_gains: float32 [2, 1024], P(None, 'col')
Inputs may be any that keep to these rules, and one draw needn't show every extreme that they name: `segment_ids`: along each sequence the ids never fall; the first position has id 0 and the last 7, and ids may skip values; the positions p with 3/8 * 2048 <= p < 5/8 * 2048 of each sequence lie in one document.
All inputs are finite; a program needn't handle non-finite values.
Results may differ from a plain program's by a relative error of at most 0.024.
Values may be sent and summed in bfloat16 or wider, within the bound.
No kernel may reach another device: no remote copies, remote signals or barrier semaphores. Data moves between devices by JAX's collectives and lax.ppermute only.
A program may use at most 192 MiB of HBM per device.

v0:
```python
import jax
import jax.numpy as jnp
from jax import lax
from jax.sharding import PartitionSpec as P

STEP = 10


NORM_EPSILON = 1e-05
ROPE_BASE = 160000.0
CLIP_NORM = 1.0
LEARN_RATE = 0.02
GAIN_RATE = 0.5
BETA_ONE = 0.9
BETA_TWO = 0.98
ADAM_EPSILON = 1e-08
WEIGHT_DECAY = 0.01
MASKED = -1e30


def column_sums(first_part, second_part):
    return lax.psum((first_part, second_part), "col")


def gather_rows(portion):
    return lax.all_gather(portion, "row", axis=0, tiled=True)


def project_in(token_rows, weight):
    portion_rows = weight.shape[2] // lax.axis_size("col")

    def partial_term(offset, amount):
        return jnp.einsum("td,dgn->ngt", token_rows, weight, preferred_element_type=jnp.float32)

    return lax.psum_scatter(
        partial_term(jnp.int32(0), portion_rows * lax.axis_size("col")),
        "col",
        scatter_dimension=0,
        tiled=True,
    )


def project_out(portion, weight, formula):
    gathered = lax.all_gather(portion, "col", axis=0, tiled=True)
    portion_rows = gathered.shape[-1] // lax.axis_size("row")

    def partial_term(offset, amount):
        return jnp.einsum(formula, gathered, weight, preferred_element_type=jnp.float32)

    return (
        lax.psum_scatter(
            partial_term(jnp.int32(0), portion_rows * lax.axis_size("row")).astype(jnp.bfloat16),
            "row",
            scatter_dimension=0,
            tiled=True,
        ).astype(jnp.float32),
        gathered,
    )


def positions(segment):
    length = segment.shape[0]
    number = jnp.arange(length, dtype=jnp.int32)
    before = jnp.concatenate([segment[:1] - 1, segment[:-1]])
    change_marks = jnp.where(segment != before, number, jnp.zeros_like(number))
    return number - lax.cummax(change_marks, axis=0)


def rope_table(place_index, head_size):
    freq_index = jnp.arange(0, head_size, 2).astype(jnp.float32)
    frequency = ROPE_BASE ** (-freq_index / head_size)
    turned = place_index.astype(jnp.float32)[None, :] * frequency[:, None]
    turned = jnp.concatenate([turned, turned], axis=0)
    return (jnp.cos(turned), jnp.sin(turned))


def rope_apply(values, cos_table, sin_table):
    half_size = values.shape[1] // 2
    turned = jnp.concatenate([-values[:, half_size:], values[:, :half_size]], axis=1)
    return values * cos_table + turned * sin_table


def rope_back(gradient, cos_table, sin_table):
    half_size = gradient.shape[1] // 2
    rotated = gradient * sin_table
    return gradient * cos_table + jnp.concatenate(
        [rotated[:, half_size:], -rotated[:, :half_size]], axis=1
    )


def normalize(values, gain_row):
    features = values.shape[1] * lax.axis_size("col")
    summed, squares = column_sums(jnp.sum(values, axis=1), jnp.sum(values * values, axis=1))
    average = summed / features
    variance = squares / features - average * average
    inverse = lax.rsqrt(variance + NORM_EPSILON)
    unit_rows = (values - average[:, None]) * inverse[:, None]
    return (unit_rows, inverse, (unit_rows * gain_row[None, :]).astype(jnp.bfloat16))


def normalize_back(gradient, unit_rows, inverse, gain_row):
    features = gradient.shape[1] * lax.axis_size("col")
    scaled = gradient * gain_row[None, :]
    summed, crossed = column_sums(jnp.sum(scaled, axis=1), jnp.sum(scaled * unit_rows, axis=1))
    grad_values = inverse[:, None] * (
        scaled - summed[:, None] / features - unit_rows * crossed[:, None] / features
    )
    return (grad_values, jnp.sum(gradient * unit_rows, axis=0))


def block_scores(query_part, key_rows, segment_part, segment, scaling):
    scores = (
        jnp.einsum("heq,hek->hqk", query_part, key_rows, preferred_element_type=jnp.float32)
        * scaling
    )
    same_doc = segment_part[:, None] == segment[None, :]
    return jnp.where(same_doc[None, :, :], scores, MASKED)


def attend(query_rows, key_rows, value_rows, segment):
    length = segment.shape[0]
    span_rows = min(512, length)
    heads_here, head_size = (query_rows.shape[0], query_rows.shape[1])
    scaling = head_size ** (-0.5)

    def one_block(number):
        offset = number * span_rows
        query_part = lax.dynamic_slice_in_dim(query_rows, offset, span_rows, 2)
        segment_part = lax.dynamic_slice_in_dim(segment, offset, span_rows, 0)
        scores = block_scores(query_part, key_rows, segment_part, segment, scaling)
        highest = jnp.max(scores, axis=-1, keepdims=True)
        exponent = jnp.exp(scores - highest)
        summed = jnp.sum(exponent, axis=-1, keepdims=True)
        weights_low = (exponent / summed).astype(jnp.bfloat16)
        mixed_part = jnp.einsum(
            "hqk,hek->heq", weights_low, value_rows, preferred_element_type=jnp.float32
        )
        return (mixed_part, (highest + jnp.log(summed))[..., 0])

    mixed_heads, log_total = lax.map(one_block, jnp.arange(length // span_rows))
    mixed_heads = jnp.moveaxis(mixed_heads, 0, 2).reshape(heads_here, head_size, length)
    log_total = jnp.moveaxis(log_total, 0, 1).reshape(heads_here, length)
    return (mixed_heads, log_total)


def attend_back(query_rows, key_rows, value_rows, segment, log_total, grad_mixed):
    length = segment.shape[0]
    span_rows = min(512, length)
    heads_here, head_size = (query_rows.shape[0], query_rows.shape[1])
    scaling = head_size ** (-0.5)

    def one_block(running, number):
        grad_keys, grad_values = running
        offset = number * span_rows
        query_part = lax.dynamic_slice_in_dim(query_rows, offset, span_rows, 2)
        segment_part = lax.dynamic_slice_in_dim(segment, offset, span_rows, 0)
        log_part = lax.dynamic_slice_in_dim(log_total, offset, span_rows, 1)
        grad_part = lax.dynamic_slice_in_dim(grad_mixed, offset, span_rows, 2)
        scores = block_scores(query_part, key_rows, segment_part, segment, scaling)
        probs_full = jnp.exp(scores - log_part[..., None])
        weights_low = probs_full.astype(jnp.bfloat16)
        grad_weights = jnp.einsum(
            "heq,hek->hqk", grad_part, value_rows, preferred_element_type=jnp.float32
        )
        inner_sum = jnp.sum(grad_weights * probs_full, axis=-1, keepdims=True)
        grad_scores = (probs_full * (grad_weights - inner_sum)).astype(jnp.bfloat16)
        grad_query = (
            jnp.einsum("hqk,hek->heq", grad_scores, key_rows, preferred_element_type=jnp.float32)
            * scaling
        )
        grad_keys = (
            grad_keys
            + jnp.einsum(
                "hqk,heq->hek", grad_scores, query_part, preferred_element_type=jnp.float32
            )
            * scaling
        )
        grad_values = grad_values + jnp.einsum(
            "hqk,heq->hek", weights_low, grad_part, preferred_element_type=jnp.float32
        )
        return ((grad_keys, grad_values), grad_query)

    zero_state = jnp.zeros((heads_here, head_size, length), jnp.float32)
    (grad_keys, grad_values), grad_query = lax.scan(
        one_block, (zero_state, zero_state), jnp.arange(length // span_rows)
    )
    grad_query = jnp.moveaxis(grad_query, 0, 2).reshape(heads_here, head_size, length)
    return (grad_query, grad_keys, grad_values)


def adam_update(master, first_moment, second, gradient, factor, decay_rate, step_rate):
    scaled = gradient * factor
    first_new = BETA_ONE * first_moment + (1.0 - BETA_ONE) * scaled
    second_new = BETA_TWO * second + (1.0 - BETA_TWO) * scaled * scaled
    first_hat = first_new / (1.0 - BETA_ONE**STEP)
    second_hat = second_new / (1.0 - BETA_TWO**STEP)
    master_new = master - step_rate * (
        first_hat / (jnp.sqrt(second_hat) + ADAM_EPSILON) + decay_rate * master
    )
    return (first_new, second_new, master_new)


def on_device(
    tokens,
    segment_ids,
    cotangent,
    qkv_weight,
    attn_weight,
    in_weight,
    out_weight,
    norm_gains,
    qkv_master,
    attn_master,
    in_master,
    out_master,
    qkv_first,
    attn_first,
    in_first,
    out_first,
    qkv_second,
    attn_second,
    in_second,
    out_second,
    gains_first,
    gains_second,
):
    segment = segment_ids[0]
    length = segment.shape[0]
    feat_here = tokens.shape[1]
    head_size = qkv_weight.shape[3]
    heads_here = qkv_weight.shape[2] // lax.axis_size("col")
    cos_table, sin_table = rope_table(positions(segment), head_size)
    qkv_flat = qkv_weight.reshape(feat_here, 3, -1)
    attn_flat = attn_weight.reshape(-1, feat_here)
    residual = tokens.astype(jnp.float32)
    first_unit, first_inverse, first_low = normalize(residual, norm_gains[0])
    first_rows = gather_rows(first_low)
    projected = project_in(first_rows, qkv_flat).reshape(heads_here, head_size, 3, length)
    query_rows = rope_apply(projected[:, :, 0], cos_table, sin_table).astype(jnp.bfloat16)
    key_rows = rope_apply(projected[:, :, 1], cos_table, sin_table).astype(jnp.bfloat16)
    value_rows = projected[:, :, 2].astype(jnp.bfloat16)
    mixed_heads, log_total = attend(query_rows, key_rows, value_rows, segment)
    mixed_low = mixed_heads.astype(jnp.bfloat16).reshape(heads_here * head_size, length)
    attn_part, mixed_rows = project_out(mixed_low, attn_flat, "nt,nd->td")
    middle = residual + attn_part
    second_unit, second_inverse, second_low = normalize(middle, norm_gains[1])
    second_rows = gather_rows(second_low)
    up_gate = project_in(second_rows, in_weight)
    hidden_full, gelu_pull = jax.vjp(
        lambda gate_part, up_part: jax.nn.gelu(gate_part, approximate=False) * up_part,
        up_gate[:, 0],
        up_gate[:, 1],
    )
    hidden = hidden_full.astype(jnp.bfloat16)
    ffn_part, hidden_rows = project_out(hidden, out_weight, "nt,nd->td")
    layer_out = (middle + ffn_part).astype(jnp.bfloat16)
    grad_rows = gather_rows(cotangent)
    grad_out_w = jnp.einsum("nt,td->nd", hidden_rows, grad_rows, preferred_element_type=jnp.float32)
    grad_hidden = project_in(grad_rows, out_weight.T[:, None, :])[:, 0]
    grad_gate, grad_up = gelu_pull(grad_hidden)
    grad_up_gate = jnp.stack([grad_gate, grad_up], axis=1).astype(jnp.bfloat16)
    grad_second, up_gate_rows = project_out(grad_up_gate, in_weight, "ngt,dgn->td")
    grad_in_w = jnp.einsum(
        "td,ngt->dgn", second_rows, up_gate_rows, preferred_element_type=jnp.float32
    )
    grad_middle, second_gain = normalize_back(
        grad_second, second_unit, second_inverse, norm_gains[1]
    )
    grad_middle = cotangent.astype(jnp.float32) + grad_middle
    middle_rows = gather_rows(grad_middle.astype(jnp.bfloat16))
    grad_attn_w = jnp.einsum(
        "nt,td->nd", mixed_rows, middle_rows, preferred_element_type=jnp.float32
    )
    grad_mixed = project_in(middle_rows, attn_flat.T[:, None, :])[:, 0]
    grad_mixed = grad_mixed.astype(jnp.bfloat16).reshape(heads_here, head_size, length)
    grad_query, grad_keys, grad_values = attend_back(
        query_rows, key_rows, value_rows, segment, log_total, grad_mixed
    )
    grad_projected = jnp.stack(
        [
            rope_back(grad_query, cos_table, sin_table),
            rope_back(grad_keys, cos_table, sin_table),
            grad_values,
        ],
        axis=2,
    )
    grad_projected = grad_projected.reshape(heads_here * head_size, 3, length).astype(jnp.bfloat16)
    grad_first, projected_rows = project_out(grad_projected, qkv_flat, "ngt,dgn->td")
    grad_qkv_w = jnp.einsum(
        "td,ngt->dgn", first_rows, projected_rows, preferred_element_type=jnp.float32
    )
    grad_input, first_gain = normalize_back(grad_first, first_unit, first_inverse, norm_gains[0])
    input_grad = grad_middle + grad_input
    reduced = (
        lax.psum_scatter(
            grad_qkv_w.astype(jnp.bfloat16), "dp", scatter_dimension=0, tiled=True
        ).astype(jnp.float32),
        lax.psum_scatter(
            grad_attn_w.astype(jnp.bfloat16), "dp", scatter_dimension=1, tiled=True
        ).astype(jnp.float32),
        lax.psum_scatter(
            grad_in_w.astype(jnp.bfloat16), "dp", scatter_dimension=0, tiled=True
        ).astype(jnp.float32),
        lax.psum_scatter(
            grad_out_w.astype(jnp.bfloat16), "dp", scatter_dimension=1, tiled=True
        ).astype(jnp.float32),
    )
    grad_qkv = reduced[0].reshape(qkv_master.shape)
    grad_attn = reduced[1].reshape(attn_master.shape)
    grad_in = reduced[2]
    grad_out = reduced[3]
    gain_part = jnp.stack([first_gain, second_gain], axis=0)
    matrix_total = sum(
        (jnp.sum(member * member) for member in (grad_qkv, grad_attn, grad_in, grad_out))
    )
    gain_grad = lax.psum(gain_part, ("dp", "row"))
    lead_device = (lax.axis_index("dp") == 0) & (lax.axis_index("row") == 0)
    own_total = matrix_total + jnp.where(
        lead_device, jnp.sum(gain_grad * gain_grad), jnp.float32(0.0)
    )
    squares = lax.psum(own_total, ("dp", "row", "col"))
    grad_norm = jnp.sqrt(squares)
    factor = CLIP_NORM / (grad_norm + 1e-06)
    qkv_new = adam_update(
        qkv_master, qkv_first, qkv_second, grad_qkv, factor, WEIGHT_DECAY, LEARN_RATE
    )
    attn_new = adam_update(
        attn_master, attn_first, attn_second, grad_attn, factor, WEIGHT_DECAY, LEARN_RATE
    )
    in_new = adam_update(in_master, in_first, in_second, grad_in, factor, WEIGHT_DECAY, LEARN_RATE)
    out_new = adam_update(
        out_master, out_first, out_second, grad_out, factor, WEIGHT_DECAY, LEARN_RATE
    )
    gains_new = adam_update(
        norm_gains, gains_first, gains_second, gain_grad, factor, 0.0, GAIN_RATE
    )
    return (
        layer_out,
        input_grad,
        grad_norm,
        qkv_new[0],
        attn_new[0],
        in_new[0],
        out_new[0],
        qkv_new[1],
        attn_new[1],
        in_new[1],
        out_new[1],
        qkv_new[2],
        attn_new[2],
        in_new[2],
        out_new[2],
        qkv_new[2].astype(jnp.bfloat16),
        attn_new[2].astype(jnp.bfloat16),
        in_new[2].astype(jnp.bfloat16),
        out_new[2].astype(jnp.bfloat16),
        gains_new[0],
        gains_new[1],
        gains_new[2],
    )


def solution(mesh):
    placed = (
        P(("dp", "row"), "col"),
        P("dp", None),
        P(("dp", "row"), "col"),
        P("col", None, "row", None),
        P("row", None, "col"),
        P("col", None, "row"),
        P("row", "col"),
        P(None, "col"),
        P(("col", "dp"), None, "row", None),
        P("row", None, ("col", "dp")),
        P(("col", "dp"), None, "row"),
        P("row", ("col", "dp")),
        P(("col", "dp"), None, "row", None),
        P("row", None, ("col", "dp")),
        P(("col", "dp"), None, "row"),
        P("row", ("col", "dp")),
        P(("col", "dp"), None, "row", None),
        P("row", None, ("col", "dp")),
        P(("col", "dp"), None, "row"),
        P("row", ("col", "dp")),
        P(None, "col"),
        P(None, "col"),
    )
    return jax.shard_map(
        on_device,
        mesh=mesh,
        in_specs=placed,
        out_specs=(
            P(("dp", "row"), "col"),
            P(("dp", "row"), "col"),
            P(),
            P(("col", "dp"), None, "row", None),
            P("row", None, ("col", "dp")),
            P(("col", "dp"), None, "row"),
            P("row", ("col", "dp")),
            P(("col", "dp"), None, "row", None),
            P("row", None, ("col", "dp")),
            P(("col", "dp"), None, "row"),
            P("row", ("col", "dp")),
            P(("col", "dp"), None, "row", None),
            P("row", None, ("col", "dp")),
            P(("col", "dp"), None, "row"),
            P("row", ("col", "dp")),
            P(("col", "dp"), None, "row", None),
            P("row", None, ("col", "dp")),
            P(("col", "dp"), None, "row"),
            P("row", ("col", "dp")),
            P(None, "col"),
            P(None, "col"),
            P(None, "col"),
        ),
        check_vma=False,
    )
```

profile of v0, /device:TPU:0, one launch (start us, length us, event | category | flops | bytes accessed | tf_op | source)
XLA Modules:
  0.0 1199.6 jit_solution(5842148244564090323)
XLA Ops:
  9.5 11.5 all-reduce.6
  23.3 8.5 all-gather.9.cloned.1.call-done
  31.8 7.6 convolution_bitcast_fusion.2
  42.9 2.6 fusion.101
  45.5 116.1 %reduce-scatter.14.cloned.1.call-done = f32[128,3,2048]{0,2,1:T(8,128)} async-done(((f32[512,3,2048]{0,2,1:T(8,128)}), f32[128,3,2048]{0,2,1:T(8,128)}) %reduce-scatter.14.cloned.1.call-update) | async-done | bytes 3145744 | tf_op jit(solution)/shard_map/reduce_scatter | solution.py:35
  161.5 3.6 copy.143
  170.6 39.9 %while.29 = (s32[]{:T(128)}, bf16[4,2,64,512]{3,2,1,0:T(8,128)(2,1)}, f32[4,2,512]{2,1,0:T(2,128)S(1)}, s32[4]{0:T(128)S(1)}, s32[2048]{0:T(1024)S(1)}, /*index=...) while((s32[]{:T(128)}, ...), condition=%wide.region_10.11_spmd.clone, body=%wide.region_7.10_spmd.sunk.clone | while | flops 563084288 | bytes 35043564 | solution.py:140
  174.6 2.5 fusion.194
  177.1 2.7 fusion.195
  187.1 2.7 fusion.195
  197.1 2.7 fusion.195
  207.1 2.7 fusion.195
  213.4 35.1 %all-gather.11.cloned.1.call-done = bf16[512,2048]{1,0:T(8,128)(2,1)} async-done(((bf16[128,2048]{1,0:T(8,128)(2,1)}), bf16[512,2048]{1,0:T(8,128)(2,1)}) %all-gather.11.cloned.1.call-update) | async-done | bytes 2097168 | tf_op jit(solution)/shard_map/all_gather | solution.py:44
  248.5 3.4 convolution_convert_fusion.1
  252.6 8.1 reduce-scatter.16.cloned.1.call-done
  262.0 10.3 all-reduce.5
  274.6 7.0 convolution_bitcast_fusion.1
  281.7 2.9 all-gather.13.cloned.1.call-done
  284.6 10.0 convolution_bitcast_fusion
  294.7 100.2 %reduce-scatter.32.cloned.1.call-done = f32[328,1,2048]{2,0,1:T(8,128)} async-done(((f32[1312,1,2048]{2,0,1:T(8,128)}), f32[328,1,2048]{2,0,1:T(8,128)}) %reduce-scatter.32.cloned.1.call-update) | async-done | bytes 2686992
  394.9 195.5 %reduce-scatter.18.cloned.1.call-done = f32[328,2,2048]{2,0,1:T(8,128)} async-done(((f32[1312,2,2048]{2,0,1:T(8,128)}), f32[328,2,2048]{2,0,1:T(8,128)}) %reduce-scatter.18.cloned.1.call-update) | async-done | bytes 5373968 | tf_op jit(solution)/shard_map/reduce_scatter | solution.py:35
  590.4 8.3 add_convert_fusion
  601.6 107.3 %all-gather.19.cloned.1.call-done = bf16[1312,2,2048]{2,0,1:T(8,128)(2,1)} async-done(((bf16[328,2,2048]{2,0,1:T(8,128)(2,1)}), bf16[1312,2,2048]{2,0,1:T(8,128)(2,1)}) %all-gather.19.cloned.1.call-update) | async-done | bytes 10747920 | tf_op jit(solution)/shard_map/all_gather | solution.py:44
  708.9 8.3 fusion.57
  717.3 8.6 reduce-scatter.22.cloned.1.call-done
  728.3 10.2 all-reduce.4
  741.2 8.2 all-gather.21.cloned.1.call-done
  749.5 4.0 convolution_bitcast_fusion.3
  755.6 2.6 copy.148
  758.2 8.2 fusion.36
  766.4 8.7 all-gather.23.cloned.1.call-start
  775.2 32.3 %reduce-scatter.24.cloned.1.call-done = f32[128,1,2048]{0,2,1:T(8,128)} async-done(((f32[512,1,2048]{0,2,1:T(8,128)}), f32[128,1,2048]{0,2,1:T(8,128)}) %reduce-scatter.24.cloned.1.call-update) | async-done | bytes 1048592 | tf_op jit(solution)/shard_map/reduce_scatter | solution.py:35
  811.6 58.6 %while.30 = (s32[]{:T(128)}, f32[2,64,2048]{2,1,0:T(8,128)S(1)}, f32[2,64,2048]{2,1,0:T(8,128)}, f32[4,2,64,512]{3,2,1,0:T(8,128)}, s32[4]{0:T(128)S(1)}, /*inde...) while((s32[]{:T(128)}, f32[2,64,2048]{2,1,0:T(8,128)S(1)}, ...), condition=%wide.region_27.28_spmd.clone.clone, body=%wide.region_25.27_spmd.clone.sunk.clone | while | flops 1376058368 | bytes 84191552 | solution.py:184
  815.0 2.6 fusion.207
  817.6 3.1 multiply_reduce_fusion.5
  820.6 2.6 multiply_convert_fusion.5
  829.6 2.6 fusion.207
  832.2 3.1 multiply_reduce_fusion.5
  835.3 2.6 multiply_convert_fusion.5
  844.3 2.6 fusion.207
  846.9 3.0 multiply_reduce_fusion.5
  849.9 2.6 multiply_convert_fusion.5
  859.0 2.6 fusion.207
  861.5 3.1 multiply_reduce_fusion.5
  864.6 2.6 multiply_convert_fusion.5
  875.4 2.5 copy.150
  880.4 4.1 copy.181
  884.5 2.8 reshape.329
  890.3 5.3 convolution_convert_fusion.2
  895.6 3.4 convolution_convert_fusion.5
  899.1 61.2 %all-gather.23.cloned.1.call-done = bf16[512,3,2048]{0,2,1:T(8,128)(2,1)} async-done(((bf16[128,3,2048]{0,2,1:T(8,128)(2,1)}), bf16[512,3,2048]{0,2,1:T(8,128)(2,1)}) %all-gather.23.cloned.1.call-update) | async-done | bytes 6291472 | tf_op jit(solution)/shard_map/all_gather | solution.py:44
  960.3 5.6 fusion.58
  965.9 7.2 fusion.32
  973.1 3.2 copy.157
  976.3 4.7 fusion.65
  983.1 5.5 convolution_convert_fusion.3
  991.6 15.6 %reduce-scatter.28.cloned.1.call-done = bf16[512,64]{0,1:T(8,128)(2,1)} async-done(((bf16[512,256]{0,1:T(8,128)(2,1)}), bf16[512,64]{0,1:T(8,128)(2,1)}) %reduce-scatter.28.cloned.1.call-update) | async-done | bytes 65552 | tf_op jit(solution)/shard_map/reduce_scatter | solution.py:298
  1008.7 8.1 reduce-scatter.26.cloned.1.call-done
  1018.6 17.6 %psum.78 = f32[2,256]{1,0:T(2,128)S(1)} all-reduce(f32[2,256]{1,0:T(2,128)S(1)} %pad_maximum_fusion.4), channel_id=1, replica_groups=mesh['dp'=4,'row'=2,'col'=4] {'dp','row'}, use_global_device_ids=true, to_apply=%region_43.44 | all-reduce | flops 512 | bytes 4096 | tf_op jit(solution)/shard_map/psum | solution.py:316
  1037.5 10.0 all-reduce.3
  1047.5 73.1 %all-reduce.10.cloned.1.call-done = (bf16[256,3,512]{2,1,0:T(4,128)(2,1)}, bf16[256,2,1312]{2,1,0:T(2,128)(2,1)}) async-done(((bf16[256,3,512]{2,1,0:T(4,128)(2,1)}, bf16[256,2,1312]{2,1,0:T(2,128)(2,1)}), (bf16[256,3,512]{2,1,0:T(4,128)(2,1)}, bf16[256,2,1312]{2,1,0:T(2,128)(2,1)})) %all-reduce.10.cloned.1.call-update) | async-done | bytes 2129936
  1127.0 3.5 reduce-scatter.20.cloned.1.call-done
  1130.5 3.9 fusion.73
  1134.4 40.4 %psum.79 = f32[]{:T(128)} all-reduce(f32[]{:T(128)S(6)} %add.225), channel_id=1, replica_groups=mesh['dp'=4,'row'=2,'col'=4] {'dp','row','col'}, use_global_device_ids=true, to_apply=%region_45.46 | all-reduce | flops 1 | bytes 8 | tf_op jit(solution)/shard_map/psum | solution.py:321
  (334 shorter events, 119.7 us)
Async XLA Ops:
  7.2 277.4 %copy-start = (bf16[256,2,1312]{0,2,1:T(8,128)(2,1)S(1)}, bf16[256,2,1312]{0,2,1:T(8,128)(2,1)}, u32[]{:S(2)}) copy-start(bf16[256,2,1312]{0,2,1:T(8,128)(2,1)} %param.31) | copy-start | bytes 4030468
  7.2 24.6 %copy-start.33 = (bf16[256,3,8,64]{0,3,2,1:T(8,128)(2,1)S(1)}, bf16[256,3,8,64]{0,3,2,1:T(8,128)(2,1)}, u32[]{:S(2)}) copy-start(bf16[256,3,8,64]{0,3,2,1:T(8,128)(2,1)} %param.29) | copy-start | bytes 2359300
  7.2 24.6 %all-gather.9.cloned.1.call-start = ((), (), s32[]{:S(2)}) async-start(), calls=%async_computation.10 | async-start | bytes 1572864 | tf_op jit(solution)/shard_map/all_gather | solution.py:26
  8.1 31.3 %copy-start.59 = (f32[1,256]{1,0:T(1,128)}, f32[1,256]{1,0:T(1,128)S(1)}, u32[]{:S(2)}) copy-start(f32[1,256]{1,0:T(1,128)S(1)} %get-tuple-element.387) | copy-start | bytes 3076
  8.1 730.5 %copy-start.57 = (f32[1,256]{1,0:T(1,128)}, f32[1,256]{1,0:T(1,128)S(1)}, u32[]{:S(2)}) copy-start(f32[1,256]{1,0:T(1,128)S(1)} %get-tuple-element.388) | copy-start | bytes 3076
  21.0 18.4 %copy-start.51 = (f32[1024]{0:T(1024)}, f32[1024]{0:T(1024)S(1)}, u32[]{:S(2)}) copy-start(f32[1024]{0:T(1024)S(1)} %get-tuple-element.385) | copy-start | bytes 12292
  21.1 18.4 %copy-start.53 = (f32[1024]{0:T(1024)}, f32[1024]{0:T(1024)S(1)}, u32[]{:S(2)}) copy-start(f32[1024]{0:T(1024)S(1)} %get-tuple-element.386) | copy-start | bytes 12292
  23.3 138.3 %reduce-scatter.14.cloned.1.call-start = ((), (), s32[]{:S(2)}) async-start(), calls=%async_computation.11 | async-start | bytes 15728640 | tf_op jit(solution)/shard_map/reduce_scatter | solution.py:35
  39.5 209.0 %all-gather.11.cloned.1.call-start = ((), (), s32[]{:S(2)}) async-start(), calls=%async_computation.12 | async-start | bytes 2621440 | tf_op jit(solution)/shard_map/all_gather | solution.py:44
  45.5 122.9 %copy-start.9 = (f32[64,2048]{1,0:T(8,128)}, f32[64,2048]{1,0:T(8,128)S(1)}, u32[]{:S(2)}) copy-start(f32[64,2048]{1,0:T(8,128)S(1)} %get-tuple-element.381) | copy-start | bytes 1572868
  210.5 41.4 %copy-start.11 = (bf16[2,64,2048]{2,1,0:T(8,128)(2,1)}, bf16[2,64,2048]{2,1,0:T(8,128)(2,1)S(1)}, u32[]{:S(2)}) copy-start(bf16[2,64,2048]{2,1,0:T(8,128)(2,1)S(1)} %get-tuple-element.693) | copy-start | bytes 1572868
  213.1 47.5 %reduce-scatter.16.cloned.1.call-start = ((), (), s32[]{:S(2)}) async-start(), calls=%async_computation.13 | async-start | bytes 1572864 | tf_op jit(solution)/shard_map/reduce_scatter | solution.py:51
  248.5 12.1 %copy-start.3 = (bf16[1024,256]{1,0:T(8,128)(2,1)S(1)}, bf16[1024,256]{1,0:T(8,128)(2,1)}, u32[]{:S(2)}) copy-start(bf16[1024,256]{1,0:T(8,128)(2,1)} %param.26) | copy-start | bytes 1572868
  251.9 22.7 %all-gather.17.cloned.1.call-start = ((), (), s32[]{:S(2)}) async-start(), calls=%async_computation.18 | async-start | bytes 1572864 | tf_op jit(solution)/shard_map/all_gather | solution.py:26
  252.5 32.1 %all-gather.13.cloned.1.call-start = ((), (), s32[]{:S(2)}) async-start(), calls=%async_computation.14 | async-start | bytes 1572864 | tf_op jit(solution)/shard_map/all_gather | solution.py:26
  272.3 466.3 %copy-start.47 = (f32[1024]{0:T(1024)}, f32[1024]{0:T(1024)S(1)}, u32[]{:S(2)}) copy-start(f32[1024]{0:T(1024)S(1)} %get-tuple-element.383) | copy-start | bytes 12292
  272.3 466.3 %copy-start.49 = (f32[1024]{0:T(1024)}, f32[1024]{0:T(1024)S(1)}, u32[]{:S(2)}) copy-start(f32[1024]{0:T(1024)S(1)} %get-tuple-element.384) | copy-start | bytes 12292
  274.5 120.4 %reduce-scatter.32.cloned.1.call-start = ((), (), s32[]{:S(2)}) async-start(), calls=%async_computation.27 | async-start | bytes 13434880
  281.6 308.8 %reduce-scatter.18.cloned.1.call-start = ((), (), s32[]{:S(2)}) async-start(), calls=%async_computation.15 | async-start | bytes 26869760 | tf_op jit(solution)/shard_map/reduce_scatter | solution.py:35
  294.7 414.3 %all-gather.19.cloned.1.call-start = ((), (), s32[]{:S(2)}) async-start(), calls=%async_computation.19 | async-start | bytes 13434880 | tf_op jit(solution)/shard_map/all_gather | solution.py:44
  590.4 8.3 copy-start.2
  590.4 8.3 copy-start.8
  601.5 124.4 %copy-start.6 = (bf16[1024,256]{1,0:T(8,128)(2,1)S(1)}, bf16[1024,256]{1,0:T(8,128)(2,1)}, u32[]{:S(2)}) copy-start(bf16[1024,256]{1,0:T(8,128)(2,1)} %reduce-scatter.16.cloned.1.call-done) | copy-start | bytes 1572868
  601.5 124.4 %reduce-scatter.22.cloned.1.call-start = ((), (), s32[]{:S(2)}) async-start(), calls=%async_computation.20 | async-start | bytes 1572864 | tf_op jit(solution)/shard_map/reduce_scatter | solution.py:51
  717.2 21.4 %copy-start.13 = (bf16[1024,256]{1,0:T(8,128)(2,1)S(1)}, bf16[1024,256]{1,0:T(8,128)(2,1)}, u32[]{:S(2)}) copy-start(bf16[1024,256]{1,0:T(8,128)(2,1)} %param.28) | copy-start | bytes 1572868
  717.2 32.2 %copy-start.42 = (bf16[8,64,256]{2,1,0:T(8,128)(2,1)S(1)}, bf16[8,64,256]{2,1,0:T(8,128)(2,1)}, u32[]{:S(2)}) copy-start(bf16[8,64,256]{2,1,0:T(8,128)(2,1)} %param.30) | copy-start | bytes 786436
  717.3 32.2 %all-gather.21.cloned.1.call-start = ((), (), s32[]{:S(2)}) async-start(), calls=%async_computation.21 | async-start | bytes 1572864 | tf_op jit(solution)/shard_map/all_gather | solution.py:26
  738.6 14.9 %copy-start.61 = (f32[1024]{0:T(1024)}, f32[1024]{0:T(1024)S(1)}, u32[]{:S(2)}) copy-start(f32[1024]{0:T(1024)S(1)} %get-tuple-element.332) | copy-start | bytes 12292
  738.6 14.9 %copy-start.55 = (f32[1024]{0:T(1024)}, f32[1024]{0:T(1024)S(1)}, u32[]{:S(2)}) copy-start(f32[1024]{0:T(1024)S(1)} %broadcast_multiply_fusion.4) | copy-start | bytes 12292
  741.2 66.3 %reduce-scatter.24.cloned.1.call-start = ((), (), s32[]{:S(2)}) async-start(), calls=%async_computation.22 | async-start | bytes 5242880 | tf_op jit(solution)/shard_map/reduce_scatter | solution.py:35
  753.5 136.7 %all-gather.15.cloned.1.call-start = ((), (), s32[]{:S(2)}) async-start(), calls=%async_computation.16 | async-start | bytes 6717440 | tf_op jit(solution)/shard_map/all_gather | solution.py:44
  766.4 45.2 %copy-start.12 = (bf16[2,64,2048]{2,1,0:T(8,128)(2,1)S(1)}, bf16[2,64,2048]{2,1,0:T(8,128)(2,1)}, u32[]{:S(2)}) copy-start(bf16[2,64,2048]{2,1,0:T(8,128)(2,1)} %copy-done.11) | copy-start | bytes 1572868
  766.4 193.9 %all-gather.23.cloned.1.call-start = ((), (), s32[]{:S(2)}) async-start(), calls=%async_computation.23 | async-start | bytes 7864320 | tf_op jit(solution)/shard_map/all_gather | solution.py:44
  880.4 6.9 copy-start.18
  890.1 5.5 copy-start.19
  890.1 99.9 %reduce-scatter.30.cloned.1.call-start = ((), (), s32[]{:S(2)}) async-start(), calls=%async_computation.26 | async-start | bytes 901120 | tf_op jit(solution)/shard_map/reduce_scatter | solution.py:304
  895.5 64.8 %copy-start.34 = (bf16[256,3,8,64]{0,3,2,1:T(8,128)(2,1)S(1)}, bf16[256,3,8,64]{0,3,2,1:T(8,128)(2,1)}, u32[]{:S(2)}) copy-start(bf16[256,3,8,64]{0,3,2,1:T(8,128)(2,1)} %param.29) | copy-start | bytes 2359300
  895.6 111.6 %reduce-scatter.28.cloned.1.call-start = ((), (), s32[]{:S(2)}) async-start(), calls=%async_computation.25 | async-start | bytes 327680 | tf_op jit(solution)/shard_map/reduce_scatter | solution.py:298
  899.1 66.9 %copy-start.20 = (bf16[2048,256]{1,0:T(8,128)(2,1)S(1)}, bf16[2048,256]{1,0:T(8,128)(2,1)}, u32[]{:S(2)}) copy-start(bf16[2048,256]{1,0:T(8,128)(2,1)} %all-gather.13.cloned.1.call-done) | copy-start | bytes 3145732
  899.1 117.7 %reduce-scatter.26.cloned.1.call-start = ((), (), s32[]{:S(2)}) async-start(), calls=%async_computation.24 | async-start | bytes 1572864 | tf_op jit(solution)/shard_map/reduce_scatter | solution.py:51
  965.9 154.7 %all-reduce.10.cloned.1.call-start = ((), (), s32[]{:S(2)}) async-start(), calls=%async_computation.28 | async-start | bytes 4980736
  982.8 5.9 copy-start.67
  982.8 34.0 %copy-start.4 = (bf16[1024,256]{1,0:T(8,128)(2,1)S(1)}, bf16[1024,256]{1,0:T(8,128)(2,1)}, u32[]{:S(2)}) copy-start(bf16[1024,256]{1,0:T(8,128)(2,1)} %param.26) | copy-start | bytes 1572868
  982.8 34.0 %copy-start.52 = (f32[1024]{0:T(1024)S(1)}, f32[1024]{0:T(1024)}, u32[]{:S(2)}) copy-start(f32[1024]{0:T(1024)} %copy-done.51) | copy-start | bytes 12292
  982.8 34.0 %copy-start.54 = (f32[1024]{0:T(1024)S(1)}, f32[1024]{0:T(1024)}, u32[]{:S(2)}) copy-start(f32[1024]{0:T(1024)} %copy-done.53) | copy-start | bytes 12292
  982.8 34.0 %copy-start.60 = (f32[1,256]{1,0:T(1,128)S(1)}, f32[1,256]{1,0:T(1,128)}, u32[]{:S(2)}) copy-start(f32[1,256]{1,0:T(1,128)} %copy-done.59) | copy-start | bytes 3076
  982.8 35.8 %copy-start.64 = (f32[256]{0:T(256)S(1)}, f32[256]{0:T(256)}, u32[]{:S(2)}) copy-start(f32[256]{0:T(256)} %get-tuple-element.278) | copy-start | bytes 3076
  982.8 147.6 %reduce-scatter.20.cloned.1.call-start = ((), (), s32[]{:S(2)}) async-start(), calls=%async_computation.17 | async-start | bytes 1572864 | tf_op jit(solution)/shard_map/reduce_scatter | solution.py:51
  988.6 141.8 %copy-start.7 = (bf16[1024,256]{1,0:T(8,128)(2,1)S(1)}, bf16[1024,256]{1,0:T(8,128)(2,1)}, u32[]{:S(2)}) copy-start(bf16[1024,256]{1,0:T(8,128)(2,1)} %reduce-scatter.16.cloned.1.call-done) | copy-start | bytes 1572868
  988.6 141.8 %copy-start.14 = (bf16[1024,256]{1,0:T(8,128)(2,1)S(1)}, bf16[1024,256]{1,0:T(8,128)(2,1)}, u32[]{:S(2)}) copy-start(bf16[1024,256]{1,0:T(8,128)(2,1)} %param.28) | copy-start | bytes 1572868
  988.6 141.8 %copy-start.15 = (bf16[1024,256]{1,0:T(8,128)(2,1)S(1)}, bf16[1024,256]{1,0:T(8,128)(2,1)}, u32[]{:S(2)}) copy-start(bf16[1024,256]{1,0:T(8,128)(2,1)} %reduce-scatter.22.cloned.1.call-done) | copy-start | bytes 1572868
  988.6 141.8 %copy-start.48 = (f32[1024]{0:T(1024)S(1)}, f32[1024]{0:T(1024)}, u32[]{:S(2)}) copy-start(f32[1024]{0:T(1024)} %copy-done.47) | copy-start | bytes 12292
  988.6 141.8 %copy-start.50 = (f32[1024]{0:T(1024)S(1)}, f32[1024]{0:T(1024)}, u32[]{:S(2)}) copy-start(f32[1024]{0:T(1024)} %copy-done.49) | copy-start | bytes 12292
  988.6 141.8 %copy-start.56 = (f32[1024]{0:T(1024)S(1)}, f32[1024]{0:T(1024)}, u32[]{:S(2)}) copy-start(f32[1024]{0:T(1024)} %copy-done.55) | copy-start | bytes 12292
  988.6 141.8 %copy-start.58 = (f32[1,256]{1,0:T(1,128)S(1)}, f32[1,256]{1,0:T(1,128)}, u32[]{:S(2)}) copy-start(f32[1,256]{1,0:T(1,128)} %copy-done.57) | copy-start | bytes 3076
  988.6 141.8 %copy-start.62 = (f32[1024]{0:T(1024)S(1)}, f32[1024]{0:T(1024)}, u32[]{:S(2)}) copy-start(f32[1024]{0:T(1024)} %copy-done.61) | copy-start | bytes 12292
  1016.8 113.7 %copy-start.22 = (bf16[1024,256]{1,0:T(8,128)(2,1)S(1)}, bf16[1024,256]{1,0:T(8,128)(2,1)}, u32[]{:S(2)}) copy-start(bf16[1024,256]{1,0:T(8,128)(2,1)} %reduce-scatter.26.cloned.1.call-done) | copy-start | bytes 1572868
  1130.5 45.1 %copy-start.46 = (bf16[512,64]{0,1:T(8,128)(2,1)S(1)}, bf16[512,64]{0,1:T(8,128)(2,1)}, u32[]{:S(2)}) copy-start(bf16[512,64]{0,1:T(8,128)(2,1)} %reduce-scatter.28.cloned.1.call-done) | copy-start | bytes 196612
  1183.1 5.5 copy-start.63
  1183.1 5.4 copy-start.65
  1183.1 6.0 copy-start.29
  1183.1 6.0 copy-start.43
  1183.2 6.0 copy-start.44
  1183.2 6.0 copy-start.45
  (38 other events, 92.1 us)
Sparse Core Ops, SparseCore 0:
  23.4 8.3 all-gather.8
  39.6 121.8 reduce-scatter.13
  213.2 35.2 all-gather.10
  252.1 8.5 reduce-scatter.15
  262.1 10.1 all-gather.16
  274.7 9.9 all-gather.12
  288.0 106.8 reduce-scatter.31
  398.3 192.0 reduce-scatter.17
  601.7 107.2 all-gather.18
  717.4 8.5 reduce-scatter.21
  741.3 8.1 all-gather.20
  753.6 53.8 reduce-scatter.23
  809.3 62.5 all-gather.14
  890.2 70.0 all-gather.22
  963.0 22.7 reduce-scatter.29
  988.5 18.6 reduce-scatter.27
  1010.0 6.7 reduce-scatter.25
  1019.1 101.4 all-reduce.9
  1122.8 7.5 reduce-scatter.19
where the time goes:
time: 1210 us; the launch traced here: 1200 us
  waiting for transfers between devices  785 us (65%)
  matrix products  130 us (11%)
  blocking collectives  99.9 us (8%)
  other arithmetic  88.2 us (7%)
  local copies, waits for them, and re-layouts  58.4 us (5%)
  between operations  21.8 us (2%)
    reduce_scatter x3, waiting for transfers between devices, project_in(): lax.psum_scatter(partial_term(jnp.int32(0), portion_rows * lax.axis_size(...  344 us
    all_gather x4, waiting for transfers between devices, project_out(): gathered = lax.all_gather(portion, 'col', axis=0, tiled=True)  204 us
    unnamed x21, waiting for transfers between devices  174 us
    psum x4, blocking collectives, column_sums(): return lax.psum((first_part, second_part), 'col')  42 us
    psum x1, blocking collectives, on_device(): squares = lax.psum(own_total, ('dp', 'row', 'col'))  40.4 us
    dot_general x4, matrix products, partial_term(): jnp.einsum('td,dgn->ngt', token_rows, weight, preferred_element_type=jnp....  28.6 us
    reduce_scatter x4, waiting for transfers between devices, project_out(): lax.psum_scatter(partial_term(jnp.int32(0), portion_rows * lax.axis_size(...  28.3 us
  transfers between devices with their start and end apart: 19, of which 16 were waited for; matrix products, arithmetic and copies ran while one was open for 14% of the time, Pallas kernels for 0%

commit v1 on v0

v1 whole, which is shorter than its diff:
```python
import functools
import math

import jax
import jax.numpy as jnp
from jax import lax
from jax.experimental import pallas as pl
from jax.experimental.pallas import tpu as pltpu
from jax.sharding import PartitionSpec as P

STEP = 10


NORM_EPSILON = 1e-05
ROPE_BASE = 160000.0
CLIP_NORM = 1.0
LEARN_RATE = 0.02
GAIN_RATE = 0.5
BETA_ONE = 0.9
BETA_TWO = 0.98
ADAM_EPSILON = 1e-08
WEIGHT_DECAY = 0.01
MASKED = -1e30

BLOCK = 256
LANES = 128
FF_PAD = 128
F32 = jnp.float32
BF16 = jnp.bfloat16

NT = (((1,), (1,)), ((), ()))
NN = (((1,), (0,)), ((), ()))
TN = (((0,), (0,)), ((), ()))


def mm(a, b, dims):
    return lax.dot_general(a, b, dims, preferred_element_type=F32)


VMEM = pl.BlockSpec(memory_space=pltpu.VMEM)
SMEM = pl.BlockSpec(memory_space=pltpu.SMEM)
PARAMS = pltpu.CompilerParams(vmem_limit_bytes=56 * 1024 * 1024)


def whole_call(body, outs, args, scratch=(), scalars=1, flops=0):
    moved = sum(a.size * a.dtype.itemsize for a in args) + sum(
        math.prod(s) * jnp.dtype(t).itemsize for s, t in outs
    )
    return pl.pallas_call(
        body,
        out_shape=[jax.ShapeDtypeStruct(s, t) for s, t in outs],
        in_specs=[SMEM] * scalars + [VMEM] * (len(args) - scalars),
        out_specs=[VMEM] * len(outs),
        scratch_shapes=list(scratch),
        compiler_params=PARAMS,
        cost_estimate=pl.CostEstimate(flops=flops, bytes_accessed=moved, transcendentals=0),
    )(*args)


def to_col(v, k):
    return lax.ppermute(v, "col", [(i, i ^ k) for i in range(4)])


def to_row(v):
    return lax.ppermute(v, "row", [(0, 1), (1, 0)])


def gather_col(v):
    half = v.shape[0] // 2
    a = to_col(v, 1)
    b = to_col(v, 2)
    d = jnp.concatenate([to_col(a[:half], 2), to_col(b[half:], 1)], axis=0)
    return [v, a, b, d]


def exchange_col(parts):
    return [parts[0]] + [to_col(parts[k], k) for k in range(1, 4)]


def sum_dp(v):
    n = lax.axis_size("dp")
    if n == 4:
        return v + sum(
            lax.ppermute(v, "dp", [(i, i ^ k) for i in range(4)]) for k in (1, 2, 3)
        )
    return lax.psum(v, "dp")


def scatter_dp(v):
    n = lax.axis_size("dp")
    if n != 4:
        return lax.psum_scatter(v, "dp", scatter_dimension=1, tiled=True).astype(F32)
    here = lax.axis_index("dp")
    rows = v.shape[1] // n
    split = v.reshape(v.shape[0], n, rows, v.shape[2])

    def piece(k):
        return lax.dynamic_index_in_dim(split, here ^ k, 1, keepdims=False)

    total = piece(0).astype(F32)
    for k in (1, 2, 3):
        total = total + lax.ppermute(piece(k), "dp", [(i, i ^ k) for i in range(4)]).astype(F32)
    return total


def natural(parts, here):
    stacked = jnp.stack(parts)
    return [lax.dynamic_index_in_dim(stacked, here ^ j, 0, keepdims=False) for j in range(4)]


def half_mask(shape):
    return lax.broadcasted_iota(jnp.int32, shape, len(shape) - 1) % LANES < 64


def swap_halves(v):
    lane = lax.broadcasted_iota(jnp.int32, v.shape, 1) % 64
    return jnp.where(lane < 32, pltpu.roll(v, LANES - 32, 1), pltpu.roll(v, 32, 1))


def moments(parts, features):
    average = sum(jnp.sum(v, axis=1, keepdims=True) for v in parts) / features
    centered = [v - average for v in parts]
    variance = sum(jnp.sum(v * v, axis=1, keepdims=True) for v in centered) / features
    inverse = lax.rsqrt(variance + NORM_EPSILON)
    return [v * inverse for v in centered], inverse


def lanes_of(ref, rows, p):
    return ref[rows, pl.ds(p * 256, 256)]


def qkv_kernel(x0, x1, x2, x3, gains, w_own, w_oth, cos, sin, own_out, oth_out, h_out):
    parts = [ref[...].astype(F32) for ref in (x0, x1, x2, x3)]
    units, _ = moments(parts, 4 * 256)
    low = [(units[k] * gains[k, 0:1, :]).astype(BF16) for k in range(4)]
    for k in range(4):
        h_out[:, k * 256 : (k + 1) * 256] = low[k]
    cos_part, sin_part = cos[...], sin[...]
    weight = [jnp.concatenate([w_own[k], w_oth[k]], axis=0) for k in range(4)]
    both = sum(mm(low[k], weight[k], NT) for k in range(4))
    for side, out in enumerate((own_out, oth_out)):
        got = both[:, side * 384 : (side + 1) * 384]
        query, key, value = got[:, :128], got[:, 128:256], got[:, 256:]
        query = (query * cos_part + swap_halves(query) * sin_part).astype(BF16)
        out[:, :128] = query * jnp.asarray(0.125, BF16)
        out[:, 128:256] = (key * cos_part + swap_halves(key) * sin_part).astype(BF16)
        out[:, 256:] = value.astype(BF16)


def run_qkv(xs, gains, w_own, w_oth, cos, sin):
    rows = xs[0].shape[0]
    step = 256
    whole = lambda shape: pl.BlockSpec(shape, lambda i: (0,) * len(shape))
    block = lambda n: pl.BlockSpec((step, n), lambda i: (i, 0))
    return pl.pallas_call(
        qkv_kernel,
        grid=(rows // step,),
        in_specs=[block(256)] * 4
        + [whole(gains.shape), whole(w_own.shape), whole(w_oth.shape), block(128), block(128)],
        out_specs=[block(384), block(384), block(1024)],
        out_shape=[
            jax.ShapeDtypeStruct((rows, 384), BF16),
            jax.ShapeDtypeStruct((rows, 384), BF16),
            jax.ShapeDtypeStruct((rows, 1024), BF16),
        ],
        compiler_params=PARAMS,
        cost_estimate=pl.CostEstimate(
            flops=2 * rows * 1024 * 768, bytes_accessed=8 * 1024 * 1024, transcendentals=0
        ),
    )(*xs, gains, w_own, w_oth, cos, sin)


def to_columns(row):
    return jnp.transpose(jnp.broadcast_to(row, (LANES, row.shape[1])))


def attend_kernel(info, own, recv, seg, own_out, oth_out, lse_out, qkv, score, mixed):
    length = qkv.shape[0]
    rows = length // 2
    here = info[4, 0]
    qkv[pl.ds(pl.multiple_of(here * rows, rows), rows), :] = own[...]
    qkv[pl.ds(pl.multiple_of((1 - here) * rows, rows), rows), :] = recv[...]
    low_half = half_mask((BLOCK, LANES))
    zero = jnp.zeros((BLOCK, LANES), BF16)

    def one_block(qb, _):
        at = pl.multiple_of(qb * BLOCK, BLOCK)
        query = qkv[pl.ds(at, BLOCK), :128]
        pair = jnp.concatenate(
            [jnp.where(low_half, query, zero), jnp.where(low_half, zero, query)], axis=0
        )
        low_block, high_block = info[0, qb], info[1, qb]
        q_first, q_last = info[2, qb], info[3, qb]

        def scores(kb, highest):
            k_at = pl.multiple_of(kb * BLOCK, BLOCK)
            key = qkv[pl.ds(k_at, BLOCK), 128:256]
            got = mm(pair, key, NT)
            inside = (info[2, kb] == q_last) & (info[3, kb] == q_first)

            @pl.when(inside)
            def _():
                score[:, pl.ds(k_at, BLOCK)] = got

            @pl.when(jnp.logical_not(inside))
            def _():
                seg_q = to_columns(seg[:, pl.ds(at, BLOCK)])
                seg_k = seg[:, pl.ds(k_at, BLOCK)]
                same = jnp.concatenate([seg_q, seg_q], axis=1) == seg_k
                score[:, pl.ds(k_at, BLOCK)] = jnp.where(
                    jnp.concatenate([same, same], axis=0), got, MASKED
                )

            got = score[:, pl.ds(k_at, BLOCK)]
            return jnp.maximum(highest, jnp.maximum(got[:, :128], got[:, 128:]))

        highest = lax.fori_loop(
            low_block, high_block, scores, jnp.full((2 * BLOCK, LANES), MASKED, F32)
        )
        highest = jnp.broadcast_to(jnp.max(highest, axis=1, keepdims=True), (2 * BLOCK, LANES))
        wide = jnp.concatenate([highest, highest], axis=1)

        def values(kb, carry):
            total, mixing = carry
            k_at = pl.multiple_of(kb * BLOCK, BLOCK)
            value = qkv[pl.ds(k_at, BLOCK), 256:]
            weight = jnp.exp(score[:, pl.ds(k_at, BLOCK)] - wide)
            total = total + weight[:, :128] + weight[:, 128:]
            return total, mixing + mm(weight.astype(BF16), value, NN)

        zeros = jnp.zeros((2 * BLOCK, LANES), F32)
        total, mixing = lax.fori_loop(low_block, high_block, values, (zeros, zeros))
        total = jnp.broadcast_to(jnp.sum(total, axis=1, keepdims=True), (2 * BLOCK, LANES))
        mixing = mixing / total
        lse = highest + jnp.log(total)
        mixed[pl.ds(at, BLOCK), :] = jnp.where(low_half, mixing[:BLOCK], mixing[BLOCK:]).astype(
            BF16
        )
        lse_t = jnp.transpose(jnp.where(low_half, lse[:BLOCK], lse[BLOCK:]))
        lse_out[0:1, pl.ds(at, BLOCK)] = lse_t[0:1, :]
        lse_out[1:2, pl.ds(at, BLOCK)] = lse_t[64:65, :]
        return 0

    lax.fori_loop(0, length // BLOCK, one_block, 0)
    own_out[...] = mixed[pl.ds(pl.multiple_of(here * rows, rows), rows), :]
    oth_out[...] = mixed[pl.ds(pl.multiple_of((1 - here) * rows, rows), rows), :]


def attend_back_kernel(
    info, own, recv, seg, lse, mix_own, mix_oth, dm_own, dm_recv, cos, sin,
    own_out, oth_out, qkv, dmix, dsum, dquery, dout,
):
    length = qkv.shape[0]
    rows = length // 2
    here = info[4, 0]
    mine = pl.ds(pl.multiple_of(here * rows, rows), rows)
    other = pl.ds(pl.multiple_of((1 - here) * rows, rows), rows)
    qkv[mine, :] = own[...]
    qkv[other, :] = recv[...]
    dmix[mine, :] = dm_own[...]
    dmix[other, :] = dm_recv[...]
    dquery[mine, :] = mix_own[...].astype(F32)
    dquery[other, :] = mix_oth[...].astype(F32)
    blocks = length // BLOCK

    def inner(qb, _):
        at = pl.multiple_of(qb * BLOCK, BLOCK)
        product = jnp.transpose(dmix[pl.ds(at, BLOCK), :].astype(F32) * dquery[pl.ds(at, BLOCK), :])
        dsum[0:1, pl.ds(at, BLOCK)] = jnp.sum(product[:64], axis=0, keepdims=True)
        dsum[1:2, pl.ds(at, BLOCK)] = jnp.sum(product[64:], axis=0, keepdims=True)
        dquery[pl.ds(at, BLOCK), :] = jnp.zeros((BLOCK, LANES), F32)
        return 0

    lax.fori_loop(0, blocks, inner, 0)
    low_half = half_mask((BLOCK, LANES))
    zero = jnp.zeros((BLOCK, LANES), BF16)

    def both(v):
        return jnp.concatenate([jnp.where(low_half, v, zero), jnp.where(low_half, zero, v)], axis=0)

    def one_block(kb, _):
        k_at = pl.multiple_of(kb * BLOCK, BLOCK)
        key_pair = both(qkv[pl.ds(k_at, BLOCK), 128:256])
        value_pair = both(qkv[pl.ds(k_at, BLOCK), 256:])
        k_first, k_last = info[2, kb], info[3, kb]
        seg_k = to_columns(seg[:, pl.ds(k_at, BLOCK)])
        seg_k = jnp.concatenate([seg_k, seg_k], axis=1)
        zeros = jnp.zeros((2 * BLOCK, LANES), F32)

        def rows_of(ref, at):
            return jnp.concatenate(
                [
                    jnp.broadcast_to(ref[0:1, pl.ds(at, BLOCK)], (BLOCK, BLOCK)),
                    jnp.broadcast_to(ref[1:2, pl.ds(at, BLOCK)], (BLOCK, BLOCK)),
                ],
                axis=0,
            )

        def step(qb, carry):
            dkey, dvalue = carry
            at = pl.multiple_of(qb * BLOCK, BLOCK)
            query = qkv[pl.ds(at, BLOCK), :128]
            grad = dmix[pl.ds(at, BLOCK), :]
            got = mm(key_pair, query, NT) - rows_of(lse, at)
            inside = (info[2, qb] == k_last) & (info[3, qb] == k_first)
            same = seg_k == seg[:, pl.ds(at, BLOCK)]
            same = jnp.logical_or(jnp.concatenate([same, same], axis=0), inside)
            weight = jnp.where(same, jnp.exp(got), 0.0)
            dweight = mm(value_pair, grad, NT)
            dscore = (weight * (dweight - rows_of(dsum, at))).astype(BF16)
            dvalue = dvalue + mm(weight.astype(BF16), grad, NN)
            dkey = dkey + mm(dscore, query, NN)
            dquery[pl.ds(at, BLOCK), :] += mm(dscore, key_pair, TN)
            return dkey, dvalue

        dkey, dvalue = lax.fori_loop(info[0, kb], info[1, kb], step, (zeros, zeros))
        dkey = jnp.where(low_half, dkey[:BLOCK], dkey[BLOCK:])
        dvalue = jnp.where(low_half, dvalue[:BLOCK], dvalue[BLOCK:])
        cos_part, sin_part = cos[pl.ds(k_at, BLOCK), :], sin[pl.ds(k_at, BLOCK), :]
        dkey = dkey * cos_part - swap_halves(dkey) * sin_part
        dout[pl.ds(k_at, BLOCK), 128:256] = dkey.astype(BF16)
        dout[pl.ds(k_at, BLOCK), 256:] = dvalue.astype(BF16)
        return 0

    lax.fori_loop(0, blocks, one_block, 0)

    def finish(qb, _):
        at = pl.multiple_of(qb * BLOCK, BLOCK)
        cos_part, sin_part = cos[pl.ds(at, BLOCK), :], sin[pl.ds(at, BLOCK), :]
        grad = dquery[pl.ds(at, BLOCK), :] * 0.125
        grad = grad * cos_part - swap_halves(grad) * sin_part
        dout[pl.ds(at, BLOCK), :128] = grad.astype(BF16)
        return 0

    lax.fori_loop(0, blocks, finish, 0)
    own_out[...] = dout[mine, :]
    oth_out[...] = dout[other, :]


def slot_rows(info, k):
    return pl.ds(pl.multiple_of((info[4, 1] ^ k) * 256, 256), 256)


def attn_out_kernel(info, mix_own, mix_oth, w_own, w_oth, *outs):
    for k in range(4):
        rows = slot_rows(info, k)
        mix = jnp.concatenate([mix_own[rows, :], mix_oth[rows, :]], axis=1)
        for p in range(4):
            weight = jnp.concatenate([w_own[k ^ p, :128], w_oth[k ^ p, :128]], axis=0)
            outs[k][:, p * 256 : (p + 1) * 256] = mm(mix, weight, NN).astype(BF16)


def middle_kernel(info, x0, x1, x2, x3, p0, p1, p2, p3, out):
    rows = slot_rows(info, 0)
    for p, x in enumerate((x0, x1, x2, x3)):
        at = slice(p * 256, (p + 1) * 256)
        total = x[rows, :].astype(F32)
        for part in (p0, p1, p2, p3):
            total = total + part[:, at].astype(F32)
        out[:, at] = total.astype(BF16)


def ffn_kernel(
    index, m0, m1, m2, m3, d0, d1, d2, d3, gains, w_own, w_oth,
    f0, f1, f2, f3, g0, g1, g2, g3, h_out, hid_out, dug_out, mid_out, mid,
):
    slot = pl.program_id(0)
    for k, part in enumerate((m0, m1, m2, m3)):

        @pl.when(slot == k)
        def _(k=k, part=part):
            for p in range(4):
                mid[:, p * 256 : (p + 1) * 256] = part[:, (k ^ p) * 256 : ((k ^ p) + 1) * 256]

    parts = [mid[:, p * 256 : (p + 1) * 256].astype(F32) for p in range(4)]
    mid_out[...] = mid[:, :256]
    units, _ = moments(parts, 4 * 256)
    low = [(units[p] * gains[p, 1:2, :]).astype(BF16) for p in range(4)]
    for p in range(4):
        h_out[:, p * 256 : (p + 1) * 256] = low[p]
    grads = [ref[...] for ref in (d0, d1, d2, d3)]

    def weight(p, first):
        return jnp.concatenate(
            [w_own[p, first : first + 384], w_oth[p, first : first + 384]], axis=0
        )

    gate = sum(mm(low[p], weight(p, 128), NT) for p in range(4))
    up = sum(mm(low[p], weight(p, 512), NT) for p in range(4))
    dhidden = sum(mm(grads[p], weight(p, 896), NT) for p in range(4))
    phi = 0.5 * (1.0 + lax.erf(gate * (2.0**-0.5)))
    density = jnp.exp(-0.5 * gate * gate) * ((2.0 * math.pi) ** -0.5)
    act = gate * phi
    hidden = (act * up).astype(BF16)
    dgate = (dhidden * up * (phi + gate * density)).astype(BF16)
    dup = (dhidden * act).astype(BF16)
    hid_out[...] = hidden
    dug_out[:, :384] = dgate[:, :384]
    dug_out[:, 384:768] = dup[:, :384]
    dug_out[:, 768:1152] = dgate[:, 384:]
    dug_out[:, 1152:] = dup[:, 384:]
    for p, out in enumerate((f0, f1, f2, f3)):
        out[...] = mm(hidden, weight(p, 896), NN).astype(BF16)
    back = [
        (mm(dgate, weight(p, 128), NN) + mm(dup, weight(p, 512), NN)).astype(BF16)
        for p in range(4)
    ]
    for k, out in enumerate((g0, g1, g2, g3)):

        @pl.when(slot == k)
        def _(k=k, out=out):
            for p in range(4):
                out[:, p * 256 : (p + 1) * 256] = back[k ^ p]


def run_ffn(index, mids, grads, gains, w_own, w_oth):
    rows = grads[0].shape[0]
    whole = lambda shape: pl.BlockSpec(shape, lambda i, s: (0,) * len(shape))
    block = lambda n: pl.BlockSpec((256, n), lambda i, s: (i ^ s[0], 0))
    shape = lambda r, n: jax.ShapeDtypeStruct((r, n), BF16)
    return pl.pallas_call(
        ffn_kernel,
        grid_spec=pltpu.PrefetchScalarGridSpec(
            num_scalar_prefetch=1,
            grid=(4,),
            in_specs=[whole((256, 1024))] * 4
            + [block(256)] * 4
            + [whole(gains.shape), whole(w_own.shape), whole(w_oth.shape)],
            out_specs=[block(256)] * 4
            + [whole((256, 1024))] * 4
            + [block(1024), block(768), block(1536), block(256)],
            scratch_shapes=[pltpu.VMEM((256, 1024), BF16)],
        ),
        out_shape=[shape(rows, 256)] * 4
        + [shape(256, 1024)] * 4
        + [shape(rows, 1024), shape(rows, 768), shape(rows, 1536), shape(rows, 256)],
        compiler_params=PARAMS,
        cost_estimate=pl.CostEstimate(
            flops=12 * rows * 1024 * 768, bytes_accessed=24 * 1024 * 1024, transcendentals=0
        ),
    )(index, *mids, *grads, gains, w_own, w_oth)


def norm_back(grads, units, inverse, gains):
    scaled = [g * w for g, w in zip(grads, gains)]
    first = sum(jnp.sum(v, axis=1, keepdims=True) for v in scaled) / 1024
    second = sum(jnp.sum(v * u, axis=1, keepdims=True) for v, u in zip(scaled, units)) / 1024
    return [inverse * (v - first - u * second) for v, u in zip(scaled, units)]


def middle_back_kernel(info, mid, p0, p1, p2, p3, d0, d1, d2, d3, gains, dx_out, dz_out, gain_out):
    rows = slot_rows(info, 0)
    at = [slice(p * 256, (p + 1) * 256) for p in range(4)]
    units, inverse = moments([mid[:, a].astype(F32) for a in at], 1024)
    grads = [sum(part[:, a].astype(F32) for part in (p0, p1, p2, p3)) for a in at]
    back = norm_back(grads, units, inverse, [gains[p, 1:2, :] for p in range(4)])
    for p, dy in enumerate((d0, d1, d2, d3)):
        total = back[p] + dy[rows, :].astype(F32)
        dx_out[:, at[p]] = total
        dz_out[:, at[p]] = total.astype(BF16)
        gain_out[p : p + 1, :] = jnp.sum(grads[p] * units[p], axis=0, keepdims=True)


def mixed_back_kernel(info, z0, z1, z2, z3, w_own, w_oth, own_out, oth_out, dz_out):
    for k, part in enumerate((z0, z1, z2, z3)):
        rows = slot_rows(info, k)
        total = None
        for p in range(4):
            piece = part[:, (k ^ p) * 256 : ((k ^ p) + 1) * 256]
            dz_out[rows, p * 256 : (p + 1) * 256] = piece
            weight = jnp.concatenate([w_own[p, :128], w_oth[p, :128]], axis=0)
            term = mm(piece, weight, NT)
            total = term if total is None else total + term
        own_out[rows, :] = total[:, :128].astype(BF16)
        oth_out[rows, :] = total[:, 128:].astype(BF16)


def input_back_kernel(info, d_own, d_oth, w_own, w_oth, h, gains, o0, o1, o2, o3, gain_out):
    sums = [None] * 4
    for k, out in enumerate((o0, o1, o2, o3)):
        rows = slot_rows(info, k)
        grad = jnp.concatenate([d_own[rows, :], d_oth[rows, :]], axis=1)
        for p in range(4):
            weight = jnp.concatenate([w_own[p], w_oth[p]], axis=0)
            got = mm(grad, weight, NN)
            out[:, (k ^ p) * 256 : ((k ^ p) + 1) * 256] = got.astype(BF16)
            part = jnp.sum(got * h[rows, p * 256 : (p + 1) * 256].astype(F32), axis=0, keepdims=True)
            sums[p] = part if sums[p] is None else sums[p] + part
    for p in range(4):
        gain_out[p : p + 1, :] = sums[p] / gains[p, 0:1, :]


def input_grad_kernel(info, x0, x1, x2, x3, p0, p1, p2, p3, dx, gains, o0, o1, o2, o3):
    rows = slot_rows(info, 0)
    at = [slice(p * 256, (p + 1) * 256) for p in range(4)]
    units, inverse = moments([x[rows, :].astype(F32) for x in (x0, x1, x2, x3)], 1024)
    grads = [sum(part[:, a].astype(F32) for part in (p0, p1, p2, p3)) for a in at]
    back = norm_back(grads, units, inverse, [gains[p, 0:1, :] for p in range(4)])
    for p, out in enumerate((o0, o1, o2, o3)):
        out[...] = (back[p] + dx[:, at[p]]).astype(BF16)


def adam_update(master, first_moment, second, gradient, factor, decay_rate, step_rate):
    scaled = gradient * factor
    first_new = BETA_ONE * first_moment + (1.0 - BETA_ONE) * scaled
    second_new = BETA_TWO * second + (1.0 - BETA_TWO) * scaled * scaled
    first_hat = first_new / (1.0 - BETA_ONE**STEP)
    second_hat = second_new / (1.0 - BETA_TWO**STEP)
    master_new = master - step_rate * (
        first_hat / (jnp.sqrt(second_hat) + ADAM_EPSILON) + decay_rate * master
    )
    return (first_new, second_new, master_new)


def positions(segment):
    length = segment.shape[0]
    number = jnp.arange(length, dtype=jnp.int32)
    before = jnp.concatenate([segment[:1] - 1, segment[:-1]])
    change_marks = jnp.where(segment != before, number, jnp.zeros_like(number))
    return number - lax.cummax(change_marks, axis=0)


def rope_tables(place):
    lane = jnp.arange(LANES) % 64
    frequency = ROPE_BASE ** (-(2.0 * (lane % 32).astype(F32)) / 64)
    turned = place.astype(F32)[:, None] * frequency[None, :]
    sign = jnp.where(lane < 32, -1.0, 1.0)
    return jnp.cos(turned), jnp.sin(turned) * sign[None, :]


def on_device(
    tokens, segment_ids, cotangent, qkv_weight, attn_weight, in_weight, out_weight, norm_gains,
    qkv_master, attn_master, in_master, out_master,
    qkv_first, attn_first, in_first, out_first,
    qkv_second, attn_second, in_second, out_second,
    gains_first, gains_second,
):
    col, row = lax.axis_index("col"), lax.axis_index("row")
    segment = segment_ids[0]
    length = segment.shape[0]
    rows = length // 2
    blocks = length // BLOCK
    ff_here = in_weight.shape[2] // 4
    ff_pad = -ff_here % FF_PAD
    ff_wide = ff_here + ff_pad

    qkv_t = jnp.transpose(qkv_weight, (1, 2, 3, 0))
    attn_t = attn_weight.reshape(4, LANES, 256)
    in_t = jnp.transpose(in_weight, (1, 2, 0)).reshape(2, 4, ff_here, 256)
    out_t = out_weight.reshape(4, ff_here, 256)

    def qkv_piece(k):
        return lax.dynamic_slice_in_dim(qkv_t, 2 * (col ^ k), 2, 1).reshape(3 * LANES, 256)

    def rest_piece(k):
        j = col ^ k
        inner = lax.dynamic_index_in_dim(in_t, j, 1, keepdims=False)
        return jnp.concatenate(
            [
                lax.dynamic_index_in_dim(attn_t, j, 0, keepdims=False),
                inner[0],
                inner[1],
                lax.dynamic_index_in_dim(out_t, j, 0, keepdims=False),
            ],
            axis=0,
        )

    xs = gather_col(tokens)
    gains = jnp.stack(exchange_col([norm_gains] * 4))
    wq_own = jnp.stack(exchange_col([qkv_piece(k) for k in range(4)]))
    wq_oth = to_row(wq_own)
    dys = gather_col(cotangent)
    rest = exchange_col([rest_piece(k) for k in range(4)])
    fill = jnp.zeros((ff_pad, 256), BF16)

    def padded(v):
        pieces = [v[:LANES]]
        for i in range(3):
            at = LANES + i * ff_here
            pieces += [v[at : at + ff_here], fill]
        return jnp.concatenate(pieces, axis=0)

    wr_own = jnp.stack([padded(v) for v in rest])
    wr_oth = to_row(wr_own)

    first = segment[::BLOCK]
    last = segment[BLOCK - 1 :: BLOCK]
    low = jnp.sum((segment[None, :] < first[:, None]).astype(jnp.int32), axis=1) // BLOCK
    high = (
        jnp.sum((segment[None, :] <= last[:, None]).astype(jnp.int32), axis=1) + BLOCK - 1
    ) // BLOCK
    place_here = jnp.zeros((blocks,), jnp.int32).at[0].set(row).at[1].set(col)
    info = jnp.stack([low, high, first, last, place_here])
    seg_row = segment_ids.astype(F32)
    cos, sin = rope_tables(positions(segment))
    cos_here = lax.dynamic_slice_in_dim(cos, row * rows, rows, 0)
    sin_here = lax.dynamic_slice_in_dim(sin, row * rows, rows, 0)

    own, oth, h1 = run_qkv(xs, gains, wq_own, wq_oth, cos_here, sin_here)
    recv = to_row(oth)
    h1_recv = to_row(h1)
    dense = 4 * length * length * LANES
    mix_own, mix_away, lse = whole_call(
        attend_kernel,
        [((rows, LANES), BF16), ((rows, LANES), BF16), ((2, length), F32)],
        (info, own, recv, seg_row),
        [
            pltpu.VMEM((length, 384), BF16),
            pltpu.VMEM((2 * BLOCK, length), F32),
            pltpu.VMEM((length, LANES), BF16),
        ],
        flops=4 * dense,
    )
    mix_oth = to_row(mix_away)
    parts = whole_call(
        attn_out_kernel,
        [((256, 1024), BF16)] * 4,
        (info, mix_own, mix_oth, wr_own, wr_oth),
        flops=2 * rows * 256 * 1024,
    )
    parts = exchange_col(parts)
    (middle,) = whole_call(middle_kernel, [((256, 1024), BF16)], (info, *xs, *parts))
    mids = gather_col(middle)
    index = jnp.reshape(col, (1,))
    ffn = run_ffn(index, mids, dys, gains, wr_own, wr_oth)
    forward, backward = ffn[:4], ffn[4:8]
    h2, hidden, dug, mid_here = ffn[8:]
    backward = exchange_col(backward)
    dx_mid, dz, gain_two = whole_call(
        middle_back_kernel,
        [((256, 1024), F32), ((256, 1024), BF16), ((4, 256), F32)],
        (info, middle, *backward, *dys, gains),
    )
    dzs = gather_col(dz)

    dy_all = jnp.concatenate(dys, axis=1)
    grad_in = mm(h2, dug, TN).astype(BF16)
    grad_out = mm(dy_all, hidden, TN).astype(BF16)
    ffn_own = jnp.concatenate([grad_in[:, : 2 * ff_wide], grad_out[:, :ff_wide]], axis=1)
    ffn_oth = jnp.concatenate([grad_in[:, 2 * ff_wide :], grad_out[:, ff_wide:]], axis=1)
    ffn_sum = (ffn_own.astype(F32) + to_row(ffn_oth).astype(F32)).astype(BF16)
    ffn_grad = lax.psum_scatter(
        ffn_sum.reshape(4, 256, 3 * ff_wide), "dp", scatter_dimension=1, tiled=True
    ).astype(F32)

    forward = exchange_col(forward)
    layer_out = (mid_here.astype(F32) + sum(v.astype(F32) for v in forward)).astype(BF16)

    dm_own, dm_away, dz_here = whole_call(
        mixed_back_kernel,
        [((rows, LANES), BF16), ((rows, LANES), BF16), ((rows, 1024), BF16)],
        (info, *dzs, wr_own, wr_oth),
        flops=2 * rows * 256 * 1024,
    )
    dm_recv = to_row(dm_away)
    dq_own, dq_away = whole_call(
        attend_back_kernel,
        [((rows, 384), BF16), ((rows, 384), BF16)],
        (info, own, recv, seg_row, lse, mix_own, mix_away, dm_own, dm_recv, cos, sin),
        [
            pltpu.VMEM((length, 384), BF16),
            pltpu.VMEM((length, LANES), BF16),
            pltpu.VMEM((2, length), F32),
            pltpu.VMEM((length, LANES), F32),
            pltpu.VMEM((length, 384), BF16),
        ],
        flops=10 * dense,
    )
    dq_oth = to_row(dq_away)

    attn_both = mm(dz_here, jnp.concatenate([mix_own, mix_oth], axis=1), TN)
    attn_sum = (attn_both[:, :LANES] + to_row(attn_both[:, LANES:].astype(BF16)).astype(F32)).astype(
        BF16
    )
    qkv_sum = (mm(h1, dq_own, TN) + mm(h1_recv, dq_away, TN)).astype(BF16)
    tail = jnp.concatenate([qkv_sum, attn_sum], axis=1).reshape(4, 256, 512)
    tail_grad = scatter_dp(tail)

    *partial_first, gain_one = whole_call(
        input_back_kernel,
        [((256, 1024), BF16)] * 4 + [((4, 256), F32)],
        (info, dq_own, dq_oth, wq_own, wq_oth, h1, gains),
        flops=2 * rows * 768 * 1024,
    )
    partial_first = exchange_col(partial_first)
    pieces = whole_call(
        input_grad_kernel,
        [((256, 256), BF16)] * 4,
        (info, *xs, *partial_first, dx_mid, gains),
    )
    input_grad = jnp.concatenate(natural(exchange_col(pieces), col), axis=0).astype(F32)

    gain_part = jnp.stack([gain_one, gain_two], axis=1)
    gain_grad = sum(exchange_col([gain_part[k] for k in range(4)]))
    gain_grad = sum_dp(gain_grad)
    gain_grad = gain_grad + to_row(gain_grad)
    lead_device = (lax.axis_index("dp") == 0) & (row == 0)
    total = (
        jnp.sum(ffn_grad * ffn_grad)
        + jnp.sum(tail_grad * tail_grad)
        + jnp.where(lead_device, jnp.sum(gain_grad * gain_grad), 0.0)
    )
    total = jnp.full((8, LANES), total)
    total = sum_dp(total)
    total = sum(exchange_col([total] * 4))
    total = total + to_row(total)
    grad_norm = jnp.sqrt(total[0, 0])
    factor = CLIP_NORM / (grad_norm + 1e-06)

    shard = tail_grad.shape[1]
    tail_low = tail_grad.astype(BF16)
    tail_nat = natural(exchange_col([tail_low[k] for k in range(4)]), col)
    grad_qkv = jnp.stack(
        [v[:, : 3 * LANES].reshape(shard, 3, 2, 64) for v in tail_nat], axis=2
    ).reshape(qkv_master.shape)
    grad_attn = jnp.concatenate([v[:, 3 * LANES :] for v in tail_nat], axis=1).T.reshape(
        attn_master.shape
    )
    ffn_low = ffn_grad.astype(BF16)
    ffn_nat = natural(exchange_col([ffn_low[k] for k in range(4)]), col)
    grad_in = jnp.stack(
        [
            jnp.concatenate([v[:, i * ff_wide : i * ff_wide + ff_here] for v in ffn_nat], axis=1)
            for i in range(2)
        ],
        axis=1,
    )
    grad_out = jnp.concatenate(
        [v[:, 2 * ff_wide : 2 * ff_wide + ff_here] for v in ffn_nat], axis=1
    ).T

    grad_qkv, grad_attn, grad_in, grad_out = (
        v.astype(F32) for v in (grad_qkv, grad_attn, grad_in, grad_out)
    )
    qkv_new = adam_update(
        qkv_master, qkv_first, qkv_second, grad_qkv, factor, WEIGHT_DECAY, LEARN_RATE
    )
    attn_new = adam_update(
        attn_master, attn_first, attn_second, grad_attn, factor, WEIGHT_DECAY, LEARN_RATE
    )
    in_new = adam_update(in_master, in_first, in_second, grad_in, factor, WEIGHT_DECAY, LEARN_RATE)
    out_new = adam_update(
        out_master, out_first, out_second, grad_out, factor, WEIGHT_DECAY, LEARN_RATE
    )
    gains_new = adam_update(
        norm_gains, gains_first, gains_second, gain_grad, factor, 0.0, GAIN_RATE
    )
    return (
        layer_out, input_grad, grad_norm,
        qkv_new[0], attn_new[0], in_new[0], out_new[0],
        qkv_new[1], attn_new[1], in_new[1], out_new[1],
        qkv_new[2], attn_new[2], in_new[2], out_new[2],
        qkv_new[2].astype(BF16), attn_new[2].astype(BF16),
        in_new[2].astype(BF16), out_new[2].astype(BF16),
        gains_new[0], gains_new[1], gains_new[2],
    )


def solution(mesh):
    activations = P(("dp", "row"), "col")
    gains = P(None, "col")
    weights = (
        P("col", None, "row", None), P("row", None, "col"), P("col", None, "row"), P("row", "col"),
    )
    states = (
        P(("col", "dp"), None, "row", None), P("row", None, ("col", "dp")),
        P(("col", "dp"), None, "row"), P("row", ("col", "dp")),
    )
    return jax.shard_map(
        on_device,
        mesh=mesh,
        in_specs=(activations, P("dp", None), activations, *weights, gains)
        + states * 3
        + (gains, gains),
        out_specs=(activations, activations, P()) + states * 4 + (gains, gains, gains),
        check_vma=False,
    )
```

time: 1210 us -> 481 us (0.40)
  waiting for transfers between devices: 785 us -> 177 us
  matrix products: 130 us -> 14 us
  Pallas kernels: 0 us -> 115 us
  blocking collectives: 99.9 us -> 0 us
  starting transfers between devices: 9.98 us -> 85.2 us
  other arithmetic: 88.2 us -> 38.2 us
  local copies, waits for them, and re-layouts: 58.4 us -> 28.1 us
    reduce_scatter x9 -> x1, waiting for transfers between devices: 388 us -> 0.02 us  [on_device(): lax.psum_scatter(ffn_sum.reshape(4, 256, 3 * ff_wide), 'dp', scatter_dime...]
    all_gather x8 -> x0, waiting for transfers between devices: 223 us -> none  [the longest x4 204 us: project_out(): gathered = lax.all_gather(portion, 'col', axis=0, tiled=True)]
    ppermute x0 -> x72, waiting for transfers between devices: none -> 177 us  [the longest x52 149 us: to_col(): return lax.ppermute(v, 'col', [(i, i ^ k) for i in range(4)])]
    unnamed x21 -> x1, waiting for transfers between devices: 174 us -> 0.02 us
    dot_general x40 -> x5, matrix products: 130 us -> 14 us  [mm(): return lax.dot_general(a, b, dims, preferred_element_type=F32)]
    pallas_call x0 -> x10, Pallas kernels: none -> 115 us  [the longest x8 88.7 us: whole_call(): pl.pallas_call(body, out_shape=[jax.ShapeDtypeStruct(s, t) for s, t in ou...]
    psum x6 -> x0, blocking collectives: 99.9 us -> none  [the longest x4 42 us: column_sums(): return lax.psum((first_part, second_part), 'col')]
    ppermute x0 -> x72, starting transfers between devices: none -> 85.2 us  [the longest x52 61.1 us: to_col(): return lax.ppermute(v, 'col', [(i, i ^ k) for i in range(4)])]
  transfers between devices with their start and end apart: 19 -> 73, of which waited for: 16 -> 36; matrix products, arithmetic and copies ran while one was open for 14% -> 11% of each run, Pallas kernels for 0% -> 19%
where the time goes in v1:
time: 481 us; the launch traced here: 478 us
  waiting for transfers between devices  177 us (37%)
  Pallas kernels  115 us (24%)
  starting transfers between devices  85.2 us (18%)
  other arithmetic  38.2 us (8%)
  local copies, waits for them, and re-layouts  28.1 us (6%)
  between operations  20.2 us (4%)
  matrix products  14 us (3%)
    ppermute x52, waiting for transfers between devices, to_col(): return lax.ppermute(v, 'col', [(i, i ^ k) for i in range(4)])  149 us
    pallas_call x8, Pallas kernels, whole_call(): pl.pallas_call(body, out_shape=[jax.ShapeDtypeStruct(s, t) for s, t in ou...  88.7 us
    ppermute x52, starting transfers between devices, to_col(): return lax.ppermute(v, 'col', [(i, i ^ k) for i in range(4)])  61.1 us
    pallas_call x1, Pallas kernels, run_ffn(): pl.pallas_call(ffn_kernel, grid_spec=pltpu.PrefetchScalarGridSpec(num_sca...  18.9 us
    ppermute x3, waiting for transfers between devices, scatter_dp(): lax.ppermute(piece(k), 'dp', [(i, i ^ k) for i in range(4)]).astype(F32)  18 us
    dot_general x5, matrix products, mm(): return lax.dot_general(a, b, dims, preferred_element_type=F32)  14 us
    unnamed x144, local copies, waits for them, and re-layouts  13.1 us
    ppermute x3, starting transfers between devices, scatter_dp(): lax.ppermute(piece(k), 'dp', [(i, i ^ k) for i in range(4)]).astype(F32)  11.7 us
  transfers between devices with their start and end apart: 73, of which 36 were waited for; matrix products, arithmetic and copies ran while one was open for 11% of the time, Pallas kernels for 19%

profile of v1, /device:TPU:0, one launch (start us, length us, event | category | flops | bytes accessed | tf_op | source)
XLA Modules:
  0.0 478.2 jit_solution(3079793167614197306)
XLA Ops:
  7.3 3.0 collective-permute-start
  10.3 2.0 constant_dynamic-slice_fusion.5
  13.9 1.9 collective-permute-start.7
  17.9 1.5 collective-permute-start.15
  22.4 6.6 %collective-permute-done.9 = bf16[384,256]{1,0:T(8,128)(2,1)} collective-permute-done((bf16[384,256]{1,0:T(8,128)(2,1)}, bf16[384,256]{1,0:T(8,128)(2,1)}, u32[]{:S(2)}, u32[]{:S(2)}) %collective-permute-start.9) | collective-permute-done | bytes 196640 | tf_op jit(solution)/shard_map/ppermute | solution.py:61
  29.1 2.9 collective-permute-start.6
  32.0 1.8 collective-permute-start.14
  33.8 2.1 pad_maximum_fusion.3.w_own
  35.9 8.5 %collective-permute-done.15 = bf16[1112,256]{1,0:T(8,128)(2,1)} collective-permute-done((bf16[1112,256]{1,0:T(8,128)(2,1)}, bf16[1112,256]{1,0:T(8,128)(2,1)}, u32[]{:S(2)}, u32[]{:S(2)}) %collective-permute-start.15) | collective-permute-done | bytes 569376 | tf_op jit(solution)/shard_map/ppermute | solution.py:61
  47.9 17.5 %collective-permute-done.14 = bf16[1112,256]{1,0:T(8,128)(2,1)S(1)} collective-permute-done((bf16[1112,256]{1,0:T(8,128)(2,1)S(1)}, bf16[1112,256]{1,0:T(8,128)(2,1)S(1)}, u32[]{:S(2)}, u32[]{:S(2)}) %collective-permute-start.14) | collective-permute-done | bytes 569376 | tf_op jit(solution)/shard_map/ppermute | solution.py:61
  67.5 5.5 %fusion.11 = (f32[2048,128]{1,0:T(8,128)}, f32[2048,128]{1,0:T(8,128)}) fusion(f32[128]{0:T(128)S(1)} %get-tuple-element.345, f32[128]{0:T(128)S(1)} %get-tuple-element.346, f32[2048]{0:T(1024)S(1)} %fusion.29), kind=kLoop, calls=%fused_computation.19 | loop fusion | flops 524288 | bytes 2106368 | tf_op jit(solution)/shard_map/mul | solution.py:528
  73.7 1.5 collective-permute-start.2
  75.2 1.9 constant_dynamic-slice_fusion.1.cos
  78.1 1.6 collective-permute-start.4
  82.4 4.9 %collective-permute-done.3 = bf16[512,256]{1,0:T(8,128)(2,1)S(1)} collective-permute-done((bf16[512,256]{1,0:T(8,128)(2,1)S(1)}, bf16[512,256]{1,0:T(8,128)(2,1)S(1)}, u32[]{:S(2)}, u32[]{:S(2)}) %collective-permute-start.3) | collective-permute-done | bytes 262176 | tf_op jit(solution)/shard_map/ppermute | solution.py:61
  88.1 7.5 %shard_map.381 = (bf16[1024,384]{1,0:T(8,128)(2,1)}, bf16[1024,384]{1,0:T(8,128)(2,1)}, bf16[1024,1024]{1,0:T(8,128)(2,1)}) custom-call(bf16[1024,256]{1,0:T(8,128)(2,1)} %x0.5, bf16[1024,256]{1,0:T(8,128)(2,1)} %copy-done.1, bf16[1024,256]{1,0:T(8,128)(2,1)} %collective-permute-done.1.x2, bf16[1024,256]{1,0:T(8,128)(2,1)} %copy-done.2, ...), custom_call_target="tpu_custom_call" | custom-call | flops 1610612736 | bytes 8388608 | tf_op jit(solution)/shard_map/pallas_call | solution.py:155
  98.2 30.1 %shard_map.382 = (bf16[1024,128]{1,0:T(8,128)(2,1)}, bf16[1024,128]{1,0:T(8,128)(2,1)}, f32[2,2048]{1,0:T(2,128)}) custom-call(s32[5,8]{1,0:T(8,128)} %stack.122.info, bf16[1024,384]{1,0:T(8,128)(2,1)} %get-tuple-element.85.own, bf16[1024,384]{1,0:T(8,128)(2,1)} %collective-permute-done.11.recv, f32[1,2048]{1,0:T(1,128)} %convert_element_type.123.seg), custom_call_target="tpu_custom_call" | custom-call | flops 8589934592 | bytes 2121888 | tf_op jit(solution)/shard_map/pallas_call | solution.py:49
  128.4 1.6 collective-permute-done.12.mix_oth
  130.7 4.4 shard_map.383
  136.2 2.4 collective-permute-start.19
  139.7 10.4 %collective-permute-done.17.p1 = bf16[256,1024]{1,0:T(8,128)(2,1)S(1)} collective-permute-done((bf16[256,1024]{1,0:T(8,128)(2,1)}, bf16[256,1024]{1,0:T(8,128)(2,1)S(1)}, u32[]{:S(2)}, u32[]{:S(2)}) %collective-permute-start.17) | collective-permute-done | bytes 524320 | tf_op jit(solution)/shard_map/ppermute | solution.py:61
  150.1 11.8 %collective-permute-done.18.p2 = bf16[256,1024]{1,0:T(8,128)(2,1)S(1)} collective-permute-done((bf16[256,1024]{1,0:T(8,128)(2,1)}, bf16[256,1024]{1,0:T(8,128)(2,1)S(1)}, u32[]{:S(2)}, u32[]{:S(2)}) %collective-permute-start.18) | collective-permute-done | bytes 524320 | tf_op jit(solution)/shard_map/ppermute | solution.py:61
  162.9 3.3 shard_map.384.m0.mid
  168.2 4.5 collective-permute-done.24.d1
  174.7 9.6 %collective-permute-done.21.m2 = bf16[256,1024]{1,0:T(8,128)(2,1)S(1)} collective-permute-done((bf16[256,1024]{1,0:T(8,128)(2,1)}, bf16[256,1024]{1,0:T(8,128)(2,1)S(1)}, u32[]{:S(2)}, u32[]{:S(2)}) %collective-permute-start.21) | collective-permute-done | bytes 524320 | tf_op jit(solution)/shard_map/ppermute | solution.py:61
  184.4 1.6 collective-permute-start.23
  186.6 3.4 collective-permute-done.26
  190.1 4.2 collective-permute-done.23
  195.4 18.9 %shard_map.385 = (bf16[1024,256]{1,0:T(8,128)(2,1)}, bf16[1024,256]{1,0:T(8,128)(2,1)}, bf16[1024,256]{1,0:T(8,128)(2,1)}, bf16[1024,256]{1,0:T(8,128)(2,1)}, bf...) custom-call(s32[1]{0:T(128)} %bitcast.index, ...), custom_call_target="tpu_custom_call" | custom-call | flops 9663676416 | bytes 25165824 | tf_op jit(solution)/shard_map/pallas_call | solution.py:421
  214.3 3.7 fusion.8
  218.2 1.7 copy-done.56
  219.9 4.0 convolution_convert_fusion
  224.2 1.6 pad_maximum_fusion.1
  227.8 1.5 collective-permute-start.33
  229.3 11.2 %collective-permute-done.31.p1 = bf16[256,1024]{1,0:T(8,128)(2,1)S(1)} collective-permute-done((bf16[256,1024]{1,0:T(8,128)(2,1)S(1)}, bf16[256,1024]{1,0:T(8,128)(2,1)S(1)}, u32[]{:S(2)}, u32[]{:S(2)}) %collective-permute-start.31) | collective-permute-done | bytes 524320 | tf_op jit(solution)/shard_map/ppermute | solution.py:61
  240.5 12.1 %collective-permute-done.32.p2 = bf16[256,1024]{1,0:T(8,128)(2,1)S(1)} collective-permute-done((bf16[256,1024]{1,0:T(8,128)(2,1)S(1)}, bf16[256,1024]{1,0:T(8,128)(2,1)S(1)}, u32[]{:S(2)}, u32[]{:S(2)}) %collective-permute-start.32) | collective-permute-done | bytes 524320 | tf_op jit(solution)/shard_map/ppermute | solution.py:61
  253.6 4.6 shard_map.386
  259.7 11.9 %collective-permute-done.35.z2 = bf16[256,1024]{1,0:T(8,128)(2,1)S(1)} collective-permute-done((bf16[256,1024]{1,0:T(8,128)(2,1)}, bf16[256,1024]{1,0:T(8,128)(2,1)S(1)}, u32[]{:S(2)}, u32[]{:S(2)}) %collective-permute-start.35) | collective-permute-done | bytes 524320 | tf_op jit(solution)/shard_map/ppermute | solution.py:61
  275.1 1.6 collective-permute-start.30
  276.7 3.7 collective-permute-done.37
  280.3 12.4 %collective-permute-done.36 = bf16[128,1024]{1,0:T(8,128)(2,1)} collective-permute-done((bf16[128,1024]{1,0:T(8,128)(2,1)}, bf16[128,1024]{1,0:T(8,128)(2,1)}, u32[]{:S(2)}, u32[]{:S(2)}) %collective-permute-start.36) | collective-permute-done | bytes 262176 | tf_op jit(solution)/shard_map/ppermute | solution.py:61
  292.7 1.9 pad_maximum_fusion.9.z3
  294.6 5.6 %shard_map.387 = (bf16[1024,128]{1,0:T(8,128)(2,1)}, bf16[1024,128]{1,0:T(8,128)(2,1)}, bf16[1024,1024]{1,0:T(8,128)(2,1)}) custom-call(s32[5,8]{1,0:T(8,128)} %stack.122.info, bf16[256,1024]{1,0:T(8,128)(2,1)} %get-tuple-element.103.z0, bf16[256,1024]{1,0:T(8,128)(2,1)} %copy-done.7, bf16[256,1024]{1,0:T(8,128)(2,1)} %copy-done.6, ...), custom_call_target="tpu_custom_call" | custom-call | flops 536870912 | bytes 9961632 | tf_op jit(solution)/shard_map/pallas_call | solution.py:49
  300.3 2.3 fusion.16
  303.9 3.7 add_convert_fusion
  307.6 31.0 %shard_map.388 = (bf16[1024,384]{1,0:T(8,128)(2,1)}, bf16[1024,384]{1,0:T(8,128)(2,1)}) custom-call(s32[5,8]{1,0:T(8,128)} %stack.122.info, bf16[1024,384]{1,0:T(8,128)(2,1)} %get-tuple-element.85.own, bf16[1024,384]{1,0:T(8,128)(2,1)} %collective-permute-done.11.recv, f32[1,2048]{1,0:T(1,128)} %convert_element_type.123.seg, ...), custom_call_target="tpu_custom_call" | custom-call | flops 21474836480 | bytes 6316192 | tf_op jit(solution)/shard_map/pallas_call | solution.py:49
  338.7 2.9 fusion.64
  344.7 11.0 %collective-permute-start.51 = (bf16[4,64,512]{2,1,0:T(8,128)(2,1)S(1)}, bf16[4,64,512]{2,1,0:T(8,128)(2,1)S(1)}, u32[]{:S(2)}, u32[]{:S(2)}) collective-permute-start(bf16[4,64,512]{2,1,0:T(8,128)(2,1)S(1)} %get-tuple-element.293), channel_id=1, source_target_pairs={{0,24},{8,16},{16,8},{24,0},{1,25},{9,17},{17,9},{25,1},{2,26},{10... | collective-permute-start | bytes 786440 | tf_op jit(solution)/shard_map/ppermute | solution.py:102
  356.4 5.2 %shard_map.389 = (bf16[256,1024]{1,0:T(8,128)(2,1)}, bf16[256,1024]{1,0:T(8,128)(2,1)}, bf16[256,1024]{1,0:T(8,128)(2,1)}, bf16[256,1024]{1,0:T(8,128)(2,1)}, f32[4,256]{1,0:T(4,128)}) custom-call(s32[5,8]{1,0:T(8,128)} %stack.122.info, bf16[1024,384]{1,0:T(8,128)(2,1)} %get-tuple-element.106.d_own, bf16[1024,384]{1,0:T(8,128)(2,1)} %collective-permute-done.39.d_oth, ...), custom_call_target="tpu_custom_call" | custom-call | flops 1610612736 | bytes 7352480 | tf_op jit(solution)/shard_map/pallas_call | solution.py:49
  362.5 4.1 collective-permute-done.51
  368.1 13.9 %collective-permute-done.50 = bf16[4,64,512]{2,1,0:T(8,128)(2,1)S(1)} collective-permute-done((bf16[4,64,512]{2,1,0:T(8,128)(2,1)S(1)}, bf16[4,64,512]{2,1,0:T(8,128)(2,1)S(1)}, u32[]{:S(2)}, u32[]{:S(2)}) %collective-permute-start.50) | collective-permute-done | bytes 262176 | tf_op jit(solution)/shard_map/ppermute | solution.py:102
  382.0 2.4 collective-permute-start.54
  391.6 1.5 collective-permute-start.66
  394.6 2.0 collective-permute-start.42
  398.0 2.3 add_convert_fusion.2
  400.4 3.5 collective-permute-start.55
  405.4 2.9 collective-permute-done.56
  409.1 8.1 %collective-permute-done.41.p2 = bf16[256,1024]{1,0:T(8,128)(2,1)S(1)} collective-permute-done((bf16[256,1024]{1,0:T(8,128)(2,1)}, bf16[256,1024]{1,0:T(8,128)(2,1)S(1)}, u32[]{:S(2)}, u32[]{:S(2)}) %collective-permute-start.41) | collective-permute-done | bytes 524320 | tf_op jit(solution)/shard_map/ppermute | solution.py:61
  418.2 4.3 shard_map.390
  431.1 2.0 multiply_reduce_fusion
  436.0 3.5 collective-permute-start.59
  441.1 2.9 collective-permute-done.60
  455.9 2.4 fusion.52
  466.6 1.7 fusion.49
  (349 shorter events, 89.6 us)
Async XLA Ops:
  7.2 423.9 %reduce-scatter.2.cloned.1.call-start = ((), (), s32[]{:S(2)}) async-start(), calls=%async_computation.1 | async-start | bytes 2949120 | tf_op jit(solution)/shard_map/reduce_scatter | solution.py:642
  7.3 65.7 %collective-permute-start = (bf16[1024,256]{1,0:T(8,128)(2,1)}, bf16[1024,256]{1,0:T(8,128)(2,1)S(1)}, u32[]{:S(2)}, u32[]{:S(2)}) collective-permute-start(bf16[1024,256]{1,0:T(8,128)(2,1)} %x0.5), channel_id=1, source_target_pairs={{0,1},{1,0},{2,3},{3,2},{4,5},{5,4},{6,7},{7,6},{8,9},{9,8},{10,11... | collective-permute-start | bytes 1572872 | tf_op jit(solution)/shard_map/ppermute | solution.py:61
  12.3 16.8 %collective-permute-start.9 = (bf16[384,256]{1,0:T(8,128)(2,1)}, bf16[384,256]{1,0:T(8,128)(2,1)}, u32[]{:S(2)}, u32[]{:S(2)}) collective-permute-start(bf16[384,256]{1,0:T(8,128)(2,1)} %bitcast.22), channel_id=1, source_target_pairs={{0,3},{1,2},{2,1},{3,0},{4,7},{5,6},{6,5},{7,4},{8,11},{9,10},{10,... | collective-permute-start | bytes 589832 | tf_op jit(solution)/shard_map/ppermute | solution.py:61
  13.8 15.3 %collective-permute-start.8 = (bf16[384,256]{1,0:T(8,128)(2,1)}, bf16[384,256]{1,0:T(8,128)(2,1)}, u32[]{:S(2)}, u32[]{:S(2)}) collective-permute-start(bf16[384,256]{1,0:T(8,128)(2,1)} %bitcast.19), channel_id=1, source_target_pairs={{0,2},{1,3},{2,0},{3,1},{4,6},{5,7},{6,4},{7,5},{8,10},{9,11},{10,... | collective-permute-start | bytes 589832 | tf_op jit(solution)/shard_map/ppermute | solution.py:61
  13.9 18.1 %collective-permute-start.7 = (bf16[384,256]{1,0:T(8,128)(2,1)}, bf16[384,256]{1,0:T(8,128)(2,1)}, u32[]{:S(2)}, u32[]{:S(2)}) collective-permute-start(bf16[384,256]{1,0:T(8,128)(2,1)} %bitcast.16), channel_id=1, source_target_pairs={{0,1},{1,0},{2,3},{3,2},{4,5},{5,4},{6,7},{7,6},{8,9},{9,8},{10,11... | collective-permute-start | bytes 589832 | tf_op jit(solution)/shard_map/ppermute | solution.py:61
  17.9 26.5 %collective-permute-start.15 = (bf16[1112,256]{1,0:T(8,128)(2,1)}, bf16[1112,256]{1,0:T(8,128)(2,1)}, u32[]{:S(2)}, u32[]{:S(2)}) collective-permute-start(bf16[1112,256]{1,0:T(8,128)(2,1)} %pad_maximum_fusion.7), channel_id=1, source_target_pairs={{0,3},{1,2},{2,1},{3,0},{4,7},{5,6},{6,5},{7,4},{8,11},{9,10},{10,... | collective-permute-start | bytes 1708040 | tf_op jit(solution)/shard_map/ppermute | solution.py:61
  29.1 44.6 %collective-permute-start.1 = (bf16[1024,256]{1,0:T(8,128)(2,1)}, bf16[1024,256]{1,0:T(8,128)(2,1)}, u32[]{:S(2)}, u32[]{:S(2)}) collective-permute-start(bf16[1024,256]{1,0:T(8,128)(2,1)} %x0.5), channel_id=1, source_target_pairs={{0,2},{1,3},{2,0},{3,1},{4,6},{5,7},{6,4},{7,5},{8,10},{9,11},{10,... | collective-permute-start | bytes 1572872 | tf_op jit(solution)/shard_map/ppermute | solution.py:61
  29.1 49.0 %collective-permute-start.6 = (f32[2,256]{1,0:T(2,128)S(1)}, f32[2,256]{1,0:T(2,128)S(1)}, u32[]{:S(2)}, u32[]{:S(2)}) collective-permute-start(f32[2,256]{1,0:T(2,128)S(1)} %copy-done.45), channel_id=1, source_target_pairs={{0,3},{1,2},{2,1},{3,0},{4,7},{5,6},{6,5},{7,4},{8,11},{9,10},{10,... | collective-permute-start | bytes 6152 | tf_op jit(solution)/shard_map/ppermute | solution.py:61
  32.0 33.3 %collective-permute-start.14 = (bf16[1112,256]{1,0:T(8,128)(2,1)S(1)}, bf16[1112,256]{1,0:T(8,128)(2,1)S(1)}, u32[]{:S(2)}, u32[]{:S(2)}) collective-permute-start(bf16[1112,256]{1,0:T(8,128)(2,1)S(1)} %pad_maximum_fusion.6), channel_id=1, source_target_pairs={{0,2},{1,3},{2,0},{3,1},{4,6},{5,7},{6,4},{7,5},{8,10},{9,11},{10,... | collective-permute-start | bytes 1708040 | tf_op jit(solution)/shard_map/ppermute | solution.py:61
  44.5 22.0 %collective-permute-start.13 = (bf16[1112,256]{1,0:T(8,128)(2,1)S(1)}, bf16[1112,256]{1,0:T(8,128)(2,1)S(1)}, u32[]{:S(2)}, u32[]{:S(2)}) collective-permute-start(bf16[1112,256]{1,0:T(8,128)(2,1)S(1)} %pad_maximum_fusion.5), channel_id=1, source_target_pairs={{0,1},{1,0},{2,3},{3,2},{4,5},{5,4},{6,7},{7,6},{8,9},{9,8},{10,11... | collective-permute-start | bytes 1708040 | tf_op jit(solution)/shard_map/ppermute | solution.py:61
  65.4 21.9 %collective-permute-start.10 = (bf16[4,384,256]{2,1,0:T(8,128)(2,1)}, bf16[4,384,256]{2,1,0:T(8,128)(2,1)}, u32[]{:S(2)}, u32[]{:S(2)}) collective-permute-start(bf16[4,384,256]{2,1,0:T(8,128)(2,1)} %pad_maximum_fusion.3.w_own), channel_id=1, source_target_pairs={{0,4},{4,0},{1,5},{5,1},{2,6},{6,2},{3,7},{7,3},{8,12},{12,8},{9,1... | collective-permute-start | bytes 2359304 | tf_op jit(solution)/shard_map/ppermute | solution.py:65
  66.9 63.2 %collective-permute-start.16 = (bf16[4,1280,256]{2,1,0:T(8,128)(2,1)S(1)}, bf16[4,1280,256]{2,1,0:T(8,128)(2,1)}, u32[]{:S(2)}, u32[]{:S(2)}) collective-permute-start(bf16[4,1280,256]{2,1,0:T(8,128)(2,1)S(1)} %pad_maximum_fusion.w_own), channel_id=1, source_target_pairs={{0,4},{4,0},{1,5},{5,1},{2,6},{6,2},{3,7},{7,3},{8,12},{12,8},{9,1... | collective-permute-start | bytes 7864328 | tf_op jit(solution)/shard_map/ppermute | solution.py:65
  73.0 6.6 %collective-permute-start.5 = (f32[2,256]{1,0:T(2,128)S(1)}, f32[2,256]{1,0:T(2,128)S(1)}, u32[]{:S(2)}, u32[]{:S(2)}) collective-permute-start(f32[2,256]{1,0:T(2,128)S(1)} %copy-done.45), channel_id=1, source_target_pairs={{0,2},{1,3},{2,0},{3,1},{4,6},{5,7},{6,4},{7,5},{8,10},{9,11},{10,... | collective-permute-start | bytes 6152 | tf_op jit(solution)/shard_map/ppermute | solution.py:61
  73.7 8.7 %collective-permute-start.2 = (bf16[512,256]{1,0:T(8,128)(2,1)S(1)}, bf16[512,256]{1,0:T(8,128)(2,1)S(1)}, u32[]{:S(2)}, u32[]{:S(2)}) collective-permute-start(bf16[512,256]{1,0:T(8,128)(2,1)S(1)} %slice.320), channel_id=1, source_target_pairs={{0,2},{1,3},{2,0},{3,1},{4,6},{5,7},{6,4},{7,5},{8,10},{9,11},{10,... | collective-permute-start | bytes 786440 | tf_op jit(solution)/shard_map/ppermute | solution.py:61
  79.6 7.6 %collective-permute-start.3 = (bf16[512,256]{1,0:T(8,128)(2,1)S(1)}, bf16[512,256]{1,0:T(8,128)(2,1)S(1)}, u32[]{:S(2)}, u32[]{:S(2)}) collective-permute-start(bf16[512,256]{1,0:T(8,128)(2,1)S(1)} %slice.321), channel_id=1, source_target_pairs={{0,1},{1,0},{2,3},{3,2},{4,5},{5,4},{6,7},{7,6},{8,9},{9,8},{10,11... | collective-permute-start | bytes 786440 | tf_op jit(solution)/shard_map/ppermute | solution.py:61
  135.1 15.0 %collective-permute-start.17 = (bf16[256,1024]{1,0:T(8,128)(2,1)}, bf16[256,1024]{1,0:T(8,128)(2,1)S(1)}, u32[]{:S(2)}, u32[]{:S(2)}) collective-permute-start(bf16[256,1024]{1,0:T(8,128)(2,1)} %get-tuple-element.90), channel_id=1, source_target_pairs={{0,1},{1,0},{2,3},{3,2},{4,5},{5,4},{6,7},{7,6},{8,9},{9,8},{10,11... | collective-permute-start | bytes 1572872 | tf_op jit(solution)/shard_map/ppermute | solution.py:61
  135.7 26.3 %collective-permute-start.18 = (bf16[256,1024]{1,0:T(8,128)(2,1)}, bf16[256,1024]{1,0:T(8,128)(2,1)S(1)}, u32[]{:S(2)}, u32[]{:S(2)}) collective-permute-start(bf16[256,1024]{1,0:T(8,128)(2,1)} %get-tuple-element.91), channel_id=1, source_target_pairs={{0,2},{1,3},{2,0},{3,1},{4,6},{5,7},{6,4},{7,5},{8,10},{9,11},{10,... | collective-permute-start | bytes 1572872 | tf_op jit(solution)/shard_map/ppermute | solution.py:61
  136.2 25.7 %collective-permute-start.19 = (bf16[256,1024]{1,0:T(8,128)(2,1)}, bf16[256,1024]{1,0:T(8,128)(2,1)S(1)}, u32[]{:S(2)}, u32[]{:S(2)}) collective-permute-start(bf16[256,1024]{1,0:T(8,128)(2,1)} %get-tuple-element.92), channel_id=1, source_target_pairs={{0,3},{1,2},{2,1},{3,0},{4,7},{5,6},{6,5},{7,4},{8,11},{9,10},{10,... | collective-permute-start | bytes 1572872 | tf_op jit(solution)/shard_map/ppermute | solution.py:61
  138.6 34.0 %collective-permute-start.24 = (bf16[1024,256]{1,0:T(8,128)(2,1)S(1)}, bf16[1024,256]{1,0:T(8,128)(2,1)S(1)}, u32[]{:S(2)}, u32[]{:S(2)}) collective-permute-start(bf16[1024,256]{1,0:T(8,128)(2,1)S(1)} %copy-done.23), channel_id=1, source_target_pairs={{0,1},{1,0},{2,3},{3,2},{4,5},{5,4},{6,7},{7,6},{8,9},{9,8},{10,11... | collective-permute-start | bytes 1572872 | tf_op jit(solution)/shard_map/ppermute | solution.py:61
  139.2 34.1 %collective-permute-start.25 = (bf16[1024,256]{1,0:T(8,128)(2,1)S(1)}, bf16[1024,256]{1,0:T(8,128)(2,1)S(1)}, u32[]{:S(2)}, u32[]{:S(2)}) collective-permute-start(bf16[1024,256]{1,0:T(8,128)(2,1)S(1)} %copy-done.23), channel_id=1, source_target_pairs={{0,2},{1,3},{2,0},{3,1},{4,6},{5,7},{6,4},{7,5},{8,10},{9,11},{10,... | collective-permute-start | bytes 1572872 | tf_op jit(solution)/shard_map/ppermute | solution.py:61
  166.2 18.2 %collective-permute-start.21 = (bf16[256,1024]{1,0:T(8,128)(2,1)}, bf16[256,1024]{1,0:T(8,128)(2,1)S(1)}, u32[]{:S(2)}, u32[]{:S(2)}) collective-permute-start(bf16[256,1024]{1,0:T(8,128)(2,1)} %shard_map.384.m0.mid), channel_id=1, source_target_pairs={{0,2},{1,3},{2,0},{3,1},{4,6},{5,7},{6,4},{7,5},{8,10},{9,11},{10,... | collective-permute-start | bytes 1572872 | tf_op jit(solution)/shard_map/ppermute | solution.py:61
  166.9 19.0 %collective-permute-start.20 = (bf16[256,1024]{1,0:T(8,128)(2,1)}, bf16[256,1024]{1,0:T(8,128)(2,1)S(1)}, u32[]{:S(2)}, u32[]{:S(2)}) collective-permute-start(bf16[256,1024]{1,0:T(8,128)(2,1)} %shard_map.384.m0.mid), channel_id=1, source_target_pairs={{0,1},{1,0},{2,3},{3,2},{4,5},{5,4},{6,7},{7,6},{8,9},{9,8},{10,11... | collective-permute-start | bytes 1572872 | tf_op jit(solution)/shard_map/ppermute | solution.py:61
  172.7 17.3 %collective-permute-start.26 = (bf16[512,256]{1,0:T(8,128)(2,1)S(1)}, bf16[512,256]{1,0:T(8,128)(2,1)S(1)}, u32[]{:S(2)}, u32[]{:S(2)}) collective-permute-start(bf16[512,256]{1,0:T(8,128)(2,1)S(1)} %slice.335), channel_id=1, source_target_pairs={{0,2},{1,3},{2,0},{3,1},{4,6},{5,7},{6,4},{7,5},{8,10},{9,11},{10,... | collective-permute-start | bytes 786440 | tf_op jit(solution)/shard_map/ppermute | solution.py:61
  173.2 16.8 %collective-permute-start.27 = (bf16[512,256]{1,0:T(8,128)(2,1)S(1)}, bf16[512,256]{1,0:T(8,128)(2,1)S(1)}, u32[]{:S(2)}, u32[]{:S(2)}) collective-permute-start(bf16[512,256]{1,0:T(8,128)(2,1)S(1)} %slice.336), channel_id=1, source_target_pairs={{0,1},{1,0},{2,3},{3,2},{4,5},{5,4},{6,7},{7,6},{8,9},{9,8},{10,11... | collective-permute-start | bytes 786440 | tf_op jit(solution)/shard_map/ppermute | solution.py:61
  184.4 9.9 %collective-permute-start.23 = (bf16[128,1024]{1,0:T(8,128)(2,1)S(1)}, bf16[128,1024]{1,0:T(8,128)(2,1)S(1)}, u32[]{:S(2)}, u32[]{:S(2)}) collective-permute-start(bf16[128,1024]{1,0:T(8,128)(2,1)S(1)} %slice.334), channel_id=1, source_target_pairs={{0,1},{1,0},{2,3},{3,2},{4,5},{5,4},{6,7},{7,6},{8,9},{9,8},{10,11... | collective-permute-start | bytes 786440 | tf_op jit(solution)/shard_map/ppermute | solution.py:61
  186.0 8.5 %collective-permute-start.22 = (bf16[128,1024]{1,0:T(8,128)(2,1)S(1)}, bf16[128,1024]{1,0:T(8,128)(2,1)S(1)}, u32[]{:S(2)}, u32[]{:S(2)}) collective-permute-start(bf16[128,1024]{1,0:T(8,128)(2,1)S(1)} %slice.333), channel_id=1, source_target_pairs={{0,2},{1,3},{2,0},{3,1},{4,6},{5,7},{6,4},{7,5},{8,10},{9,11},{10,... | collective-permute-start | bytes 786440 | tf_op jit(solution)/shard_map/ppermute | solution.py:61
  225.8 77.6 %collective-permute-start.46 = (bf16[1024,1152]{1,0:T(8,128)(2,1)}, bf16[1024,1152]{1,0:T(8,128)(2,1)}, u32[]{:S(2)}, u32[]{:S(2)}) collective-permute-start(bf16[1024,1152]{1,0:T(8,128)(2,1)} %pad_maximum_fusion.1), channel_id=1, source_target_pairs={{0,4},{4,0},{1,5},{5,1},{2,6},{6,2},{3,7},{7,3},{8,12},{12,8},{9,1... | collective-permute-start | bytes 7077896 | tf_op jit(solution)/shard_map/ppermute | solution.py:65
  225.8 14.7 %collective-permute-start.31 = (bf16[256,1024]{1,0:T(8,128)(2,1)S(1)}, bf16[256,1024]{1,0:T(8,128)(2,1)S(1)}, u32[]{:S(2)}, u32[]{:S(2)}) collective-permute-start(bf16[256,1024]{1,0:T(8,128)(2,1)S(1)} %copy-done.54), channel_id=1, source_target_pairs={{0,1},{1,0},{2,3},{3,2},{4,5},{5,4},{6,7},{7,6},{8,9},{9,8},{10,11... | collective-permute-start | bytes 1572872 | tf_op jit(solution)/shard_map/ppermute | solution.py:61
  227.3 25.3 %collective-permute-start.32 = (bf16[256,1024]{1,0:T(8,128)(2,1)S(1)}, bf16[256,1024]{1,0:T(8,128)(2,1)S(1)}, u32[]{:S(2)}, u32[]{:S(2)}) collective-permute-start(bf16[256,1024]{1,0:T(8,128)(2,1)S(1)} %copy-done.53), channel_id=1, source_target_pairs={{0,2},{1,3},{2,0},{3,1},{4,6},{5,7},{6,4},{7,5},{8,10},{9,11},{10,... | collective-permute-start | bytes 1572872 | tf_op jit(solution)/shard_map/ppermute | solution.py:61
  227.8 24.8 %collective-permute-start.33 = (bf16[256,1024]{1,0:T(8,128)(2,1)S(1)}, bf16[256,1024]{1,0:T(8,128)(2,1)S(1)}, u32[]{:S(2)}, u32[]{:S(2)}) collective-permute-start(bf16[256,1024]{1,0:T(8,128)(2,1)S(1)} %copy-done.52), channel_id=1, source_target_pairs={{0,3},{1,2},{2,1},{3,0},{4,7},{5,6},{6,5},{7,4},{8,11},{9,10},{10,... | collective-permute-start | bytes 1572872 | tf_op jit(solution)/shard_map/ppermute | solution.py:61
  258.2 13.4 %collective-permute-start.35 = (bf16[256,1024]{1,0:T(8,128)(2,1)}, bf16[256,1024]{1,0:T(8,128)(2,1)S(1)}, u32[]{:S(2)}, u32[]{:S(2)}) collective-permute-start(bf16[256,1024]{1,0:T(8,128)(2,1)} %get-tuple-element.103.z0), channel_id=1, source_target_pairs={{0,2},{1,3},{2,0},{3,1},{4,6},{5,7},{6,4},{7,5},{8,10},{9,11},{10,... | collective-permute-start | bytes 1572872 | tf_op jit(solution)/shard_map/ppermute | solution.py:61
  258.7 14.1 %collective-permute-start.34 = (bf16[256,1024]{1,0:T(8,128)(2,1)}, bf16[256,1024]{1,0:T(8,128)(2,1)S(1)}, u32[]{:S(2)}, u32[]{:S(2)}) collective-permute-start(bf16[256,1024]{1,0:T(8,128)(2,1)} %get-tuple-element.103.z0), channel_id=1, source_target_pairs={{0,1},{1,0},{2,3},{3,2},{4,5},{5,4},{6,7},{7,6},{8,9},{9,8},{10,11... | collective-permute-start | bytes 1572872 | tf_op jit(solution)/shard_map/ppermute | solution.py:61
  272.4 7.9 %collective-permute-start.37 = (bf16[128,1024]{1,0:T(8,128)(2,1)}, bf16[128,1024]{1,0:T(8,128)(2,1)}, u32[]{:S(2)}, u32[]{:S(2)}) collective-permute-start(bf16[128,1024]{1,0:T(8,128)(2,1)} %slice.338), channel_id=1, source_target_pairs={{0,1},{1,0},{2,3},{3,2},{4,5},{5,4},{6,7},{7,6},{8,9},{9,8},{10,11... | collective-permute-start | bytes 786440 | tf_op jit(solution)/shard_map/ppermute | solution.py:61
  273.6 19.2 %collective-permute-start.36 = (bf16[128,1024]{1,0:T(8,128)(2,1)}, bf16[128,1024]{1,0:T(8,128)(2,1)}, u32[]{:S(2)}, u32[]{:S(2)}) collective-permute-start(bf16[128,1024]{1,0:T(8,128)(2,1)} %slice.337), channel_id=1, source_target_pairs={{0,2},{1,3},{2,0},{3,1},{4,6},{5,7},{6,4},{7,5},{8,10},{9,11},{10,... | collective-permute-start | bytes 786440 | tf_op jit(solution)/shard_map/ppermute | solution.py:61
  275.1 63.7 %collective-permute-start.47 = (bf16[1024,1024]{1,0:T(8,128)(2,1)}, bf16[1024,1024]{1,0:T(8,128)(2,1)}, u32[]{:S(2)}, u32[]{:S(2)}) collective-permute-start(bf16[1024,1024]{1,0:T(8,128)(2,1)} %get-tuple-element.108.h), channel_id=1, source_target_pairs={{0,4},{4,0},{1,5},{5,1},{2,6},{6,2},{3,7},{7,3},{8,12},{12,8},{9,1... | collective-permute-start | bytes 6291464 | tf_op jit(solution)/shard_map/ppermute | solution.py:65
  275.1 116.5 %collective-permute-start.30 = (bf16[1024,256]{1,0:T(8,128)(2,1)}, bf16[1024,256]{1,0:T(8,128)(2,1)}, u32[]{:S(2)}, u32[]{:S(2)}) collective-permute-start(bf16[1024,256]{1,0:T(8,128)(2,1)} %get-tuple-element.97), channel_id=1, source_target_pairs={{0,3},{1,2},{2,1},{3,0},{4,7},{5,6},{6,5},{7,4},{8,11},{9,10},{10,... | collective-permute-start | bytes 1572872 | tf_op jit(solution)/shard_map/ppermute | solution.py:61
  280.3 112.7 %collective-permute-start.29 = (bf16[1024,256]{1,0:T(8,128)(2,1)}, bf16[1024,256]{1,0:T(8,128)(2,1)}, u32[]{:S(2)}, u32[]{:S(2)}) collective-permute-start(bf16[1024,256]{1,0:T(8,128)(2,1)} %get-tuple-element.96), channel_id=1, source_target_pairs={{0,2},{1,3},{2,0},{3,1},{4,6},{5,7},{6,4},{7,5},{8,10},{9,11},{10,... | collective-permute-start | bytes 1572872 | tf_op jit(solution)/shard_map/ppermute | solution.py:61
  300.3 7.3 %collective-permute-start.38 = (bf16[1024,128]{1,0:T(8,128)(2,1)}, bf16[1024,128]{1,0:T(8,128)(2,1)}, u32[]{:S(2)}, u32[]{:S(2)}) collective-permute-start(bf16[1024,128]{1,0:T(8,128)(2,1)} %get-tuple-element.105), channel_id=1, source_target_pairs={{0,4},{4,0},{1,5},{5,1},{2,6},{6,2},{3,7},{7,3},{8,12},{12,8},{9,1... | collective-permute-start | bytes 786440 | tf_op jit(solution)/shard_map/ppermute | solution.py:65
  303.4 38.3 %collective-permute-start.48 = (bf16[1024,128]{0,1:T(8,128)(2,1)}, bf16[1024,128]{0,1:T(8,128)(2,1)}, u32[]{:S(2)}, u32[]{:S(2)}) collective-permute-start(bf16[1024,128]{0,1:T(8,128)(2,1)} %slice.417), channel_id=1, source_target_pairs={{0,4},{4,0},{1,5},{5,1},{2,6},{6,2},{3,7},{7,3},{8,12},{12,8},{9,1... | collective-permute-start | bytes 786440 | tf_op jit(solution)/shard_map/ppermute | solution.py:65
  338.6 17.1 %collective-permute-start.39 = (bf16[1024,384]{1,0:T(8,128)(2,1)}, bf16[1024,384]{1,0:T(8,128)(2,1)}, u32[]{:S(2)}, u32[]{:S(2)}) collective-permute-start(bf16[1024,384]{1,0:T(8,128)(2,1)} %get-tuple-element.107), channel_id=1, source_target_pairs={{0,4},{4,0},{1,5},{5,1},{2,6},{6,2},{3,7},{7,3},{8,12},{12,8},{9,1... | collective-permute-start | bytes 2359304 | tf_op jit(solution)/shard_map/ppermute | solution.py:65
  344.7 21.9 %collective-permute-start.51 = (bf16[4,64,512]{2,1,0:T(8,128)(2,1)S(1)}, bf16[4,64,512]{2,1,0:T(8,128)(2,1)S(1)}, u32[]{:S(2)}, u32[]{:S(2)}) collective-permute-start(bf16[4,64,512]{2,1,0:T(8,128)(2,1)S(1)} %get-tuple-element.293), channel_id=1, source_target_pairs={{0,24},{8,16},{16,8},{24,0},{1,25},{9,17},{17,9},{25,1},{2,26},{10... | collective-permute-start | bytes 786440 | tf_op jit(solution)/shard_map/ppermute | solution.py:102
  355.8 26.2 %collective-permute-start.50 = (bf16[4,64,512]{2,1,0:T(8,128)(2,1)S(1)}, bf16[4,64,512]{2,1,0:T(8,128)(2,1)S(1)}, u32[]{:S(2)}, u32[]{:S(2)}) collective-permute-start(bf16[4,64,512]{2,1,0:T(8,128)(2,1)S(1)} %get-tuple-element.294), channel_id=1, source_target_pairs={{0,16},{8,24},{16,0},{24,8},{1,17},{9,25},{17,1},{25,9},{2,18},{10... | collective-permute-start | bytes 786440 | tf_op jit(solution)/shard_map/ppermute | solution.py:102
  355.8 28.6 %collective-permute-start.49 = (bf16[4,64,512]{2,1,0:T(8,128)(2,1)S(1)}, bf16[4,64,512]{2,1,0:T(8,128)(2,1)S(1)}, u32[]{:S(2)}, u32[]{:S(2)}) collective-permute-start(bf16[4,64,512]{2,1,0:T(8,128)(2,1)S(1)} %get-tuple-element.292), channel_id=1, source_target_pairs={{0,8},{8,0},{16,24},{24,16},{1,9},{9,1},{17,25},{25,17},{2,10},{10... | collective-permute-start | bytes 786440 | tf_op jit(solution)/shard_map/ppermute | solution.py:102
  366.6 27.0 %collective-permute-start.28 = (bf16[1024,256]{1,0:T(8,128)(2,1)S(1)}, bf16[1024,256]{1,0:T(8,128)(2,1)S(1)}, u32[]{:S(2)}, u32[]{:S(2)}) collective-permute-start(bf16[1024,256]{1,0:T(8,128)(2,1)S(1)} %copy-done.51), channel_id=1, source_target_pairs={{0,1},{1,0},{2,3},{3,2},{4,5},{5,4},{6,7},{7,6},{8,9},{9,8},{10,11... | collective-permute-start | bytes 1572872 | tf_op jit(solution)/shard_map/ppermute | solution.py:61
  388.7 5.9 %collective-permute-start.68 = (bf16[64,512]{1,0:T(8,128)(2,1)S(1)}, bf16[64,512]{1,0:T(8,128)(2,1)S(1)}, u32[]{:S(2)}, u32[]{:S(2)}) collective-permute-start(bf16[64,512]{1,0:T(8,128)(2,1)S(1)} %get-tuple-element.319), channel_id=1, source_target_pairs={{0,3},{1,2},{2,1},{3,0},{4,7},{5,6},{6,5},{7,4},{8,11},{9,10},{10,... | collective-permute-start | bytes 196616 | tf_op jit(solution)/shard_map/ppermute | solution.py:61
  390.0 6.5 %collective-permute-start.67 = (bf16[64,512]{1,0:T(8,128)(2,1)S(1)}, bf16[64,512]{1,0:T(8,128)(2,1)S(1)}, u32[]{:S(2)}, u32[]{:S(2)}) collective-permute-start(bf16[64,512]{1,0:T(8,128)(2,1)S(1)} %get-tuple-element.320), channel_id=1, source_target_pairs={{0,2},{1,3},{2,0},{3,1},{4,6},{5,7},{6,4},{7,5},{8,10},{9,11},{10,... | collective-permute-start | bytes 196616 | tf_op jit(solution)/shard_map/ppermute | solution.py:61
  391.6 8.8 %collective-permute-start.66 = (bf16[64,512]{1,0:T(8,128)(2,1)S(1)}, bf16[64,512]{1,0:T(8,128)(2,1)S(1)}, u32[]{:S(2)}, u32[]{:S(2)}) collective-permute-start(bf16[64,512]{1,0:T(8,128)(2,1)S(1)} %get-tuple-element.321), channel_id=1, source_target_pairs={{0,1},{1,0},{2,3},{3,2},{4,5},{5,4},{6,7},{7,6},{8,9},{9,8},{10,11... | collective-permute-start | bytes 196616 | tf_op jit(solution)/shard_map/ppermute | solution.py:61
  393.1 16.0 %collective-permute-start.40 = (bf16[256,1024]{1,0:T(8,128)(2,1)}, bf16[256,1024]{1,0:T(8,128)(2,1)S(1)}, u32[]{:S(2)}, u32[]{:S(2)}) collective-permute-start(bf16[256,1024]{1,0:T(8,128)(2,1)} %get-tuple-element.110), channel_id=1, source_target_pairs={{0,1},{1,0},{2,3},{3,2},{4,5},{5,4},{6,7},{7,6},{8,9},{9,8},{10,11... | collective-permute-start | bytes 1572872 | tf_op jit(solution)/shard_map/ppermute | solution.py:61
  393.7 23.5 %collective-permute-start.41 = (bf16[256,1024]{1,0:T(8,128)(2,1)}, bf16[256,1024]{1,0:T(8,128)(2,1)S(1)}, u32[]{:S(2)}, u32[]{:S(2)}) collective-permute-start(bf16[256,1024]{1,0:T(8,128)(2,1)} %get-tuple-element.111), channel_id=1, source_target_pairs={{0,2},{1,3},{2,0},{3,1},{4,6},{5,7},{6,4},{7,5},{8,10},{9,11},{10,... | collective-permute-start | bytes 1572872 | tf_op jit(solution)/shard_map/ppermute | solution.py:61
  394.6 22.6 %collective-permute-start.42 = (bf16[256,1024]{1,0:T(8,128)(2,1)}, bf16[256,1024]{1,0:T(8,128)(2,1)S(1)}, u32[]{:S(2)}, u32[]{:S(2)}) collective-permute-start(bf16[256,1024]{1,0:T(8,128)(2,1)} %get-tuple-element.112), channel_id=1, source_target_pairs={{0,3},{1,2},{2,1},{3,0},{4,7},{5,6},{6,5},{7,4},{8,11},{9,10},{10,... | collective-permute-start | bytes 1572872 | tf_op jit(solution)/shard_map/ppermute | solution.py:61
  396.6 7.3 %collective-permute-start.57 = (f32[2,256]{1,0:T(2,128)S(1)}, f32[2,256]{1,0:T(2,128)S(1)}, u32[]{:S(2)}, u32[]{:S(2)}) collective-permute-start(f32[2,256]{1,0:T(2,128)S(1)} %fusion.36), channel_id=1, source_target_pairs={{0,24},{8,16},{16,8},{24,0},{1,25},{9,17},{17,9},{25,1},{2,26},{10... | collective-permute-start | bytes 6152 | tf_op jit(solution)/shard_map/ppermute | solution.py:84
  400.4 5.0 %collective-permute-start.55 = (f32[2,256]{1,0:T(2,128)S(1)}, f32[2,256]{1,0:T(2,128)S(1)}, u32[]{:S(2)}, u32[]{:S(2)}) collective-permute-start(f32[2,256]{1,0:T(2,128)S(1)} %fusion.36), channel_id=1, source_target_pairs={{0,8},{8,0},{16,24},{24,16},{1,9},{9,1},{17,25},{25,17},{2,10},{10... | collective-permute-start | bytes 6152 | tf_op jit(solution)/shard_map/ppermute | solution.py:84
  403.8 4.5 collective-permute-start.56
  408.3 17.7 %collective-permute-start.58 = (f32[2,256]{1,0:T(2,128)S(1)}, f32[2,256]{1,0:T(2,128)S(1)}, u32[]{:S(2)}, u32[]{:S(2)}) collective-permute-start(f32[2,256]{1,0:T(2,128)S(1)} %add_add_fusion.2), channel_id=1, source_target_pairs={{0,4},{4,0},{1,5},{5,1},{2,6},{6,2},{3,7},{7,3},{8,12},{12,8},{9,1... | collective-permute-start | bytes 6152 | tf_op jit(solution)/shard_map/ppermute | solution.py:65
  422.5 6.2 %collective-permute-start.45 = (bf16[256,256]{1,0:T(8,128)(2,1)}, bf16[256,256]{1,0:T(8,128)(2,1)S(1)}, u32[]{:S(2)}, u32[]{:S(2)}) collective-permute-start(bf16[256,256]{1,0:T(8,128)(2,1)} %get-tuple-element.117), channel_id=1, source_target_pairs={{0,3},{1,2},{2,1},{3,0},{4,7},{5,6},{6,5},{7,4},{8,11},{9,10},{10,... | collective-permute-start | bytes 393224 | tf_op jit(solution)/shard_map/ppermute | solution.py:61
  423.7 6.3 %collective-permute-start.44 = (bf16[256,256]{1,0:T(8,128)(2,1)}, bf16[256,256]{1,0:T(8,128)(2,1)S(1)}, u32[]{:S(2)}, u32[]{:S(2)}) collective-permute-start(bf16[256,256]{1,0:T(8,128)(2,1)} %get-tuple-element.116), channel_id=1, source_target_pairs={{0,2},{1,3},{2,0},{3,1},{4,6},{5,7},{6,4},{7,5},{8,10},{9,11},{10,... | collective-permute-start | bytes 393224 | tf_op jit(solution)/shard_map/ppermute | solution.py:61
  424.9 5.2 %collective-permute-start.43 = (bf16[256,256]{1,0:T(8,128)(2,1)}, bf16[256,256]{1,0:T(8,128)(2,1)S(1)}, u32[]{:S(2)}, u32[]{:S(2)}) collective-permute-start(bf16[256,256]{1,0:T(8,128)(2,1)} %get-tuple-element.115), channel_id=1, source_target_pairs={{0,1},{1,0},{2,3},{3,2},{4,5},{5,4},{6,7},{7,6},{8,9},{9,8},{10,11... | collective-permute-start | bytes 393224 | tf_op jit(solution)/shard_map/ppermute | solution.py:61
  434.5 5.7 %collective-permute-start.61 = (f32[8,128]{1,0:T(8,128)S(1)}, f32[8,128]{1,0:T(8,128)S(1)}, u32[]{:S(2)}, u32[]{:S(2)}) collective-permute-start(f32[8,128]{1,0:T(8,128)S(1)} %broadcast_in_dim.26), channel_id=1, source_target_pairs={{0,24},{8,16},{16,8},{24,0},{1,25},{9,17},{17,9},{25,1},{2,26},{10... | collective-permute-start | bytes 12296 | tf_op jit(solution)/shard_map/ppermute | solution.py:84
  436.0 5.1 %collective-permute-start.59 = (f32[8,128]{1,0:T(8,128)S(1)}, f32[8,128]{1,0:T(8,128)S(1)}, u32[]{:S(2)}, u32[]{:S(2)}) collective-permute-start(f32[8,128]{1,0:T(8,128)S(1)} %broadcast_in_dim.26), channel_id=1, source_target_pairs={{0,8},{8,0},{16,24},{24,16},{1,9},{9,1},{17,25},{25,17},{2,10},{10... | collective-permute-start | bytes 12296 | tf_op jit(solution)/shard_map/ppermute | solution.py:84
  439.5 4.5 collective-permute-start.60
  444.0 4.5 collective-permute-start.64
  450.7 9.3 %collective-permute-start.71 = (bf16[64,1152]{1,0:T(8,128)(2,1)}, bf16[64,1152]{1,0:T(8,128)(2,1)}, u32[]{:S(2)}, u32[]{:S(2)}) collective-permute-start(bf16[64,1152]{1,0:T(8,128)(2,1)} %get-tuple-element.307), channel_id=1, source_target_pairs={{0,3},{1,2},{2,1},{3,0},{4,7},{5,6},{6,5},{7,4},{8,11},{9,10},{10,... | collective-permute-start | bytes 442376 | tf_op jit(solution)/shard_map/ppermute | solution.py:61
  452.0 9.3 %collective-permute-start.70 = (bf16[64,1152]{1,0:T(8,128)(2,1)}, bf16[64,1152]{1,0:T(8,128)(2,1)}, u32[]{:S(2)}, u32[]{:S(2)}) collective-permute-start(bf16[64,1152]{1,0:T(8,128)(2,1)} %get-tuple-element.308), channel_id=1, source_target_pairs={{0,2},{1,3},{2,0},{3,1},{4,6},{5,7},{6,4},{7,5},{8,10},{9,11},{10,... | collective-permute-start | bytes 442376 | tf_op jit(solution)/shard_map/ppermute | solution.py:61
  453.3 8.0 %collective-permute-start.69 = (bf16[64,1152]{1,0:T(8,128)(2,1)}, bf16[64,1152]{1,0:T(8,128)(2,1)}, u32[]{:S(2)}, u32[]{:S(2)}) collective-permute-start(bf16[64,1152]{1,0:T(8,128)(2,1)} %get-tuple-element.309), channel_id=1, source_target_pairs={{0,1},{1,0},{2,3},{3,2},{4,5},{5,4},{6,7},{7,6},{8,9},{9,8},{10,11... | collective-permute-start | bytes 442376 | tf_op jit(solution)/shard_map/ppermute | solution.py:61
  (67 other events, 501.5 us)
Sparse Core Ops, SparseCore 0:
  307.7 55.0 reduce-scatter.1

commit v2 on v1

v2 whole, which is shorter than its diff:
```python
import functools
import math

import jax
import jax.numpy as jnp
from jax import lax
from jax.experimental import pallas as pl
from jax.experimental.pallas import tpu as pltpu
from jax.sharding import PartitionSpec as P

STEP = 10


NORM_EPSILON = 1e-05
ROPE_BASE = 160000.0
CLIP_NORM = 1.0
LEARN_RATE = 0.02
GAIN_RATE = 0.5
BETA_ONE = 0.9
BETA_TWO = 0.98
ADAM_EPSILON = 1e-08
WEIGHT_DECAY = 0.01
MASKED = -1e30
SIZES = (1, 2, 3, 4, 6, 8)

BLOCK = 256
LANES = 128
FF_PAD = 128
F32 = jnp.float32
BF16 = jnp.bfloat16

NT = (((1,), (1,)), ((), ()))
NN = (((1,), (0,)), ((), ()))
TN = (((0,), (0,)), ((), ()))


def mm(a, b, dims):
    return lax.dot_general(a, b, dims, preferred_element_type=F32)


VMEM = pl.BlockSpec(memory_space=pltpu.VMEM)
SMEM = pl.BlockSpec(memory_space=pltpu.SMEM)

def room(mib):
    return pltpu.CompilerParams(vmem_limit_bytes=mib * 1024 * 1024)


COST = pl.CostEstimate(flops=1024, bytes_accessed=1024, transcendentals=0)


def whole_call(body, outs, args, scratch=(), scalars=1, extra=6, away=0):
    inside = len(args) - scalars - away
    held = sum(
        math.prod(a.shape) * a.dtype.itemsize
        for a in (*args[: scalars + inside], *scratch)
        if a.dtype in (F32, BF16)
    ) + sum(math.prod(s) * jnp.dtype(t).itemsize for s, t in outs)
    return pl.pallas_call(
        body,
        out_shape=[jax.ShapeDtypeStruct(s, t) for s, t in outs],
        in_specs=[SMEM] * scalars
        + [VMEM] * inside
        + [pl.BlockSpec(memory_space=pltpu.HBM)] * away,
        out_specs=[VMEM] * len(outs),
        scratch_shapes=list(scratch),
        compiler_params=room(held // 2**20 + extra),
        cost_estimate=COST,
    )(*args)


def to_col(v, k):
    return lax.ppermute(v, "col", [(i, i ^ k) for i in range(4)])


def to_row(v):
    return lax.ppermute(v, "row", [(0, 1), (1, 0)])


def gather_col(v):
    half = v.shape[0] // 2
    a = to_col(v, 1)
    b = to_col(v, 2)
    d = jnp.concatenate([to_col(a[:half], 2), to_col(b[half:], 1)], axis=0)
    return [v, a, b, d]


def exchange_col(parts):
    return [parts[0]] + [to_col(parts[k], k) for k in range(1, 4)]


def after(values, *gates):
    tied = lax.optimization_barrier((values, gates))
    return tied[0]


def sum_dp(v):
    n = lax.axis_size("dp")
    if n == 4:
        return v + sum(
            lax.ppermute(v, "dp", [(i, i ^ k) for i in range(4)]) for k in (1, 2, 3)
        )
    return lax.psum(v, "dp")


def scatter_dp(v):
    if lax.axis_size("dp") != 4:
        return lax.psum_scatter(v, "dp", scatter_dimension=0).astype(F32)
    here = lax.axis_index("dp")
    piece = lambda k: lax.dynamic_index_in_dim(v, here ^ k, 0, keepdims=False)
    total = piece(0).astype(F32)
    for k in (1, 2, 3):
        total = total + lax.ppermute(piece(k), "dp", [(i, i ^ k) for i in range(4)]).astype(F32)
    return total


def natural(parts, here):
    stacked = jnp.stack(parts) if isinstance(parts, list) else parts
    return [lax.dynamic_index_in_dim(stacked, here ^ j, 0, keepdims=False) for j in range(4)]


def half_mask(shape):
    return lax.broadcasted_iota(jnp.int32, shape, len(shape) - 1) % LANES < 64


def swap_halves(v):
    lane = lax.broadcasted_iota(jnp.int32, v.shape, 1) % 64
    return jnp.where(lane < 32, pltpu.roll(v, LANES - 32, 1), pltpu.roll(v, 32, 1))


def rope_of(table):
    first = lax.broadcasted_iota(jnp.int32, table.shape, 1) % 64 < 32
    cos_part = jnp.where(first, table, pltpu.roll(table, 32, 1))
    sin_part = jnp.where(first, -pltpu.roll(table, LANES - 32, 1), table)
    return cos_part, sin_part


def moments(parts, features):
    average = sum(jnp.sum(v, axis=1, keepdims=True) for v in parts) / features
    centered = [v - average for v in parts]
    variance = sum(jnp.sum(v * v, axis=1, keepdims=True) for v in centered) / features
    inverse = lax.rsqrt(variance + NORM_EPSILON)
    return [v * inverse for v in centered], inverse


def lanes_of(ref, rows, p):
    return ref[rows, pl.ds(p * 256, 256)]


def project(low, w_own, table, out):
    cos_part, sin_part = rope_of(table[...])
    got = sum(mm(low[k], w_own[k, :384], NT) for k in range(4))
    query, key, value = got[:, :128], got[:, 128:256], got[:, 256:]
    query = (query * cos_part + swap_halves(query) * sin_part).astype(BF16)
    out[:, :128] = query * jnp.asarray(0.125, BF16)
    out[:, 128:256] = (key * cos_part + swap_halves(key) * sin_part).astype(BF16)
    out[:, 256:] = value.astype(BF16)


def qkv_kernel(
    index, x0, x1, x2, x3a, x3b, gains, w_own, table, own_out, h_out, inv_out, slot_out, x3
):
    step = pl.program_id(0)
    halves = pl.num_programs(0) // 2

    @pl.when(step < halves)
    def _():
        x3[...] = x3a[...]

    @pl.when(step >= halves)
    def _():
        x3[...] = x3b[...]

    refs = (x0, x1, x2, x3)

    @pl.when(step == index[0])
    def _():
        for k, ref in enumerate(refs):
            slot_out[:, k * 256 : (k + 1) * 256] = ref[...]

    parts = [ref[...].astype(F32) for ref in refs]
    units, inverse = moments(parts, 4 * 256)
    inv_out[...] = jnp.broadcast_to(inverse, inv_out.shape)
    low = [(units[k] * gains[k, 0:1, :]).astype(BF16) for k in range(4)]
    for k in range(4):
        h_out[:, k * 256 : (k + 1) * 256] = low[k]
    project(low, w_own, table, own_out)


def away_kernel(index, h, w_own, table, out):
    low = [h[:, k * 256 : (k + 1) * 256] for k in range(4)]
    project(low, w_own, table, out)


def run_qkv(index, xs, gains, w_own, table):
    rows = xs[0].shape[0]
    step = 256
    last = rows // step // 2 - 1
    whole = lambda shape: pl.BlockSpec(shape, lambda i, s: (0,) * len(shape))
    block = lambda n: pl.BlockSpec((step, n), lambda i, s: (i, 0))
    shape = lambda n, t=BF16: jax.ShapeDtypeStruct((rows, n), t)
    return pl.pallas_call(
        qkv_kernel,
        grid_spec=pltpu.PrefetchScalarGridSpec(
            num_scalar_prefetch=1,
            grid=(rows // step,),
            in_specs=[block(256)] * 3
            + [
                pl.BlockSpec((step, 256), lambda i, s: (jnp.minimum(i, last), 0)),
                pl.BlockSpec((step, 256), lambda i, s: (jnp.maximum(i - last - 1, 0), 0)),
            ]
            + [
                whole(gains.shape),
                whole(w_own.shape),
                pl.BlockSpec((step, 128), lambda i, s: (s[1] * (rows // step) + i, 0)),
            ],
            out_specs=[block(384), block(1024), block(128), whole((step, 1024))],
            scratch_shapes=[pltpu.VMEM((step, 256), BF16)],
        ),
        out_shape=[
            shape(384), shape(1024), shape(128, F32), jax.ShapeDtypeStruct((step, 1024), BF16),
        ],
        compiler_params=room(20),
        cost_estimate=COST,
    )(index, *xs, gains, w_own, table)


def run_away(index, h, w_own, table):
    rows = h.shape[0]
    block = lambda n: pl.BlockSpec((256, n), lambda i, s: (i, 0))
    return pl.pallas_call(
        away_kernel,
        grid_spec=pltpu.PrefetchScalarGridSpec(
            num_scalar_prefetch=1,
            grid=(rows // 256,),
            in_specs=[
                block(1024),
                pl.BlockSpec(w_own.shape, lambda i, s: (0, 0, 0)),
                pl.BlockSpec((256, 128), lambda i, s: ((1 - s[1]) * (rows // 256) + i, 0)),
            ],
            out_specs=block(384),
        ),
        out_shape=jax.ShapeDtypeStruct((rows, 384), BF16),
        compiler_params=room(16),
        cost_estimate=COST,
    )(index, h, w_own, table)


def to_columns(row):
    return jnp.transpose(jnp.broadcast_to(row, (LANES, row.shape[1])))


def attend_kernel(info, seg, own, recv, own_out, oth_out, lse_out, qkv, mixed, seg_col, sems):
    length = qkv.shape[0]
    rows = length // 2
    blocks = length // BLOCK
    here = info[4, 0]
    mine = pl.ds(pl.multiple_of(here * rows, rows), rows)
    other = pl.ds(pl.multiple_of((1 - here) * rows, rows), rows)
    copies = [
        pltpu.make_async_copy(own, qkv.at[mine, :], sems.at[0]),
        pltpu.make_async_copy(recv, qkv.at[other, :], sems.at[1]),
    ]
    for copy in copies:
        copy.start()
    for i in range(blocks):
        seg_col[i * BLOCK : (i + 1) * BLOCK, :] = to_columns(seg[:, i * BLOCK : (i + 1) * BLOCK])
    for copy in copies:
        copy.wait()
    low_half = half_mask((BLOCK, LANES))
    zero = jnp.zeros((BLOCK, LANES), BF16)

    def wide_block(at, first, count):
        query = qkv[pl.ds(at, BLOCK), :128]
        pair = jnp.concatenate(
            [jnp.where(low_half, query, zero), jnp.where(low_half, zero, query)], axis=0
        )
        k_at = pl.multiple_of(jnp.minimum(first, blocks - count) * BLOCK, BLOCK)
        span = pl.ds(k_at, count * BLOCK)
        got = mm(pair, qkv[span, 128:256], NT)
        seg_q = seg_col[pl.ds(at, BLOCK), :]
        seg_k = seg[:, span]
        chunks = []
        for j in range(count * 2):
            lanes = slice(j * LANES, (j + 1) * LANES)
            same = seg_q == seg_k[:, lanes]
            chunks.append(
                [
                    jnp.where(same, got[:BLOCK, lanes], MASKED),
                    jnp.where(same, got[BLOCK:, lanes], MASKED),
                ]
            )
        mixing, lse = [], []
        weights = []
        for head in range(2):
            highest = chunks[0][head]
            for j in range(1, count * 2):
                highest = jnp.maximum(highest, chunks[j][head])
            highest = jnp.max(highest, axis=1, keepdims=True)
            weight = [jnp.exp(chunks[j][head] - highest) for j in range(count * 2)]
            total = weight[0]
            for j in range(1, count * 2):
                total = total + weight[j]
            total = jnp.sum(total, axis=1, keepdims=True)
            weights.append(jnp.concatenate([w.astype(BF16) for w in weight], axis=1))
            mixing.append(total)
            lse.append(highest + jnp.log(total))
        both = mm(jnp.concatenate(weights, axis=0), qkv[span, 256:], NN)
        mixed[pl.ds(at, BLOCK), :] = jnp.where(
            low_half, both[:BLOCK] / mixing[0], both[BLOCK:] / mixing[1]
        ).astype(BF16)
        for head in range(2):
            lse_out[head : head + 1, pl.ds(at, BLOCK)] = to_row_form(lse[head])

    def one_block(qb, _):
        at = pl.multiple_of(qb * BLOCK, BLOCK)
        first = info[0, qb]
        need = info[1, qb] - first
        sizes = SIZES
        for i, count in enumerate(sizes):
            least = sizes[i - 1] if i else 0

            @pl.when((need > least) & (need <= count))
            def _(count=count):
                wide_block(at, first, count)

        return 0

    lax.fori_loop(0, blocks, one_block, 0)
    own_out[...] = mixed[pl.ds(pl.multiple_of(here * rows, rows), rows), :]
    oth_out[...] = mixed[pl.ds(pl.multiple_of((1 - here) * rows, rows), rows), :]


def attend_back_kernel(
    info, seg, lse, dm_own, dm_recv, mix_own, mix_oth, own, recv, table_from,
    own_out, oth_out, qkv, dmix, dsum, dquery, dout, seg_col, table, mixed, sems,
):
    length = qkv.shape[0]
    rows = length // 2
    here = info[4, 0]
    mine = pl.ds(pl.multiple_of(here * rows, rows), rows)
    other = pl.ds(pl.multiple_of((1 - here) * rows, rows), rows)
    early = [
        pltpu.make_async_copy(mix_own, mixed.at[mine, :], sems.at[3]),
        pltpu.make_async_copy(mix_oth, mixed.at[other, :], sems.at[4]),
    ]
    copies = [
        pltpu.make_async_copy(own, qkv.at[mine, :], sems.at[0]),
        pltpu.make_async_copy(recv, qkv.at[other, :], sems.at[1]),
        pltpu.make_async_copy(table_from, table, sems.at[2]),
    ]
    for copy in early + copies:
        copy.start()
    dmix[mine, :] = dm_own[...]
    dmix[other, :] = dm_recv[...]
    blocks = length // BLOCK
    for i in range(blocks):
        seg_col[i * BLOCK : (i + 1) * BLOCK, :] = to_columns(seg[:, i * BLOCK : (i + 1) * BLOCK])

    for copy in early:
        copy.wait()

    def inner(qb, _):
        at = pl.multiple_of(qb * BLOCK, BLOCK)
        block = pl.ds(at, BLOCK)
        product = jnp.transpose(dmix[block, :].astype(F32) * mixed[block, :].astype(F32))
        dsum[0:1, pl.ds(at, BLOCK)] = jnp.sum(product[:64], axis=0, keepdims=True)
        dsum[1:2, pl.ds(at, BLOCK)] = jnp.sum(product[64:], axis=0, keepdims=True)
        dquery[pl.ds(at, BLOCK), :] = jnp.zeros((BLOCK, LANES), F32)
        return 0

    lax.fori_loop(0, blocks, inner, 0)
    for copy in copies:
        copy.wait()
    low_half = half_mask((BLOCK, LANES))
    zero = jnp.zeros((BLOCK, LANES), BF16)

    def both(v):
        return jnp.concatenate([jnp.where(low_half, v, zero), jnp.where(low_half, zero, v)], axis=0)

    def wide_block(k_at, first, count):
        key_pair = both(qkv[pl.ds(k_at, BLOCK), 128:256])
        value_pair = both(qkv[pl.ds(k_at, BLOCK), 256:])
        seg_k = seg_col[pl.ds(k_at, BLOCK), :]
        at = pl.multiple_of(jnp.minimum(first, blocks - count) * BLOCK, BLOCK)
        span = pl.ds(at, count * BLOCK)
        query, grad = qkv[span, :128], dmix[span, :]
        got = mm(key_pair, query, NT)
        dgot = mm(value_pair, grad, NT)
        lse_q, dsum_q, seg_q = lse[:, span], dsum[:, span], seg[:, span]
        weights, dscores = [], []
        for head in range(2):
            rows_h = slice(head * BLOCK, (head + 1) * BLOCK)
            weight_h, dscore_h = [], []
            for j in range(count * 2):
                lanes = slice(j * LANES, (j + 1) * LANES)
                same = seg_k == seg_q[:, lanes]
                weight = jnp.exp(
                    jnp.where(same, got[rows_h, lanes] - lse_q[head : head + 1, lanes], MASKED)
                )
                weight_h.append(weight.astype(BF16))
                dscore_h.append(
                    (weight * (dgot[rows_h, lanes] - dsum_q[head : head + 1, lanes])).astype(BF16)
                )
            weights.append(jnp.concatenate(weight_h, axis=1))
            dscores.append(jnp.concatenate(dscore_h, axis=1))
        weights = jnp.concatenate(weights, axis=0)
        dscores = jnp.concatenate(dscores, axis=0)
        dvalue = mm(weights, grad, NN)
        dkey = mm(dscores, query, NN)
        dquery[span, :] += jnp.transpose(mm(key_pair, dscores, TN))
        dkey = jnp.where(low_half, dkey[:BLOCK], dkey[BLOCK:])
        dvalue = jnp.where(low_half, dvalue[:BLOCK], dvalue[BLOCK:])
        cos_part, sin_part = rope_of(table[pl.ds(k_at, BLOCK), :])
        dkey = dkey * cos_part - swap_halves(dkey) * sin_part
        dout[pl.ds(k_at, BLOCK), 128:256] = dkey.astype(BF16)
        dout[pl.ds(k_at, BLOCK), 256:] = dvalue.astype(BF16)

    def one_block(kb, _):
        k_at = pl.multiple_of(kb * BLOCK, BLOCK)
        first = info[0, kb]
        need = info[1, kb] - first
        for i, count in enumerate(SIZES):
            least = SIZES[i - 1] if i else 0

            @pl.when((need > least) & (need <= count))
            def _(count=count):
                wide_block(k_at, first, count)

        return 0

    lax.fori_loop(0, blocks, one_block, 0)

    def finish(qb, _):
        at = pl.multiple_of(qb * BLOCK, BLOCK)
        cos_part, sin_part = rope_of(table[pl.ds(at, BLOCK), :])
        grad = dquery[pl.ds(at, BLOCK), :] * 0.125
        grad = grad * cos_part - swap_halves(grad) * sin_part
        dout[pl.ds(at, BLOCK), :128] = grad.astype(BF16)
        return 0

    lax.fori_loop(0, blocks, finish, 0)
    own_out[...] = dout[mine, :]
    oth_out[...] = dout[other, :]


def run_attend(info, own, recv, seg_row):
    rows, length = own.shape[0], seg_row.shape[1]
    return whole_call(
        attend_kernel,
        [((rows, LANES), BF16), ((rows, LANES), BF16), ((2, length), F32)],
        (info, seg_row, own, recv),
        [
            pltpu.VMEM((length, 384), BF16),
            pltpu.VMEM((length, LANES), BF16),
            pltpu.VMEM((length, LANES), F32),
            pltpu.SemaphoreType.DMA((2,)),
        ],
        away=2,
        extra=46,
    )


def run_attend_back(
    info, own, recv, seg_row, lse, mix_own, mix_away, dm_own, dm_recv, table
):
    rows, length = own.shape[0], seg_row.shape[1]
    return whole_call(
        attend_back_kernel,
        [((rows, 384), BF16), ((rows, 384), BF16)],
        (info, seg_row, lse, dm_own, dm_recv, mix_own, mix_away, own, recv, table),
        [
            pltpu.VMEM((length, 384), BF16),
            pltpu.VMEM((length, LANES), BF16),
            pltpu.VMEM((2, length), F32),
            pltpu.VMEM((length, LANES), F32),
            pltpu.VMEM((length, 384), BF16),
            pltpu.VMEM((length, LANES), F32),
            pltpu.VMEM((length, LANES), F32),
            pltpu.VMEM((length, LANES), BF16),
            pltpu.SemaphoreType.DMA((5,)),
        ],
        extra=36,
        away=5,
    )


def slot_rows(info, k):
    return pl.ds(pl.multiple_of((info[4, 1] ^ k) * 256, 256), 256)


def attn_out_kernel(plan, info, mix_own, mix_oth, w_own, w_oth, *outs):
    for out, pieces in zip(outs, plan):
        at = 0
        for k, first, count in pieces:
            start = pl.multiple_of((info[4, 1] ^ k) * 256 + first, 128)
            rows = pl.ds(start, count)
            mix = jnp.concatenate([mix_own[rows, :], mix_oth[rows, :]], axis=1)
            for p in range(4):
                weight = jnp.concatenate([w_own[k ^ p, 384:512], w_oth[k ^ p, 384:512]], axis=0)
                out[at : at + count, p * 256 : (p + 1) * 256] = mm(mix, weight, NN).astype(BF16)
            at += count


def relay_kernel(first, x, p0, got, part, sent_out, kept_out):
    half = got.shape[0] // 2
    sent_out[...] = (part[...].astype(F32) + got[half:, :].astype(F32)).astype(BF16)
    rows = slice(first, first + half)
    kept_out[...] = x[rows, :].astype(F32) + p0[rows, :].astype(F32) + got[:half, :].astype(F32)


def middle_kernel(kept_a, got_a, kept_b, got_b, out):
    half = kept_a.shape[0]
    out[:half, :] = (kept_a[...] + got_a[...].astype(F32)).astype(BF16)
    out[half:, :] = (kept_b[...] + got_b[...].astype(F32)).astype(BF16)


def ffn_kernel(k, index, *refs):
    pieces = 2 if k == 3 else 1
    part = jnp.concatenate([ref[...] for ref in refs[:pieces]], axis=0)
    d0, d1, d2, d3, gains, w_own, w_oth, *refs = refs[pieces:]
    backs = refs[-pieces:]
    f0, f1, f2, f3, h_out, hid_out, dug_out, mid_out = refs[-8 - pieces : -pieces]
    parts = [part[:, (k ^ p) * 256 : ((k ^ p) + 1) * 256] for p in range(4)]
    mid_out[...] = parts[0]
    units, _ = moments([v.astype(F32) for v in parts], 4 * 256)
    low = [(units[p] * gains[p, 1:2, :]).astype(BF16) for p in range(4)]
    for p in range(4):
        h_out[:, p * 256 : (p + 1) * 256] = low[p]
    grads = [ref[...] for ref in (d0, d1, d2, d3)]

    def weight(p, i):
        rows = slice(i * 384, (i + 1) * 384)
        return jnp.concatenate([w_own[p, rows], w_oth[p, rows]], axis=0)

    gate = sum(mm(low[p], weight(p, 0), NT) for p in range(4))
    up = sum(mm(low[p], weight(p, 1), NT) for p in range(4))
    dhidden = sum(mm(grads[p], weight(p, 2), NT) for p in range(4))
    phi = 0.5 * (1.0 + lax.erf(gate * (2.0**-0.5)))
    density = jnp.exp(-0.5 * gate * gate) * ((2.0 * math.pi) ** -0.5)
    act = gate * phi
    hidden = (act * up).astype(BF16)
    dgate = (dhidden * up * (phi + gate * density)).astype(BF16)
    dup = (dhidden * act).astype(BF16)
    hid_out[...] = hidden
    dug_out[:, :384] = dgate[:, :384]
    dug_out[:, 384:768] = dup[:, :384]
    dug_out[:, 768:1152] = dgate[:, 384:]
    dug_out[:, 1152:] = dup[:, 384:]
    for p in range(4):
        got = mm(dgate, weight(p, 0), NN) + mm(dup, weight(p, 1), NN)
        got = got.astype(BF16)
        for i, out in enumerate(backs):
            out[:, (k ^ p) * 256 : ((k ^ p) + 1) * 256] = got[i * (256 // pieces) : (i + 1) * (256 // pieces)]
    for p, out in enumerate((f0, f1, f2, f3)):
        out[...] = mm(hidden, weight(p, 2), NN).astype(BF16)


def run_ffn(k, index, mids, grads, gains, w_own, w_oth, held):
    rows = grads[0].shape[0]
    whole = lambda shape: pl.BlockSpec(shape, lambda i, s: (0,) * len(shape))
    block = lambda n: pl.BlockSpec((256, n), lambda i, s: (s[0] ^ k, 0))
    widths = [256] * 4 + [1024, 768, 1536, 256]
    outs = pl.pallas_call(
        functools.partial(ffn_kernel, k),
        grid_spec=pltpu.PrefetchScalarGridSpec(
            num_scalar_prefetch=1,
            grid=(1,),
            in_specs=[whole(v.shape) for v in mids]
            + [block(256)] * 4
            + [whole(gains.shape), whole(w_own.shape), whole(w_oth.shape)]
            + [pl.BlockSpec(memory_space=pl.ANY)] * len(held),
            out_specs=[block(n) for n in widths] + [whole(v.shape) for v in mids],
        ),
        out_shape=[jax.ShapeDtypeStruct((rows, n), BF16) for n in widths]
        + [jax.ShapeDtypeStruct(v.shape, BF16) for v in mids],
        input_output_aliases={8 + len(mids) + i: i for i in range(len(held))},
        compiler_params=room(26),
        cost_estimate=COST,
    )(index, *mids, *grads, gains, w_own, w_oth, *held)
    return outs[:8], list(outs[8:])


def pack_kernel(*refs):
    out = refs[-1]
    planes, _, rows, _ = out.shape
    for p in range(4):
        block = slice(p * 256, (p + 1) * 256)
        total = sum(ref[block, :].astype(F32) for ref in refs[:-1]).astype(BF16)
        for d in range(planes):
            out[d, p] = total[d * rows : (d + 1) * rows]


def pack_dp(*terms):
    planes, width = lax.axis_size("dp"), terms[0].shape[1]
    if planes > 16:
        total = sum(v.astype(F32) for v in terms).astype(BF16)
        return jnp.swapaxes(total.reshape(4, planes, 256 // planes, width), 0, 1)
    return whole_call(
        pack_kernel, [((planes, 4, 256 // planes, width), BF16)], terms, scalars=0
    )[0]


def norm_back(grads, units, inverse, gains):
    scaled = [g * w for g, w in zip(grads, gains)]
    first = sum(jnp.sum(v, axis=1, keepdims=True) for v in scaled) / 1024
    second = sum(jnp.sum(v * u, axis=1, keepdims=True) for v, u in zip(scaled, units)) / 1024
    return [inverse * (v - first - u * second) for v, u in zip(scaled, units)]


def middle_back_kernel(info, mid, p0, p1, p2, p3a, p3b, d0, d1, d2, d3, gains, dx_out, dz_out, gain_out):
    rows = slot_rows(info, 0)
    at = [slice(p * 256, (p + 1) * 256) for p in range(4)]
    units, inverse = moments([mid[:, a].astype(F32) for a in at], 1024)
    last = jnp.concatenate([p3a[...], p3b[...]], axis=0)
    grads = [sum(part[:, a].astype(F32) for part in (p0, p1, p2, last)) for a in at]
    back = norm_back(grads, units, inverse, [gains[p, 1:2, :] for p in range(4)])
    for p, dy in enumerate((d0, d1, d2, d3)):
        total = back[p] + dy[rows, :].astype(F32)
        dx_out[:, at[p]] = total
        dz_out[:, at[p]] = total.astype(BF16)
        gain_out[p : p + 1, :] = jnp.sum(grads[p] * units[p], axis=0, keepdims=True)


def mixed_back_kernel(k, index, *refs):
    pieces = 2 if k == 3 else 1
    part = jnp.concatenate([ref[...] for ref in refs[:pieces]], axis=0)
    w_own, w_oth = refs[pieces : pieces + 2]
    own_out, oth_out, dz_out = refs[-3:]
    total = None
    for p in range(4):
        piece = part[:, (k ^ p) * 256 : ((k ^ p) + 1) * 256]
        dz_out[:, p * 256 : (p + 1) * 256] = piece
        term = mm(piece, jnp.concatenate([w_own[p], w_oth[p]], axis=0), NT)
        total = term if total is None else total + term
    own_out[...] = total[:, :128].astype(BF16)
    oth_out[...] = total[:, 128:].astype(BF16)


def run_mixed_back(k, index, parts, w_own, w_oth, held):
    rows = 4 * 256
    whole = lambda shape: pl.BlockSpec(shape, lambda i, s: (0,) * len(shape))
    block = lambda n: pl.BlockSpec((256, n), lambda i, s: (s[0] ^ k, 0))
    weight = pl.BlockSpec((4, 128, 256), lambda i, s: (0, 3, 0))
    return pl.pallas_call(
        functools.partial(mixed_back_kernel, k),
        grid_spec=pltpu.PrefetchScalarGridSpec(
            num_scalar_prefetch=1,
            grid=(1,),
            in_specs=[whole(v.shape) for v in parts]
            + [weight, weight]
            + [pl.BlockSpec(memory_space=pl.ANY)] * len(held),
            out_specs=[block(128), block(128), block(1024)],
        ),
        out_shape=[jax.ShapeDtypeStruct((rows, n), BF16) for n in (128, 128, 1024)],
        input_output_aliases={3 + len(parts) + i: i for i in range(len(held))},
        compiler_params=room(12),
        cost_estimate=COST,
    )(index, *parts, w_own, w_oth, *held)


def to_row_form(column):
    return jnp.transpose(jnp.broadcast_to(column, (column.shape[0], LANES)))[0:1, :]


def input_back_kernel(d_own, d_oth, w_own, w_oth, h, gains, o0, o1, o2, o3, sums_out, gain_out):
    step = pl.program_id(0)
    grad = jnp.concatenate([d_own[...], d_oth[...]], axis=1)
    first = second = None
    for p, out in enumerate((o0, o1, o2, o3)):
        weight = jnp.concatenate([w_own[p, :384], w_oth[p, :384]], axis=0)
        got = mm(grad, weight, NN)
        out[...] = got.astype(BF16)
        crossed = got * h[:, p * 256 : (p + 1) * 256].astype(F32)
        scaled = got * gains[p, 0:1, :]
        scaled = scaled[:, :128] + scaled[:, 128:]
        across = crossed[:, :128] + crossed[:, 128:]
        first = scaled if first is None else first + scaled
        second = across if second is None else second + across
        part = jnp.sum(crossed, axis=0, keepdims=True) / gains[p, 0:1, :]

        @pl.when(step == 0)
        def _():
            gain_out[p : p + 1, :] = part

        @pl.when(step > 0)
        def _():
            gain_out[p : p + 1, :] += part

    sums_out[0:1, :] = jnp.sum(jnp.transpose(first), axis=0, keepdims=True)
    sums_out[1:2, :] = jnp.sum(jnp.transpose(second), axis=0, keepdims=True)


def run_input_back(d_own, d_oth, w_own, w_oth, h, gains):
    rows = h.shape[0]
    whole = lambda shape: pl.BlockSpec(shape, lambda i: (0,) * len(shape))
    block = lambda n: pl.BlockSpec((256, n), lambda i: (i, 0))
    return pl.pallas_call(
        input_back_kernel,
        grid=(rows // 256,),
        in_specs=[block(384), block(384), whole(w_own.shape), whole(w_oth.shape), block(1024), whole(gains.shape)],
        out_specs=[block(256)] * 4 + [pl.BlockSpec((2, 256), lambda i: (0, i)), whole((4, 256))],
        out_shape=[jax.ShapeDtypeStruct((rows, 256), BF16)] * 4
        + [jax.ShapeDtypeStruct((2, rows), F32), jax.ShapeDtypeStruct((4, 256), F32)],
        compiler_params=room(24),
        cost_estimate=COST,
    )(d_own, d_oth, w_own, w_oth, h, gains)


def input_grad_kernel(p0, p1, p2, p3, sums, h, dz, inv, gains, out):
    first = to_columns(sums[0:1, :]) / 1024
    second = to_columns(sums[1:2, :]) / 1024
    both = lambda v: jnp.concatenate([v, v], axis=1)
    gain = gains[0, 0:1, :]
    total = sum(ref[...].astype(F32) for ref in (p0, p1, p2, p3)) * gain
    unit = h[...].astype(F32) / gain
    out[...] = dz[...].astype(F32) + both(inv[...]) * (total - both(first) - unit * both(second))


def run_input_grad(parts, sums, h, dz, inv, gains):
    rows = h.shape[0]
    block = lambda n: pl.BlockSpec((256, n), lambda i: (i, 0))
    return pl.pallas_call(
        input_grad_kernel,
        grid=(rows // 256,),
        in_specs=[block(256)] * 4
        + [pl.BlockSpec((2, 256), lambda i: (0, i)), block(256), block(256), block(128)]
        + [pl.BlockSpec(gains.shape, lambda i: (0, 0, 0))],
        out_specs=block(256),
        out_shape=jax.ShapeDtypeStruct((rows, 256), F32),
        compiler_params=room(12),
        cost_estimate=COST,
    )(*parts, sums, h, dz, inv, gains)


def adam_update(master, first_moment, second, gradient, factor, decay_rate, step_rate):
    scaled = gradient * factor
    first_new = BETA_ONE * first_moment + (1.0 - BETA_ONE) * scaled
    second_new = BETA_TWO * second + (1.0 - BETA_TWO) * scaled * scaled
    first_hat = first_new / (1.0 - BETA_ONE**STEP)
    second_hat = second_new / (1.0 - BETA_TWO**STEP)
    master_new = master - step_rate * (
        first_hat / (jnp.sqrt(second_hat) + ADAM_EPSILON) + decay_rate * master
    )
    return (first_new, second_new, master_new)


def positions(segment):
    length = segment.shape[0]
    number = jnp.arange(length, dtype=jnp.int32)
    before = jnp.concatenate([segment[:1] - 1, segment[:-1]])
    change_marks = jnp.where(segment != before, number, jnp.zeros_like(number))
    return number - lax.cummax(change_marks, axis=0)


def rope_table(place):
    lane = jnp.arange(LANES) % 64
    frequency = ROPE_BASE ** (-(2.0 * (lane % 32).astype(F32)) / 64)
    turned = place.astype(F32)[:, None] * frequency[None, :]
    return jnp.where(lane[None, :] < 32, jnp.cos(turned), jnp.sin(turned))


def on_device(
    tokens, segment_ids, cotangent, qkv_weight, attn_weight, in_weight, out_weight, norm_gains,
    qkv_master, attn_master, in_master, out_master,
    qkv_first, attn_first, in_first, out_first,
    qkv_second, attn_second, in_second, out_second,
    gains_first, gains_second,
):
    col, row = lax.axis_index("col"), lax.axis_index("row")
    segment = segment_ids[0]
    length = segment.shape[0]
    rows = length // 2
    blocks = length // BLOCK
    ff_here = in_weight.shape[2] // 4
    ff_pad = -ff_here % FF_PAD
    ff_wide = ff_here + ff_pad

    qkv_t = jnp.transpose(qkv_weight, (1, 2, 3, 0))
    attn_t = attn_weight.reshape(4, LANES, 256)
    in_t = jnp.transpose(in_weight, (1, 2, 0)).reshape(2, 4, ff_here, 256)
    out_t = out_weight.reshape(4, ff_here, 256)

    index = jnp.stack([col, row])
    a = to_col(tokens, 1)
    b = to_col(tokens, 2)
    high = norm_gains.astype(BF16)
    rest = norm_gains - high.astype(F32)
    middle = rest.astype(BF16)
    lowest = (rest - middle.astype(F32)).astype(BF16)
    gain_rows = jnp.concatenate([high, middle, lowest, jnp.zeros((10, 256), BF16)], axis=0)
    gain_rows = lax.optimization_barrier(gain_rows)

    def wide_piece(k):
        qkv = lax.dynamic_slice_in_dim(qkv_t, 2 * (col ^ k), 2, 1).reshape(3 * LANES, 256)
        return jnp.concatenate(
            [qkv, lax.dynamic_index_in_dim(attn_t, col ^ k, 0, keepdims=False), gain_rows], axis=0
        )

    half = tokens.shape[0] // 2
    x3a, x3b = to_col(a[:half], 2), to_col(b[half:], 1)
    xs = [tokens, a, b, x3a, x3b]
    wa_parts = exchange_col([wide_piece(k) for k in range(4)])
    wa_own = jnp.stack(after(wa_parts, x3a, x3b))
    ff_gate = (x3a, x3b)
    gains = wa_own[:, 512:518].astype(F32).reshape(4, 3, 2, 256)
    gains = gains[:, 0] + gains[:, 1] + gains[:, 2]

    planes = lax.axis_size("dp")
    fill = [(0, 0), (0, 0), (0, ff_pad), (0, 0)]
    ff_t = jnp.pad(jnp.concatenate([in_t, out_t[None]], axis=0), fill)
    ff_t = ff_t.reshape(3, 4, planes, ff_wide // planes, 256)
    ff_t = lax.dynamic_index_in_dim(ff_t, lax.axis_index("dp"), 2, keepdims=False)
    ff_parts = [lax.dynamic_index_in_dim(ff_t, col ^ k, 1, keepdims=False) for k in range(4)]
    ff_parts = exchange_col(after(ff_parts, *ff_gate))
    first = segment[::BLOCK]
    last = segment[BLOCK - 1 :: BLOCK]
    low = jnp.sum((segment[None, :] < first[:, None]).astype(jnp.int32), axis=1) // BLOCK
    high = (
        jnp.sum((segment[None, :] <= last[:, None]).astype(jnp.int32), axis=1) + BLOCK - 1
    ) // BLOCK
    place_here = jnp.zeros((blocks,), jnp.int32).at[0].set(row).at[1].set(col)
    info = jnp.stack([low, high, first, last, place_here])
    seg_row = segment_ids.astype(F32)
    table = rope_table(positions(segment))
    own, h1, inv, x_slot = run_qkv(index, xs, gains, wa_own, table)
    h1_recv = to_row(h1)
    dys = exchange_col([after(cotangent, own)] * 4)
    wa_oth = to_row(after(wa_own, own))
    ff_own = lax.all_gather(jnp.stack(after(ff_parts, own)), "dp", axis=2)
    recv = run_away(index, h1_recv, wa_own, table)
    mix_own, mix_away, lse = run_attend(info, own, recv, seg_row)
    mix_own, mix_away, lse, dys, wa_oth = after((mix_own, mix_away, lse, dys, wa_oth), wa_oth)
    mix_oth = to_row(mix_away)
    def attn_out(*plan):
        return whole_call(
            functools.partial(attn_out_kernel, plan),
            [((sum(count for _, _, count in pieces), 1024), BF16) for pieces in plan],
            (info, mix_own, mix_oth, wa_own, wa_oth),
        )

    x_first, y_first = attn_out(((1, 0, 128), (3, 0, 128)), ((2, 128, 128), (3, 128, 128)))
    x_first, y_first = to_col(x_first, 1), to_col(y_first, 2)
    x_part, y_part, part = attn_out(((1, 128, 128),), ((2, 0, 128),), ((0, 0, 256),))
    relay = lambda first, got, mine: whole_call(
        functools.partial(relay_kernel, first),
        [((128, 1024), BF16), ((128, 1024), F32)],
        (x_slot, part, got, mine),
        scalars=0,
    )
    y_second, kept_a = relay(0, x_first, y_part)
    x_second, kept_b = relay(128, y_first, x_part)
    y_second, x_second = to_col(y_second, 2), to_col(x_second, 1)
    (middle,) = whole_call(
        middle_kernel, [((256, 1024), BF16)], (kept_a, y_second, kept_b, x_second), scalars=0
    )
    ff_own = after(ff_own, x_second, y_second).reshape(4, 3 * ff_wide, 256)
    ff_oth = to_row(ff_own)
    m1, m2 = to_col(middle, 1), to_col(middle, 2)
    m3a, m3b = to_col(m1[:128], 2), to_col(m2[128:], 1)
    held, backward = (), [None] * 4
    for k, mids in enumerate(((middle,), (m1,), (m2,), (m3a, m3b))):
        held, part = run_ffn(k, index, mids, dys, gains, ff_own, ff_oth, held)
        backward[k] = [to_col(v, k) for v in part] if k else part
    forward = held[:4]
    h2, hidden, dug, mid_here = held[4:]
    dx_mid, dz, gain_two = whole_call(
        middle_back_kernel,
        [((256, 1024), F32), ((256, 1024), BF16), ((4, 256), F32)],
        (info, middle, *sum(backward, []), *dys, gains),
    )
    z1, z2 = to_col(dz, 1), to_col(dz, 2)
    z3a, z3b = to_col(z1[:128], 2), to_col(z2[128:], 1)

    h2, hidden, dug = after((h2, hidden, dug), z1, z2)
    dy_all = jnp.concatenate(dys, axis=1)
    ffn_own, ffn_oth = (
        jnp.concatenate(
            [
                mm(h2, dug[:, i * 2 * ff_wide : (i + 1) * 2 * ff_wide], TN).astype(BF16),
                mm(dy_all, hidden[:, i * ff_wide : (i + 1) * ff_wide], TN).astype(BF16),
            ],
            axis=1,
        )
        for i in range(2)
    )
    ffn_oth = to_row(ffn_oth)
    ffn_oth, z3a, z3b = after((ffn_oth, z3a, z3b), z3a, z3b)
    ffn_grad = lax.psum_scatter(pack_dp(ffn_own, ffn_oth), "dp", scatter_dimension=0).astype(F32)

    held = ()
    for k, parts in enumerate(((dz,), (z1,), (z2,), (z3a, z3b))):
        held = run_mixed_back(k, index, parts, wa_own, wa_oth, held)
    dm_own, dm_away, dz_here = held
    dm_recv = to_row(dm_away)
    forward = exchange_col(after(forward, dm_own))
    dq_own, dq_away = run_attend_back(
        info, own, recv, seg_row, lse, mix_own, mix_away, dm_own, dm_recv, table
    )
    dq_own, dq_away, forward, dz_here = after((dq_own, dq_away, forward, dz_here), forward[1:])
    layer_out = (mid_here.astype(F32) + sum(v.astype(F32) for v in forward)).astype(BF16)
    dq_oth = to_row(dq_away)

    attn_both = mm(dz_here, jnp.concatenate([mix_own, mix_oth], axis=1), TN)
    attn_sent = to_row(attn_both[:, LANES:].astype(BF16))
    attn_sum = (attn_both[:, :LANES] + attn_sent.astype(F32)).astype(BF16)
    qkv_sum = (mm(h1, dq_own, TN) + mm(h1_recv, dq_away, TN)).astype(BF16)

    *partial_first, sums, gain_one = run_input_back(dq_own, dq_oth, wa_own, wa_oth, h1, gains)
    notes = [
        jnp.concatenate([sums, jnp.pad(jnp.stack([gain_one[k], gain_two[k]]), [(0, 0), (0, rows - 256)])])
        for k in range(4)
    ]
    late = after(pack_dp(jnp.concatenate([qkv_sum, attn_sum], axis=1)), gain_one)
    late = scatter_dp(late)
    notes = exchange_col(notes)
    partial_first = exchange_col(after(partial_first, notes[1]))
    note = sum(notes)
    input_grad = run_input_grad(partial_first, note[:2], h1, dz_here, inv, gains)

    early = ffn_grad.astype(BF16)
    early = natural(exchange_col([early[k] for k in range(4)]), col)
    late = after(late, early, *partial_first[1:])
    squares = jnp.sum(ffn_grad * ffn_grad) + jnp.sum(late * late)
    message = jnp.concatenate([note[2:, :256], jnp.full((6, 256), squares)], axis=0)
    message = sum_dp(message)
    message = message + to_row(message)
    gain_grad = message[:2]
    total = message[2:3, :LANES] + jnp.sum(gain_grad * gain_grad)
    total = jnp.broadcast_to(total, (8, LANES))
    total = sum(exchange_col([total] * 4))
    grad_norm = jnp.sqrt(total[0, 0])
    factor = CLIP_NORM / (grad_norm + 1e-06)

    shard = late.shape[1]
    late = late.astype(BF16)
    late = natural(exchange_col([late[k] for k in range(4)]), col)
    grad_qkv = jnp.stack([v[:, : 3 * LANES].reshape(shard, 3, 2, 64) for v in late], axis=2).reshape(
        qkv_master.shape
    )
    grad_attn = jnp.concatenate([v[:, 3 * LANES :] for v in late], axis=1).T.reshape(
        attn_master.shape
    )
    grad_in = jnp.stack(
        [
            jnp.concatenate([v[:, i * ff_wide : i * ff_wide + ff_here] for v in early], axis=1)
            for i in range(2)
        ],
        axis=1,
    )
    grad_out = jnp.concatenate([v[:, 2 * ff_wide : 2 * ff_wide + ff_here] for v in early], axis=1).T

    grad_qkv, grad_attn, grad_in, grad_out = (
        v.astype(F32) for v in (grad_qkv, grad_attn, grad_in, grad_out)
    )
    qkv_new = adam_update(
        qkv_master, qkv_first, qkv_second, grad_qkv, factor, WEIGHT_DECAY, LEARN_RATE
    )
    attn_new = adam_update(
        attn_master, attn_first, attn_second, grad_attn, factor, WEIGHT_DECAY, LEARN_RATE
    )
    in_new = adam_update(in_master, in_first, in_second, grad_in, factor, WEIGHT_DECAY, LEARN_RATE)
    out_new = adam_update(
        out_master, out_first, out_second, grad_out, factor, WEIGHT_DECAY, LEARN_RATE
    )
    gains_new = adam_update(
        norm_gains, gains_first, gains_second, gain_grad, factor, 0.0, GAIN_RATE
    )
    return (
        layer_out, input_grad, grad_norm,
        qkv_new[0], attn_new[0], in_new[0], out_new[0],
        qkv_new[1], attn_new[1], in_new[1], out_new[1],
        qkv_new[2], attn_new[2], in_new[2], out_new[2],
        qkv_new[2].astype(BF16), attn_new[2].astype(BF16),
        in_new[2].astype(BF16), out_new[2].astype(BF16),
        gains_new[0], gains_new[1], gains_new[2],
    )


def solution(mesh):
    activations = P(("dp", "row"), "col")
    gains = P(None, "col")
    weights = (
        P("col", None, "row", None), P("row", None, "col"), P("col", None, "row"), P("row", "col"),
    )
    states = (
        P(("col", "dp"), None, "row", None), P("row", None, ("col", "dp")),
        P(("col", "dp"), None, "row"), P("row", ("col", "dp")),
    )
    return jax.shard_map(
        on_device,
        mesh=mesh,
        in_specs=(activations, P("dp", None), activations, *weights, gains)
        + states * 3
        + (gains, gains),
        out_specs=(activations, activations, P()) + states * 4 + (gains, gains, gains),
        check_vma=False,
    )
```

time: 481 us -> 360 us (0.75)
  waiting for transfers between devices: 177 us -> 98.3 us
  Pallas kernels: 115 us -> 87.9 us
  starting transfers between devices: 85.2 us -> 69.4 us
  local copies, waits for them, and re-layouts: 28.1 us -> 40.1 us
  other arithmetic: 38.2 us -> 27.6 us
    ppermute x52 -> x47, waiting for transfers between devices: 149 us -> 74.9 us  [to_col(): return lax.ppermute(v, 'col', [(i, i ^ k) for i in range(4)])]
    pallas_call x8 -> x10, Pallas kernels: 88.7 us -> 42.2 us  [whole_call(): pl.pallas_call(body, out_shape=[jax.ShapeDtypeStruct(s, t) for s, t in ou...]
    pallas_call x2 -> x12, Pallas kernels: 26.4 us -> 45.7 us  [the longest x4 22.2 us: run_ffn(): pl.pallas_call(functools.partial(ffn_kernel, k), grid_spec=pltpu.Prefetch...]
    unnamed x144 -> x139, local copies, waits for them, and re-layouts: 13.1 us -> 26.2 us
    ppermute x6 -> x3, starting transfers between devices: 11.2 us -> 4.45 us  [sum_dp(): lax.ppermute(v, 'dp', [(i, i ^ k) for i in range(4)])]
    ppermute x52 -> x47, starting transfers between devices: 61.1 us -> 55 us  [to_col(): return lax.ppermute(v, 'col', [(i, i ^ k) for i in range(4)])]
    mul x1 -> x0, other arithmetic: 5.54 us -> none  [rope_tables(): return (jnp.cos(turned), jnp.sin(turned) * sign[None, :])]
    convert_element_type x5 -> x4, other arithmetic: 6.58 us -> 1.63 us  [the longest x1 0.76 us: on_device(): high = norm_gains.astype(BF16)]
  transfers between devices with their start and end apart: 73 -> 64, of which waited for: 36 -> 21; matrix products, arithmetic and copies ran while one was open for 11% -> 12% of each run, Pallas kernels for 19% -> 24%
where the time goes in v2:
time: 360 us; the launch traced here: 354 us
  waiting for transfers between devices  98.3 us (27%)
  Pallas kernels  87.9 us (24%)
  starting transfers between devices  69.4 us (19%)
  local copies, waits for them, and re-layouts  40.1 us (11%)
  other arithmetic  27.6 us (8%)
  between operations  19.6 us (5%)
  matrix products  11.3 us (3%)
    ppermute x47, waiting for transfers between devices, to_col(): return lax.ppermute(v, 'col', [(i, i ^ k) for i in range(4)])  74.9 us
    ppermute x47, starting transfers between devices, to_col(): return lax.ppermute(v, 'col', [(i, i ^ k) for i in range(4)])  55 us
    pallas_call x10, Pallas kernels, whole_call(): pl.pallas_call(body, out_shape=[jax.ShapeDtypeStruct(s, t) for s, t in ou...  42.2 us
    unnamed x139, local copies, waits for them, and re-layouts  26.2 us
    pallas_call x4, Pallas kernels, run_ffn(): pl.pallas_call(functools.partial(ffn_kernel, k), grid_spec=pltpu.Prefetch...  22.2 us
    ppermute x3, waiting for transfers between devices, scatter_dp(): lax.ppermute(piece(k), 'dp', [(i, i ^ k) for i in range(4)]).astype(F32)  13.2 us
    dot_general x7, matrix products, mm(): return lax.dot_general(a, b, dims, preferred_element_type=F32)  11.3 us
    ppermute x3, starting transfers between devices, scatter_dp(): lax.ppermute(piece(k), 'dp', [(i, i ^ k) for i in range(4)]).astype(F32)  8.52 us
  transfers between devices with their start and end apart: 64, of which 21 were waited for; matrix products, arithmetic and copies ran while one was open for 12% of the time, Pallas kernels for 24%

profile of v2, /device:TPU:0, one launch (start us, length us, event | category | flops | bytes accessed | tf_op | source)
XLA Modules:
  0.0 354.2 jit_solution(10537728492821731566)
XLA Ops:
  7.2 3.0 collective-permute-start
  10.2 1.5 collective-permute-start.1
  16.6 2.9 collective-permute-start.6
  21.3 3.7 %fusion.5.table.table_from = f32[2048,128]{1,0:T(8,128)S(1)} fusion(f32[128]{0:T(128)S(1)} %fusion.33, f32[2048]{0:T(1024)S(1)} %fusion.26, pred[128]{0:T(512)(128)(4,1)S(1)} %broadcast_compare_fusion), kind=kLoop, calls=%fused_computation.19 | loop fusion | flops 524288 | bytes 1057408 | tf_op jit(solution)/shard_map/jit(_where)/select_n | solution.py:759
  28.3 2.9 fusion.2
  32.5 8.5 %collective-permute-done.2.x3a = bf16[512,256]{1,0:T(8,128)(2,1)S(1)} collective-permute-done((bf16[512,256]{1,0:T(8,128)(2,1)}, bf16[512,256]{1,0:T(8,128)(2,1)S(1)}, u32[]{:S(2)}, u32[]{:S(2)}) %collective-permute-start.2) | collective-permute-done | bytes 262176 | tf_op jit(solution)/shard_map/ppermute | solution.py:72
  42.1 1.7 collective-permute-start.22
  43.8 1.4 collective-permute-start.23
  45.2 1.3 pad_maximum_fusion.2.w_own.refs_1_.refs_2_
  47.7 4.2 %shard_map.381 = (bf16[1024,384]{1,0:T(8,128)(2,1)S(1)}, bf16[1024,1024]{1,0:T(8,128)(2,1)S(1)}, f32[1024,128]{1,0:T(8,128)S(1)}, bf16[256,1024]{1,0:T(8,128)(2,1)S(1)}) custom-call(s32[2]{0:T(128)S(1)} %pad_add_fusion.index, bf16[1024,256]{1,0:T(8,128)(2,1)S(1)} %copy-done.31, bf16[1024,256]{1,0:T(8,128)(2,1)S(1)} %collective-permute-done.x1, ...), custom_call_target="tpu_custom_call" | custom-call | flops 1024 | bytes 1024 | tf_op jit(solution)/shard_map/pallas_call | solution.py:201
  52.0 1.4 copy-done.12
  57.4 1.5 collective-permute-start.10
  58.9 1.5 collective-permute-start.8
  64.2 4.5 %shard_map.382.recv = bf16[1024,384]{1,0:T(8,128)(2,1)S(1)} custom-call(s32[2]{0:T(128)S(1)} %pad_add_fusion.index, bf16[1024,1024]{1,0:T(8,128)(2,1)} %collective-permute-done.7.h, bf16[4,528,256]{2,1,0:T(8,128)(2,1)S(1)} %pad_maximum_fusion.2.w_own.refs_1_.refs_2_, f32[2048,128]{1,0:T(8,128)S(1)} %copy-done.5), custom_call_target="tpu_custom_call" | custom-call | flops 1024 | bytes 1024 | tf_op jit(solution)/shard_map/pallas_call | solution.py:230
  68.7 16.1 %shard_map.383 = (bf16[1024,128]{1,0:T(8,128)(2,1)S(1)}, bf16[1024,128]{1,0:T(8,128)(2,1)S(1)}, f32[2,2048]{1,0:T(2,128)S(1)}) custom-call(s32[5,8]{1,0:T(8,128)S(1)} %stack.115.info, f32[1,2048]{1,0:T(1,128)S(1)} %convert_element_type.146.seg, bf16[1024,384]{1,0:T(8,128)(2,1)S(1)} %copy-done.17, bf16[1024,384]{1,0:T(8,128)(2,1)S(1)} %shard_map.382.recv), custom_call_target="tpu_custom_call" | custom-call | flops 1024 | bytes 1024 | tf_op jit(solution)/shard_map/pallas_call | solution.py:58
  85.1 1.4 collective-permute-done.12.mix_oth
  87.6 1.6 collective-permute-start.15
  90.8 10.8 %collective-permute-done.15.got = bf16[256,1024]{1,0:T(8,128)(2,1)S(1)} collective-permute-done((bf16[256,1024]{1,0:T(8,128)(2,1)S(1)}, bf16[256,1024]{1,0:T(8,128)(2,1)S(1)}, u32[]{:S(2)}, u32[]{:S(2)}) %collective-permute-start.15) | collective-permute-done | bytes 524320 | tf_op jit(solution)/shard_map/ppermute | solution.py:72
  104.9 4.6 %collective-permute-done.16.got_b = bf16[128,1024]{1,0:T(8,128)(2,1)S(1)} collective-permute-done((bf16[128,1024]{1,0:T(8,128)(2,1)S(1)}, bf16[128,1024]{1,0:T(8,128)(2,1)S(1)}, u32[]{:S(2)}, u32[]{:S(2)}) %collective-permute-start.16) | collective-permute-done | bytes 262176 | tf_op jit(solution)/shard_map/ppermute | solution.py:72
  109.5 1.6 collective-permute-done.14.got_a
  116.2 1.5 collective-permute-start.19
  117.8 11.6 %collective-permute-done.17.refs_0_ = bf16[256,1024]{1,0:T(8,128)(2,1)S(1)} collective-permute-done((bf16[256,1024]{1,0:T(8,128)(2,1)S(1)}, bf16[256,1024]{1,0:T(8,128)(2,1)S(1)}, u32[]{:S(2)}, u32[]{:S(2)}) %collective-permute-start.17) | collective-permute-done | bytes 524320 | tf_op jit(solution)/shard_map/ppermute | solution.py:72
  129.4 1.4 collective-permute-start.18
  132.1 5.5 %shard_map.389 = (bf16[1024,256]{1,0:T(8,128)(2,1)S(1)}, bf16[1024,256]{1,0:T(8,128)(2,1)}, bf16[1024,256]{1,0:T(8,128)(2,1)}, bf16[1024,256]{1,0:T(8,128)(2,1)}...) custom-call(s32[2]{0:T(128)S(1)} %pad_add_fusion.index, ...), custom_call_target="tpu_custom_call" | custom-call | flops 1024 | bytes 1024 | tf_op jit(solution)/shard_map/pallas_call | solution.py:563
  137.6 5.5 %shard_map.390 = (bf16[1024,256]{1,0:T(8,128)(2,1)S(1)}, bf16[1024,256]{1,0:T(8,128)(2,1)}, bf16[1024,256]{1,0:T(8,128)(2,1)}, bf16[1024,256]{1,0:T(8,128)(2,1)}...) custom-call(s32[2]{0:T(128)S(1)} %pad_add_fusion.index, ...), custom_call_target="tpu_custom_call", output_to_operand_aliasing={{0}: (9, {}), {1}: (10, {}), {2}: (11, {}), {3}: (12, {}), ... | custom-call | flops 1024 | bytes 1024 | tf_op jit(solution)/shard_map/pallas_call | solution.py:563
  143.1 5.5 %shard_map.391 = (bf16[1024,256]{1,0:T(8,128)(2,1)S(1)}, bf16[1024,256]{1,0:T(8,128)(2,1)}, bf16[1024,256]{1,0:T(8,128)(2,1)}, bf16[1024,256]{1,0:T(8,128)(2,1)}...) custom-call(s32[2]{0:T(128)S(1)} %pad_add_fusion.index, ...), custom_call_target="tpu_custom_call", output_to_operand_aliasing={{0}: (9, {}), {1}: (10, {}), {2}: (11, {}), {3}: (12, {}), ... | custom-call | flops 1024 | bytes 1024 | tf_op jit(solution)/shard_map/pallas_call | solution.py:563
  150.3 5.7 %shard_map.392 = (bf16[1024,256]{1,0:T(8,128)(2,1)S(1)}, bf16[1024,256]{1,0:T(8,128)(2,1)}, bf16[1024,256]{1,0:T(8,128)(2,1)}, bf16[1024,256]{1,0:T(8,128)(2,1)}...) custom-call(s32[2]{0:T(128)S(1)} %pad_add_fusion.index, ...), custom_call_target="tpu_custom_call", output_to_operand_aliasing={{0}: (10, {}), {1}: (11, {}), {2}: (12, {}), {3}: (13, {}),... | custom-call | flops 1024 | bytes 1024 | tf_op jit(solution)/shard_map/pallas_call | solution.py:563
  155.9 1.8 collective-permute-start.27
  158.9 11.7 %collective-permute-done.27.p3a = bf16[128,1024]{1,0:T(8,128)(2,1)S(1)} collective-permute-done((bf16[128,1024]{1,0:T(8,128)(2,1)S(1)}, bf16[128,1024]{1,0:T(8,128)(2,1)S(1)}, u32[]{:S(2)}, u32[]{:S(2)}) %collective-permute-start.27) | collective-permute-done | bytes 262176 | tf_op jit(solution)/shard_map/ppermute | solution.py:72
  170.5 3.3 collective-permute-done.28.p3b
  173.8 3.4 shard_map.393
  181.3 7.6 %collective-permute-done.29.refs_0_ = bf16[256,1024]{1,0:T(8,128)(2,1)S(1)} collective-permute-done((bf16[256,1024]{1,0:T(8,128)(2,1)S(1)}, bf16[256,1024]{1,0:T(8,128)(2,1)S(1)}, u32[]{:S(2)}, u32[]{:S(2)}) %collective-permute-start.29) | collective-permute-done | bytes 524320 | tf_op jit(solution)/shard_map/ppermute | solution.py:72
  189.4 1.9 convolution_convert_fusion.1
  196.0 1.9 convolution_convert_fusion
  198.1 3.6 %collective-permute-done.32.refs_0_ = bf16[128,1024]{1,0:T(8,128)(2,1)S(1)} collective-permute-done((bf16[128,1024]{1,0:T(8,128)(2,1)S(1)}, bf16[128,1024]{1,0:T(8,128)(2,1)S(1)}, u32[]{:S(2)}, u32[]{:S(2)}) %collective-permute-start.32) | collective-permute-done | bytes 262176 | tf_op jit(solution)/shard_map/ppermute | solution.py:72
  203.6 1.4 copy-done.7
  206.1 1.5 shard_map.394
  207.6 1.5 shard_map.395
  209.1 1.5 shard_map.396
  210.6 1.5 shard_map.397
  212.1 1.4 copy-done.1
  217.0 1.9 collective-permute-done.34.dm_recv
  223.0 19.7 %shard_map.398 = (bf16[1024,384]{1,0:T(8,128)(2,1)S(1)}, bf16[1024,384]{1,0:T(8,128)(2,1)S(1)}) custom-call(s32[5,8]{1,0:T(8,128)S(1)} %stack.115.info, f32[1,2048]{1,0:T(1,128)S(1)} %convert_element_type.146.seg, f32[2,2048]{1,0:T(2,128)S(1)} %get-tuple-element.229.lse, bf16[1024,128]{1,0:T(8,128)(2,1)S(1)} %get-tuple-element.253.dm_own, ...), custom_call_target="tpu_custom_call" | custom-call | flops 1024 | bytes 1024 | tf_op jit(solution)/shard_map/pallas_call | solution.py:58
  244.1 2.9 fusion.58
  248.7 6.5 %shard_map.399 = (bf16[1024,256]{1,0:T(8,128)(2,1)S(1)}, bf16[1024,256]{1,0:T(8,128)(2,1)S(1)}, bf16[1024,256]{1,0:T(8,128)(2,1)S(1)}, bf16[1024,256]{1,0:T(8,12...) custom-call(bf16[1024,384]{1,0:T(8,128)(2,1)S(1)} %get-tuple-element.270.d_own, ...), custom_call_target="tpu_custom_call" | custom-call | flops 1024 | bytes 1024 | tf_op jit(solution)/shard_map/pallas_call | solution.py:697
  255.2 3.8 %collective-permute-start.46 = (bf16[4,64,512]{2,1,0:T(8,128)(2,1)S(1)}, bf16[4,64,512]{2,1,0:T(8,128)(2,1)S(1)}, u32[]{:S(2)}, u32[]{:S(2)}) collective-permute-start(bf16[4,64,512]{2,1,0:T(8,128)(2,1)S(1)} %get-tuple-element.424), channel_id=1, source_target_pairs={{0,8},{8,0},{16,24},{24,16},{1,9},{9,1},{17,25},{25,17},{2,10},{10... | collective-permute-start | bytes 786440 | tf_op jit(solution)/shard_map/ppermute | solution.py:112
  262.7 2.5 add_convert_fusion.1
  265.2 4.7 %collective-permute-start.47 = (bf16[4,64,512]{2,1,0:T(8,128)(2,1)S(1)}, bf16[4,64,512]{2,1,0:T(8,128)(2,1)S(1)}, u32[]{:S(2)}, u32[]{:S(2)}) collective-permute-start(bf16[4,64,512]{2,1,0:T(8,128)(2,1)S(1)} %get-tuple-element.426), channel_id=1, source_target_pairs={{0,16},{8,24},{16,0},{24,8},{1,17},{9,25},{17,1},{25,9},{2,18},{10... | collective-permute-start | bytes 786440 | tf_op jit(solution)/shard_map/ppermute | solution.py:112
  269.9 1.3 collective-permute-start.40
  273.5 13.2 %collective-permute-done.47 = bf16[4,64,512]{2,1,0:T(8,128)(2,1)S(1)} collective-permute-done((bf16[4,64,512]{2,1,0:T(8,128)(2,1)S(1)}, bf16[4,64,512]{2,1,0:T(8,128)(2,1)S(1)}, u32[]{:S(2)}, u32[]{:S(2)}) %collective-permute-start.47) | collective-permute-done | bytes 262176 | tf_op jit(solution)/shard_map/ppermute | solution.py:112
  286.9 7.8 %collective-permute-done.41.p2 = bf16[1024,256]{1,0:T(8,128)(2,1)S(1)} collective-permute-done((bf16[1024,256]{1,0:T(8,128)(2,1)S(1)}, bf16[1024,256]{1,0:T(8,128)(2,1)S(1)}, u32[]{:S(2)}, u32[]{:S(2)}) %collective-permute-start.41) | collective-permute-done | bytes 524320 | tf_op jit(solution)/shard_map/ppermute | solution.py:72
  294.7 2.3 shard_map.400
  300.3 1.5 collective-permute-start.51
  301.8 2.0 multiply_reduce_fusion
  304.3 2.0 collective-permute-done.51
  309.1 3.5 collective-permute-start.53
  314.3 3.8 %collective-permute-done.54 = f32[8,256]{1,0:T(8,128)S(1)} collective-permute-done((f32[8,256]{1,0:T(8,128)S(1)}, f32[8,256]{1,0:T(8,128)S(1)}, u32[]{:S(2)}, u32[]{:S(2)}) %collective-permute-start.54) | collective-permute-done | bytes 8224 | tf_op jit(solution)/shard_map/ppermute | solution.py:100
  322.7 1.4 collective-permute-start.58
  327.4 1.5 collective-permute-start.61
  330.8 1.7 fusion.41
  334.4 1.4 copy.201
  335.8 1.4 copy.202
  341.2 2.0 fusion.42
  343.4 2.4 fusion.44
  (341 shorter events, 86.5 us)
Async XLA Ops:
  7.2 104.6 %all-gather.3.cloned.1.call-start = ((), (), s32[]{:S(2)}) async-start(), calls=%async_computation.2 | async-start | bytes 2949120 | tf_op jit(solution)/shard_map/all_gather | solution.py:829
  7.2 17.8 %collective-permute-start = (bf16[1024,256]{1,0:T(8,128)(2,1)}, bf16[1024,256]{1,0:T(8,128)(2,1)S(1)}, u32[]{:S(2)}, u32[]{:S(2)}) collective-permute-start(bf16[1024,256]{1,0:T(8,128)(2,1)} %x0.1), channel_id=1, source_target_pairs={{0,1},{1,0},{2,3},{3,2},{4,5},{5,4},{6,7},{7,6},{8,9},{9,8},{10,11... | collective-permute-start | bytes 1572872 | tf_op jit(solution)/shard_map/ppermute | solution.py:72
  10.2 16.1 %collective-permute-start.1 = (bf16[1024,256]{1,0:T(8,128)(2,1)}, bf16[1024,256]{1,0:T(8,128)(2,1)S(1)}, u32[]{:S(2)}, u32[]{:S(2)}) collective-permute-start(bf16[1024,256]{1,0:T(8,128)(2,1)} %x0.1), channel_id=1, source_target_pairs={{0,2},{1,3},{2,0},{3,1},{4,6},{5,7},{6,4},{7,5},{8,10},{9,11},{10,... | collective-permute-start | bytes 1572872 | tf_op jit(solution)/shard_map/ppermute | solution.py:72
  16.0 27.8 %collective-permute-start.4 = (bf16[528,256]{1,0:T(8,128)(2,1)}, bf16[528,256]{1,0:T(8,128)(2,1)}, u32[]{:S(2)}, u32[]{:S(2)}) collective-permute-start(bf16[528,256]{1,0:T(8,128)(2,1)} %get-tuple-element.472), channel_id=1, source_target_pairs={{0,1},{1,0},{2,3},{3,2},{4,5},{5,4},{6,7},{7,6},{8,9},{9,8},{10,11... | collective-permute-start | bytes 811016 | tf_op jit(solution)/shard_map/ppermute | solution.py:72
  16.5 28.7 %collective-permute-start.5 = (bf16[528,256]{1,0:T(8,128)(2,1)}, bf16[528,256]{1,0:T(8,128)(2,1)}, u32[]{:S(2)}, u32[]{:S(2)}) collective-permute-start(bf16[528,256]{1,0:T(8,128)(2,1)} %get-tuple-element.473), channel_id=1, source_target_pairs={{0,2},{1,3},{2,0},{3,1},{4,6},{5,7},{6,4},{7,5},{8,10},{9,11},{10,... | collective-permute-start | bytes 811016 | tf_op jit(solution)/shard_map/ppermute | solution.py:72
  16.6 28.7 %collective-permute-start.6 = (bf16[528,256]{1,0:T(8,128)(2,1)}, bf16[528,256]{1,0:T(8,128)(2,1)}, u32[]{:S(2)}, u32[]{:S(2)}) collective-permute-start(bf16[528,256]{1,0:T(8,128)(2,1)} %get-tuple-element.471), channel_id=1, source_target_pairs={{0,3},{1,2},{2,1},{3,0},{4,7},{5,6},{6,5},{7,4},{8,11},{9,10},{10,... | collective-permute-start | bytes 811016 | tf_op jit(solution)/shard_map/ppermute | solution.py:72
  25.9 15.2 %collective-permute-start.2 = (bf16[512,256]{1,0:T(8,128)(2,1)}, bf16[512,256]{1,0:T(8,128)(2,1)S(1)}, u32[]{:S(2)}, u32[]{:S(2)}) collective-permute-start(bf16[512,256]{1,0:T(8,128)(2,1)} %slice.285), channel_id=1, source_target_pairs={{0,2},{1,3},{2,0},{3,1},{4,6},{5,7},{6,4},{7,5},{8,10},{9,11},{10,... | collective-permute-start | bytes 786440 | tf_op jit(solution)/shard_map/ppermute | solution.py:72
  27.2 13.9 %collective-permute-start.3 = (bf16[512,256]{1,0:T(8,128)(2,1)}, bf16[512,256]{1,0:T(8,128)(2,1)S(1)}, u32[]{:S(2)}, u32[]{:S(2)}) collective-permute-start(bf16[512,256]{1,0:T(8,128)(2,1)} %slice.286), channel_id=1, source_target_pairs={{0,1},{1,0},{2,3},{3,2},{4,5},{5,4},{6,7},{7,6},{8,9},{9,8},{10,11... | collective-permute-start | bytes 786440 | tf_op jit(solution)/shard_map/ppermute | solution.py:72
  41.7 14.1 %collective-permute-start.21 = (bf16[3,96,256]{2,1,0:T(8,128)(2,1)S(1)}, bf16[3,96,256]{2,1,0:T(8,128)(2,1)S(1)}, u32[]{:S(2)}, u32[]{:S(2)}) collective-permute-start(bf16[3,96,256]{2,1,0:T(8,128)(2,1)S(1)} %get-tuple-element.196), channel_id=1, source_target_pairs={{0,1},{1,0},{2,3},{3,2},{4,5},{5,4},{6,7},{7,6},{8,9},{9,8},{10,11... | collective-permute-start | bytes 442376 | tf_op jit(solution)/shard_map/ppermute | solution.py:72
  42.1 13.7 %collective-permute-start.22 = (bf16[3,96,256]{2,1,0:T(8,128)(2,1)S(1)}, bf16[3,96,256]{2,1,0:T(8,128)(2,1)S(1)}, u32[]{:S(2)}, u32[]{:S(2)}) collective-permute-start(bf16[3,96,256]{2,1,0:T(8,128)(2,1)S(1)} %get-tuple-element.197), channel_id=1, source_target_pairs={{0,2},{1,3},{2,0},{3,1},{4,6},{5,7},{6,4},{7,5},{8,10},{9,11},{10,... | collective-permute-start | bytes 442376 | tf_op jit(solution)/shard_map/ppermute | solution.py:72
  43.8 12.0 %collective-permute-start.23 = (bf16[3,96,256]{2,1,0:T(8,128)(2,1)S(1)}, bf16[3,96,256]{2,1,0:T(8,128)(2,1)S(1)}, u32[]{:S(2)}, u32[]{:S(2)}) collective-permute-start(bf16[3,96,256]{2,1,0:T(8,128)(2,1)S(1)} %get-tuple-element.198), channel_id=1, source_target_pairs={{0,3},{1,2},{2,1},{3,0},{4,7},{5,6},{6,5},{7,4},{8,11},{9,10},{10,... | collective-permute-start | bytes 442376 | tf_op jit(solution)/shard_map/ppermute | solution.py:72
  56.7 240.3 %reduce-scatter.2.cloned.1.call-start = ((), (), s32[]{:S(2)}) async-start(), calls=%async_computation.1 | async-start | bytes 2949120 | tf_op jit(solution)/shard_map/reduce_scatter | solution.py:888
  56.8 6.1 %collective-permute-start.7 = (bf16[1024,1024]{1,0:T(8,128)(2,1)}, bf16[1024,1024]{1,0:T(8,128)(2,1)}, u32[]{:S(2)}, u32[]{:S(2)}) collective-permute-start(bf16[1024,1024]{1,0:T(8,128)(2,1)} %copy-done.12), channel_id=1, source_target_pairs={{0,4},{4,0},{1,5},{5,1},{2,6},{6,2},{3,7},{7,3},{8,12},{12,8},{9,1... | collective-permute-start | bytes 6291464 | tf_op jit(solution)/shard_map/ppermute | solution.py:76
  56.9 28.0 %collective-permute-start.11 = (bf16[4,528,256]{2,1,0:T(8,128)(2,1)S(1)}, bf16[4,528,256]{2,1,0:T(8,128)(2,1)S(1)}, u32[]{:S(2)}, u32[]{:S(2)}) collective-permute-start(bf16[4,528,256]{2,1,0:T(8,128)(2,1)S(1)} %pad_maximum_fusion.2.w_own.refs_1_.refs_2_), channel_id=1, source_target_pairs={{0,4},{4,0},{1,5},{5,1},{2,6},{6,2},{3,7},{7,3},{8,12},{12,8},{9,1... | collective-permute-start | bytes 3244040 | tf_op jit(solution)/shard_map/ppermute | solution.py:76
  57.4 27.5 %collective-permute-start.10 = (bf16[1024,256]{1,0:T(8,128)(2,1)S(1)}, bf16[1024,256]{1,0:T(8,128)(2,1)S(1)}, u32[]{:S(2)}, u32[]{:S(2)}) collective-permute-start(bf16[1024,256]{1,0:T(8,128)(2,1)S(1)} %copy-done.3), channel_id=1, source_target_pairs={{0,3},{1,2},{2,1},{3,0},{4,7},{5,6},{6,5},{7,4},{8,11},{9,10},{10,... | collective-permute-start | bytes 1572872 | tf_op jit(solution)/shard_map/ppermute | solution.py:72
  58.9 26.0 %collective-permute-start.8 = (bf16[1024,256]{1,0:T(8,128)(2,1)S(1)}, bf16[1024,256]{1,0:T(8,128)(2,1)}, u32[]{:S(2)}, u32[]{:S(2)}) collective-permute-start(bf16[1024,256]{1,0:T(8,128)(2,1)S(1)} %copy-done.3), channel_id=1, source_target_pairs={{0,1},{1,0},{2,3},{3,2},{4,5},{5,4},{6,7},{7,6},{8,9},{9,8},{10,11... | collective-permute-start | bytes 1572872 | tf_op jit(solution)/shard_map/ppermute | solution.py:72
  60.4 24.5 %collective-permute-start.9 = (bf16[1024,256]{1,0:T(8,128)(2,1)S(1)}, bf16[1024,256]{1,0:T(8,128)(2,1)}, u32[]{:S(2)}, u32[]{:S(2)}) collective-permute-start(bf16[1024,256]{1,0:T(8,128)(2,1)S(1)} %copy-done.3), channel_id=1, source_target_pairs={{0,2},{1,3},{2,0},{3,1},{4,6},{5,7},{6,4},{7,5},{8,10},{9,11},{10,... | collective-permute-start | bytes 1572872 | tf_op jit(solution)/shard_map/ppermute | solution.py:72
  84.9 1.6 collective-permute-start.12
  87.6 14.0 %collective-permute-start.15 = (bf16[256,1024]{1,0:T(8,128)(2,1)S(1)}, bf16[256,1024]{1,0:T(8,128)(2,1)S(1)}, u32[]{:S(2)}, u32[]{:S(2)}) collective-permute-start(bf16[256,1024]{1,0:T(8,128)(2,1)S(1)} %get-tuple-element.187), channel_id=1, source_target_pairs={{0,2},{1,3},{2,0},{3,1},{4,6},{5,7},{6,4},{7,5},{8,10},{9,11},{10,... | collective-permute-start | bytes 1572872 | tf_op jit(solution)/shard_map/ppermute | solution.py:72
  89.2 13.7 %collective-permute-start.13 = (bf16[256,1024]{1,0:T(8,128)(2,1)S(1)}, bf16[256,1024]{1,0:T(8,128)(2,1)S(1)}, u32[]{:S(2)}, u32[]{:S(2)}) collective-permute-start(bf16[256,1024]{1,0:T(8,128)(2,1)S(1)} %get-tuple-element.183), channel_id=1, source_target_pairs={{0,1},{1,0},{2,3},{3,2},{4,5},{5,4},{6,7},{7,6},{8,9},{9,8},{10,11... | collective-permute-start | bytes 1572872 | tf_op jit(solution)/shard_map/ppermute | solution.py:72
  101.8 7.7 %collective-permute-start.16 = (bf16[128,1024]{1,0:T(8,128)(2,1)S(1)}, bf16[128,1024]{1,0:T(8,128)(2,1)S(1)}, u32[]{:S(2)}, u32[]{:S(2)}) collective-permute-start(bf16[128,1024]{1,0:T(8,128)(2,1)S(1)} %get-tuple-element.190), channel_id=1, source_target_pairs={{0,1},{1,0},{2,3},{3,2},{4,5},{5,4},{6,7},{7,6},{8,9},{9,8},{10,11... | collective-permute-start | bytes 786440 | tf_op jit(solution)/shard_map/ppermute | solution.py:72
  103.8 7.3 %collective-permute-start.14 = (bf16[128,1024]{1,0:T(8,128)(2,1)S(1)}, bf16[128,1024]{1,0:T(8,128)(2,1)S(1)}, u32[]{:S(2)}, u32[]{:S(2)}) collective-permute-start(bf16[128,1024]{1,0:T(8,128)(2,1)S(1)} %get-tuple-element.186), channel_id=1, source_target_pairs={{0,2},{1,3},{2,0},{3,1},{4,6},{5,7},{6,4},{7,5},{8,10},{9,11},{10,... | collective-permute-start | bytes 786440 | tf_op jit(solution)/shard_map/ppermute | solution.py:72
  111.8 20.3 %collective-permute-start.24 = (bf16[4,1152,256]{2,1,0:T(8,128)(2,1)}, bf16[4,1152,256]{2,1,0:T(8,128)(2,1)S(1)}, u32[]{:S(2)}, u32[]{:S(2)}) collective-permute-start(bf16[4,1152,256]{2,1,0:T(8,128)(2,1)} %bitcast.155), channel_id=1, source_target_pairs={{0,4},{4,0},{1,5},{5,1},{2,6},{6,2},{3,7},{7,3},{8,12},{12,8},{9,1... | collective-permute-start | bytes 7077896 | tf_op jit(solution)/shard_map/ppermute | solution.py:76
  115.1 14.3 %collective-permute-start.17 = (bf16[256,1024]{1,0:T(8,128)(2,1)S(1)}, bf16[256,1024]{1,0:T(8,128)(2,1)S(1)}, u32[]{:S(2)}, u32[]{:S(2)}) collective-permute-start(bf16[256,1024]{1,0:T(8,128)(2,1)S(1)} %shard_map.388.refs_0_.mid), channel_id=1, source_target_pairs={{0,1},{1,0},{2,3},{3,2},{4,5},{5,4},{6,7},{7,6},{8,9},{9,8},{10,11... | collective-permute-start | bytes 1572872 | tf_op jit(solution)/shard_map/ppermute | solution.py:72
  116.2 14.6 %collective-permute-start.19 = (bf16[256,1024]{1,0:T(8,128)(2,1)S(1)}, bf16[256,1024]{1,0:T(8,128)(2,1)S(1)}, u32[]{:S(2)}, u32[]{:S(2)}) collective-permute-start(bf16[256,1024]{1,0:T(8,128)(2,1)S(1)} %shard_map.388.refs_0_.mid), channel_id=1, source_target_pairs={{0,2},{1,3},{2,0},{3,1},{4,6},{5,7},{6,4},{7,5},{8,10},{9,11},{10,... | collective-permute-start | bytes 1572872 | tf_op jit(solution)/shard_map/ppermute | solution.py:72
  129.4 20.9 %collective-permute-start.18 = (bf16[128,1024]{1,0:T(8,128)(2,1)S(1)}, bf16[128,1024]{1,0:T(8,128)(2,1)S(1)}, u32[]{:S(2)}, u32[]{:S(2)}) collective-permute-start(bf16[128,1024]{1,0:T(8,128)(2,1)S(1)} %slice.293), channel_id=1, source_target_pairs={{0,2},{1,3},{2,0},{3,1},{4,6},{5,7},{6,4},{7,5},{8,10},{9,11},{10,... | collective-permute-start | bytes 786440 | tf_op jit(solution)/shard_map/ppermute | solution.py:72
  130.9 19.4 %collective-permute-start.20 = (bf16[128,1024]{1,0:T(8,128)(2,1)S(1)}, bf16[128,1024]{1,0:T(8,128)(2,1)S(1)}, u32[]{:S(2)}, u32[]{:S(2)}) collective-permute-start(bf16[128,1024]{1,0:T(8,128)(2,1)S(1)} %slice.294), channel_id=1, source_target_pairs={{0,1},{1,0},{2,3},{3,2},{4,5},{5,4},{6,7},{7,6},{8,9},{9,8},{10,11... | collective-permute-start | bytes 786440 | tf_op jit(solution)/shard_map/ppermute | solution.py:72
  148.6 25.2 %collective-permute-start.26 = (bf16[256,1024]{1,0:T(8,128)(2,1)S(1)}, bf16[256,1024]{1,0:T(8,128)(2,1)S(1)}, u32[]{:S(2)}, u32[]{:S(2)}) collective-permute-start(bf16[256,1024]{1,0:T(8,128)(2,1)S(1)} %get-tuple-element.235), channel_id=1, source_target_pairs={{0,2},{1,3},{2,0},{3,1},{4,6},{5,7},{6,4},{7,5},{8,10},{9,11},{10,... | collective-permute-start | bytes 1572872 | tf_op jit(solution)/shard_map/ppermute | solution.py:72
  149.1 24.7 %collective-permute-start.25 = (bf16[256,1024]{1,0:T(8,128)(2,1)S(1)}, bf16[256,1024]{1,0:T(8,128)(2,1)S(1)}, u32[]{:S(2)}, u32[]{:S(2)}) collective-permute-start(bf16[256,1024]{1,0:T(8,128)(2,1)S(1)} %get-tuple-element.234), channel_id=1, source_target_pairs={{0,1},{1,0},{2,3},{3,2},{4,5},{5,4},{6,7},{7,6},{8,9},{9,8},{10,11... | collective-permute-start | bytes 1572872 | tf_op jit(solution)/shard_map/ppermute | solution.py:72
  155.9 14.6 %collective-permute-start.27 = (bf16[128,1024]{1,0:T(8,128)(2,1)S(1)}, bf16[128,1024]{1,0:T(8,128)(2,1)S(1)}, u32[]{:S(2)}, u32[]{:S(2)}) collective-permute-start(bf16[128,1024]{1,0:T(8,128)(2,1)S(1)} %get-tuple-element.236), channel_id=1, source_target_pairs={{0,3},{1,2},{2,1},{3,0},{4,7},{5,6},{6,5},{7,4},{8,11},{9,10},{10,... | collective-permute-start | bytes 786440 | tf_op jit(solution)/shard_map/ppermute | solution.py:72
  157.8 16.0 %collective-permute-start.28 = (bf16[128,1024]{1,0:T(8,128)(2,1)S(1)}, bf16[128,1024]{1,0:T(8,128)(2,1)S(1)}, u32[]{:S(2)}, u32[]{:S(2)}) collective-permute-start(bf16[128,1024]{1,0:T(8,128)(2,1)S(1)} %get-tuple-element.237), channel_id=1, source_target_pairs={{0,3},{1,2},{2,1},{3,0},{4,7},{5,6},{6,5},{7,4},{8,11},{9,10},{10,... | collective-permute-start | bytes 786440 | tf_op jit(solution)/shard_map/ppermute | solution.py:72
  177.2 11.7 %collective-permute-start.29 = (bf16[256,1024]{1,0:T(8,128)(2,1)S(1)}, bf16[256,1024]{1,0:T(8,128)(2,1)S(1)}, u32[]{:S(2)}, u32[]{:S(2)}) collective-permute-start(bf16[256,1024]{1,0:T(8,128)(2,1)S(1)} %get-tuple-element.238.refs_0_), channel_id=1, source_target_pairs={{0,1},{1,0},{2,3},{3,2},{4,5},{5,4},{6,7},{7,6},{8,9},{9,8},{10,11... | collective-permute-start | bytes 1572872 | tf_op jit(solution)/shard_map/ppermute | solution.py:72
  178.1 11.3 %collective-permute-start.30 = (bf16[256,1024]{1,0:T(8,128)(2,1)S(1)}, bf16[256,1024]{1,0:T(8,128)(2,1)S(1)}, u32[]{:S(2)}, u32[]{:S(2)}) collective-permute-start(bf16[256,1024]{1,0:T(8,128)(2,1)S(1)} %get-tuple-element.238.refs_0_), channel_id=1, source_target_pairs={{0,2},{1,3},{2,0},{3,1},{4,6},{5,7},{6,4},{7,5},{8,10},{9,11},{10,... | collective-permute-start | bytes 1572872 | tf_op jit(solution)/shard_map/ppermute | solution.py:72
  192.8 10.3 %collective-permute-start.31 = (bf16[1024,1152]{1,0:T(8,128)(2,1)S(1)}, bf16[1024,1152]{1,0:T(8,128)(2,1)S(1)}, u32[]{:S(2)}, u32[]{:S(2)}) collective-permute-start(bf16[1024,1152]{1,0:T(8,128)(2,1)S(1)} %pad_maximum_fusion), channel_id=1, source_target_pairs={{0,4},{4,0},{1,5},{5,1},{2,6},{6,2},{3,7},{7,3},{8,12},{12,8},{9,1... | collective-permute-start | bytes 7077896 | tf_op jit(solution)/shard_map/ppermute | solution.py:76
  192.9 8.8 %collective-permute-start.32 = (bf16[128,1024]{1,0:T(8,128)(2,1)S(1)}, bf16[128,1024]{1,0:T(8,128)(2,1)S(1)}, u32[]{:S(2)}, u32[]{:S(2)}) collective-permute-start(bf16[128,1024]{1,0:T(8,128)(2,1)S(1)} %slice.295), channel_id=1, source_target_pairs={{0,2},{1,3},{2,0},{3,1},{4,6},{5,7},{6,4},{7,5},{8,10},{9,11},{10,... | collective-permute-start | bytes 786440 | tf_op jit(solution)/shard_map/ppermute | solution.py:72
  193.7 8.6 %collective-permute-start.33 = (bf16[128,1024]{1,0:T(8,128)(2,1)S(1)}, bf16[128,1024]{1,0:T(8,128)(2,1)S(1)}, u32[]{:S(2)}, u32[]{:S(2)}) collective-permute-start(bf16[128,1024]{1,0:T(8,128)(2,1)S(1)} %slice.296), channel_id=1, source_target_pairs={{0,1},{1,0},{2,3},{3,2},{4,5},{5,4},{6,7},{7,6},{8,9},{9,8},{10,11... | collective-permute-start | bytes 786440 | tf_op jit(solution)/shard_map/ppermute | solution.py:72
  213.5 29.2 %collective-permute-start.35 = (bf16[1024,256]{1,0:T(8,128)(2,1)}, bf16[1024,256]{1,0:T(8,128)(2,1)}, u32[]{:S(2)}, u32[]{:S(2)}) collective-permute-start(bf16[1024,256]{1,0:T(8,128)(2,1)} %get-tuple-element.262), channel_id=1, source_target_pairs={{0,1},{1,0},{2,3},{3,2},{4,5},{5,4},{6,7},{7,6},{8,9},{9,8},{10,11... | collective-permute-start | bytes 1572872 | tf_op jit(solution)/shard_map/ppermute | solution.py:72
  214.7 28.0 %collective-permute-start.36 = (bf16[1024,256]{1,0:T(8,128)(2,1)}, bf16[1024,256]{1,0:T(8,128)(2,1)}, u32[]{:S(2)}, u32[]{:S(2)}) collective-permute-start(bf16[1024,256]{1,0:T(8,128)(2,1)} %get-tuple-element.263), channel_id=1, source_target_pairs={{0,2},{1,3},{2,0},{3,1},{4,6},{5,7},{6,4},{7,5},{8,10},{9,11},{10,... | collective-permute-start | bytes 1572872 | tf_op jit(solution)/shard_map/ppermute | solution.py:72
  215.8 26.9 %collective-permute-start.37 = (bf16[1024,256]{1,0:T(8,128)(2,1)}, bf16[1024,256]{1,0:T(8,128)(2,1)}, u32[]{:S(2)}, u32[]{:S(2)}) collective-permute-start(bf16[1024,256]{1,0:T(8,128)(2,1)} %get-tuple-element.264), channel_id=1, source_target_pairs={{0,3},{1,2},{2,1},{3,0},{4,7},{5,6},{6,5},{7,4},{8,11},{9,10},{10,... | collective-permute-start | bytes 1572872 | tf_op jit(solution)/shard_map/ppermute | solution.py:72
  217.0 1.9 collective-permute-start.34
  243.6 4.8 %collective-permute-start.45 = (bf16[1024,128]{1,0:T(8,128)(2,1)S(1)}, bf16[1024,128]{1,0:T(8,128)(2,1)S(1)}, u32[]{:S(2)}, u32[]{:S(2)}) collective-permute-start(bf16[1024,128]{1,0:T(8,128)(2,1)S(1)} %slice.361), channel_id=1, source_target_pairs={{0,4},{4,0},{1,5},{5,1},{2,6},{6,2},{3,7},{7,3},{8,12},{12,8},{9,1... | collective-permute-start | bytes 786440 | tf_op jit(solution)/shard_map/ppermute | solution.py:76
  243.8 4.9 %collective-permute-start.38 = (bf16[1024,384]{1,0:T(8,128)(2,1)S(1)}, bf16[1024,384]{1,0:T(8,128)(2,1)S(1)}, u32[]{:S(2)}, u32[]{:S(2)}) collective-permute-start(bf16[1024,384]{1,0:T(8,128)(2,1)S(1)} %get-tuple-element.271), channel_id=1, source_target_pairs={{0,4},{4,0},{1,5},{5,1},{2,6},{6,2},{3,7},{7,3},{8,12},{12,8},{9,1... | collective-permute-start | bytes 2359304 | tf_op jit(solution)/shard_map/ppermute | solution.py:76
  255.2 17.1 %collective-permute-start.46 = (bf16[4,64,512]{2,1,0:T(8,128)(2,1)S(1)}, bf16[4,64,512]{2,1,0:T(8,128)(2,1)S(1)}, u32[]{:S(2)}, u32[]{:S(2)}) collective-permute-start(bf16[4,64,512]{2,1,0:T(8,128)(2,1)S(1)} %get-tuple-element.424), channel_id=1, source_target_pairs={{0,8},{8,0},{16,24},{24,16},{1,9},{9,1},{17,25},{25,17},{2,10},{10... | collective-permute-start | bytes 786440 | tf_op jit(solution)/shard_map/ppermute | solution.py:112
  259.1 10.8 %collective-permute-start.39 = (f32[4,1024]{1,0:T(4,128)S(1)}, f32[4,1024]{1,0:T(4,128)S(1)}, u32[]{:S(2)}, u32[]{:S(2)}) collective-permute-start(f32[4,1024]{1,0:T(4,128)S(1)} %get-tuple-element.470), channel_id=1, source_target_pairs={{0,1},{1,0},{2,3},{3,2},{4,5},{5,4},{6,7},{7,6},{8,9},{9,8},{10,11... | collective-permute-start | bytes 49160 | tf_op jit(solution)/shard_map/ppermute | solution.py:72
  260.4 9.6 %collective-permute-start.43 = (f32[4,1024]{1,0:T(4,128)S(1)}, f32[4,1024]{1,0:T(4,128)S(1)}, u32[]{:S(2)}, u32[]{:S(2)}) collective-permute-start(f32[4,1024]{1,0:T(4,128)S(1)} %get-tuple-element.468), channel_id=1, source_target_pairs={{0,2},{1,3},{2,0},{3,1},{4,6},{5,7},{6,4},{7,5},{8,10},{9,11},{10,... | collective-permute-start | bytes 49160 | tf_op jit(solution)/shard_map/ppermute | solution.py:72
  261.5 9.7 %collective-permute-start.44 = (f32[4,1024]{1,0:T(4,128)S(1)}, f32[4,1024]{1,0:T(4,128)S(1)}, u32[]{:S(2)}, u32[]{:S(2)}) collective-permute-start(f32[4,1024]{1,0:T(4,128)S(1)} %get-tuple-element.469), channel_id=1, source_target_pairs={{0,3},{1,2},{2,1},{3,0},{4,7},{5,6},{6,5},{7,4},{8,11},{9,10},{10,... | collective-permute-start | bytes 49160 | tf_op jit(solution)/shard_map/ppermute | solution.py:72
  265.2 21.5 %collective-permute-start.47 = (bf16[4,64,512]{2,1,0:T(8,128)(2,1)S(1)}, bf16[4,64,512]{2,1,0:T(8,128)(2,1)S(1)}, u32[]{:S(2)}, u32[]{:S(2)}) collective-permute-start(bf16[4,64,512]{2,1,0:T(8,128)(2,1)S(1)} %get-tuple-element.426), channel_id=1, source_target_pairs={{0,16},{8,24},{16,0},{24,8},{1,17},{9,25},{17,1},{25,9},{2,18},{10... | collective-permute-start | bytes 786440 | tf_op jit(solution)/shard_map/ppermute | solution.py:112
  269.9 16.8 %collective-permute-start.48 = (bf16[4,64,512]{2,1,0:T(8,128)(2,1)S(1)}, bf16[4,64,512]{2,1,0:T(8,128)(2,1)S(1)}, u32[]{:S(2)}, u32[]{:S(2)}) collective-permute-start(bf16[4,64,512]{2,1,0:T(8,128)(2,1)S(1)} %get-tuple-element.425), channel_id=1, source_target_pairs={{0,24},{8,16},{16,8},{24,0},{1,25},{9,17},{17,9},{25,1},{2,26},{10... | collective-permute-start | bytes 786440 | tf_op jit(solution)/shard_map/ppermute | solution.py:112
  269.9 16.9 %collective-permute-start.40 = (bf16[1024,256]{1,0:T(8,128)(2,1)S(1)}, bf16[1024,256]{1,0:T(8,128)(2,1)S(1)}, u32[]{:S(2)}, u32[]{:S(2)}) collective-permute-start(bf16[1024,256]{1,0:T(8,128)(2,1)S(1)} %get-tuple-element.280), channel_id=1, source_target_pairs={{0,1},{1,0},{2,3},{3,2},{4,5},{5,4},{6,7},{7,6},{8,9},{9,8},{10,11... | collective-permute-start | bytes 1572872 | tf_op jit(solution)/shard_map/ppermute | solution.py:72
  271.2 23.5 %collective-permute-start.41 = (bf16[1024,256]{1,0:T(8,128)(2,1)S(1)}, bf16[1024,256]{1,0:T(8,128)(2,1)S(1)}, u32[]{:S(2)}, u32[]{:S(2)}) collective-permute-start(bf16[1024,256]{1,0:T(8,128)(2,1)S(1)} %get-tuple-element.281), channel_id=1, source_target_pairs={{0,2},{1,3},{2,0},{3,1},{4,6},{5,7},{6,4},{7,5},{8,10},{9,11},{10,... | collective-permute-start | bytes 1572872 | tf_op jit(solution)/shard_map/ppermute | solution.py:72
  272.4 22.4 %collective-permute-start.42 = (bf16[1024,256]{1,0:T(8,128)(2,1)S(1)}, bf16[1024,256]{1,0:T(8,128)(2,1)S(1)}, u32[]{:S(2)}, u32[]{:S(2)}) collective-permute-start(bf16[1024,256]{1,0:T(8,128)(2,1)S(1)} %get-tuple-element.282), channel_id=1, source_target_pairs={{0,3},{1,2},{2,1},{3,0},{4,7},{5,6},{6,5},{7,4},{8,11},{9,10},{10,... | collective-permute-start | bytes 1572872 | tf_op jit(solution)/shard_map/ppermute | solution.py:72
  298.2 5.5 %collective-permute-start.49 = (bf16[64,1152]{1,0:T(8,128)(2,1)S(1)}, bf16[64,1152]{1,0:T(8,128)(2,1)S(1)}, u32[]{:S(2)}, u32[]{:S(2)}) collective-permute-start(bf16[64,1152]{1,0:T(8,128)(2,1)S(1)} %get-tuple-element.438), channel_id=1, source_target_pairs={{0,1},{1,0},{2,3},{3,2},{4,5},{5,4},{6,7},{7,6},{8,9},{9,8},{10,11... | collective-permute-start | bytes 442376 | tf_op jit(solution)/shard_map/ppermute | solution.py:72
  299.2 5.1 %collective-permute-start.50 = (bf16[64,1152]{1,0:T(8,128)(2,1)S(1)}, bf16[64,1152]{1,0:T(8,128)(2,1)S(1)}, u32[]{:S(2)}, u32[]{:S(2)}) collective-permute-start(bf16[64,1152]{1,0:T(8,128)(2,1)S(1)} %get-tuple-element.437), channel_id=1, source_target_pairs={{0,2},{1,3},{2,0},{3,1},{4,6},{5,7},{6,4},{7,5},{8,10},{9,11},{10,... | collective-permute-start | bytes 442376 | tf_op jit(solution)/shard_map/ppermute | solution.py:72
  300.3 6.0 %collective-permute-start.51 = (bf16[64,1152]{1,0:T(8,128)(2,1)S(1)}, bf16[64,1152]{1,0:T(8,128)(2,1)S(1)}, u32[]{:S(2)}, u32[]{:S(2)}) collective-permute-start(bf16[64,1152]{1,0:T(8,128)(2,1)S(1)} %get-tuple-element.436), channel_id=1, source_target_pairs={{0,3},{1,2},{2,1},{3,0},{4,7},{5,6},{6,5},{7,4},{8,11},{9,10},{10,... | collective-permute-start | bytes 442376 | tf_op jit(solution)/shard_map/ppermute | solution.py:72
  308.5 5.1 %collective-permute-start.52 = (f32[8,256]{1,0:T(8,128)S(1)}, f32[8,256]{1,0:T(8,128)S(1)}, u32[]{:S(2)}, u32[]{:S(2)}) collective-permute-start(f32[8,256]{1,0:T(8,128)S(1)} %concatenate.86), channel_id=1, source_target_pairs={{0,8},{8,0},{16,24},{24,16},{1,9},{9,1},{17,25},{25,17},{2,10},{10... | collective-permute-start | bytes 24584 | tf_op jit(solution)/shard_map/ppermute | solution.py:100
  309.1 5.2 %collective-permute-start.53 = (f32[8,256]{1,0:T(8,128)S(1)}, f32[8,256]{1,0:T(8,128)S(1)}, u32[]{:S(2)}, u32[]{:S(2)}) collective-permute-start(f32[8,256]{1,0:T(8,128)S(1)} %concatenate.86), channel_id=1, source_target_pairs={{0,16},{8,24},{16,0},{24,8},{1,17},{9,25},{17,1},{25,9},{2,18},{10... | collective-permute-start | bytes 24584 | tf_op jit(solution)/shard_map/ppermute | solution.py:100
  312.6 5.4 %collective-permute-start.54 = (f32[8,256]{1,0:T(8,128)S(1)}, f32[8,256]{1,0:T(8,128)S(1)}, u32[]{:S(2)}, u32[]{:S(2)}) collective-permute-start(f32[8,256]{1,0:T(8,128)S(1)} %concatenate.86), channel_id=1, source_target_pairs={{0,24},{8,16},{16,8},{24,0},{1,25},{9,17},{17,9},{25,1},{2,26},{10... | collective-permute-start | bytes 24584 | tf_op jit(solution)/shard_map/ppermute | solution.py:100
  318.1 1.2 collective-permute-start.55
  320.6 6.8 %collective-permute-start.56 = (f32[8,128]{1,0:T(8,128)S(1)}, f32[8,128]{1,0:T(8,128)S(1)}, u32[]{:S(2)}, u32[]{:S(2)}) collective-permute-start(f32[8,128]{1,0:T(8,128)S(1)} %broadcast_in_dim.31), channel_id=1, source_target_pairs={{0,1},{1,0},{2,3},{3,2},{4,5},{5,4},{6,7},{7,6},{8,9},{9,8},{10,11... | collective-permute-start | bytes 12296 | tf_op jit(solution)/shard_map/ppermute | solution.py:72
  321.8 7.0 %collective-permute-start.57 = (f32[8,128]{1,0:T(8,128)S(1)}, f32[8,128]{1,0:T(8,128)S(1)}, u32[]{:S(2)}, u32[]{:S(2)}) collective-permute-start(f32[8,128]{1,0:T(8,128)S(1)} %broadcast_in_dim.31), channel_id=1, source_target_pairs={{0,2},{1,3},{2,0},{3,1},{4,6},{5,7},{6,4},{7,5},{8,10},{9,11},{10,... | collective-permute-start | bytes 12296 | tf_op jit(solution)/shard_map/ppermute | solution.py:72
  322.7 6.2 %collective-permute-start.58 = (f32[8,128]{1,0:T(8,128)S(1)}, f32[8,128]{1,0:T(8,128)S(1)}, u32[]{:S(2)}, u32[]{:S(2)}) collective-permute-start(f32[8,128]{1,0:T(8,128)S(1)} %broadcast_in_dim.31), channel_id=1, source_target_pairs={{0,3},{1,2},{2,1},{3,0},{4,7},{5,6},{6,5},{7,4},{8,11},{9,10},{10,... | collective-permute-start | bytes 12296 | tf_op jit(solution)/shard_map/ppermute | solution.py:72
  324.8 12.5 %collective-permute-start.59 = (bf16[64,512]{1,0:T(8,128)(2,1)}, bf16[64,512]{1,0:T(8,128)(2,1)S(1)}, u32[]{:S(2)}, u32[]{:S(2)}) collective-permute-start(bf16[64,512]{1,0:T(8,128)(2,1)} %get-tuple-element.448), channel_id=1, source_target_pairs={{0,1},{1,0},{2,3},{3,2},{4,5},{5,4},{6,7},{7,6},{8,9},{9,8},{10,11... | collective-permute-start | bytes 196616 | tf_op jit(solution)/shard_map/ppermute | solution.py:72
  326.0 11.2 %collective-permute-start.60 = (bf16[64,512]{1,0:T(8,128)(2,1)}, bf16[64,512]{1,0:T(8,128)(2,1)S(1)}, u32[]{:S(2)}, u32[]{:S(2)}) collective-permute-start(bf16[64,512]{1,0:T(8,128)(2,1)} %get-tuple-element.447), channel_id=1, source_target_pairs={{0,2},{1,3},{2,0},{3,1},{4,6},{5,7},{6,4},{7,5},{8,10},{9,11},{10,... | collective-permute-start | bytes 196616 | tf_op jit(solution)/shard_map/ppermute | solution.py:72
  327.4 9.9 %collective-permute-start.61 = (bf16[64,512]{1,0:T(8,128)(2,1)}, bf16[64,512]{1,0:T(8,128)(2,1)S(1)}, u32[]{:S(2)}, u32[]{:S(2)}) collective-permute-start(bf16[64,512]{1,0:T(8,128)(2,1)} %get-tuple-element.446), channel_id=1, source_target_pairs={{0,3},{1,2},{2,1},{3,0},{4,7},{5,6},{6,5},{7,4},{8,11},{9,10},{10,... | collective-permute-start | bytes 196616 | tf_op jit(solution)/shard_map/ppermute | solution.py:72
  (67 other events, 476.1 us)
Sparse Core Ops, SparseCore 0:
  56.9 50.7 all-gather.2
  205.2 50.8 reduce-scatter.1

commit v3 on v2

--- a/solution.py
+++ b/solution.py
@@ -21,7 +21,7 @@
 ADAM_EPSILON = 1e-08
 WEIGHT_DECAY = 0.01
 MASKED = -1e30
-SIZES = (1, 2, 3, 4, 6, 8)
+SIZES = (1, 2, 3, 4, 5, 6, 7, 8)
 
 BLOCK = 256
 LANES = 128
@@ -856,10 +856,15 @@
     ff_own = after(ff_own, x_second, y_second).reshape(4, 3 * ff_wide, 256)
     ff_oth = to_row(ff_own)
     m1, m2 = to_col(middle, 1), to_col(middle, 2)
-    m3a, m3b = to_col(m1[:128], 2), to_col(m2[128:], 1)
     held, backward = (), [None] * 4
-    for k, mids in enumerate(((middle,), (m1,), (m2,), (m3a, m3b))):
+    for k in range(4):
+        if k == 1:
+            r1, r2 = after((m1, m2), held[0])
+            m3a, m3b = to_col(r1[:128], 2), to_col(r2[128:], 1)
+        mids = ((middle,), (m1,), (m2,), (m3a, m3b))[k] if k else (middle,)
         held, part = run_ffn(k, index, mids, dys, gains, ff_own, ff_oth, held)
+        if k == 1:
+            part, m2 = after((part, m2), m3a, m3b)
         backward[k] = [to_col(v, k) for v in part] if k else part
     forward = held[:4]
     h2, hidden, dug, mid_here = held[4:]
@@ -919,7 +924,7 @@
 
     early = ffn_grad.astype(BF16)
     early = natural(exchange_col([early[k] for k in range(4)]), col)
-    late = after(late, early, *partial_first[1:])
+    late = after(late, *partial_first[1:])
     squares = jnp.sum(ffn_grad * ffn_grad) + jnp.sum(late * late)
     message = jnp.concatenate([note[2:, :256], jnp.full((6, 256), squares)], axis=0)
     message = sum_dp(message)
@@ -927,6 +932,7 @@
     gain_grad = message[:2]
     total = message[2:3, :LANES] + jnp.sum(gain_grad * gain_grad)
     total = jnp.broadcast_to(total, (8, LANES))
+    total, early = after((total, early), *early)
     total = sum(exchange_col([total] * 4))
     grad_norm = jnp.sqrt(total[0, 0])
     factor = CLIP_NORM / (grad_norm + 1e-06)

time: 360 us -> 351 us (0.975)
  waiting for transfers between devices: 98.3 us -> 92.9 us
  Pallas kernels: 87.9 us -> 91.7 us
    unnamed x139 -> x141, local copies, waits for them, and re-layouts: 26.2 us -> 28.5 us
  transfers between devices with their start and end apart: 64 -> 64, of which waited for: 21 -> 26; matrix products, arithmetic and copies ran while one was open for 12% -> 10% of each run, Pallas kernels for 24% -> 24%
where the time goes in v3:
time: 351 us; the launch traced here: 345 us
  waiting for transfers between devices  92.9 us (26%)
  Pallas kernels  91.7 us (26%)
  starting transfers between devices  66.5 us (19%)
  local copies, waits for them, and re-layouts  36.7 us (10%)
  other arithmetic  26.7 us (8%)
  between operations  19.4 us (6%)
  matrix products  11.2 us (3%)
    ppermute x47, waiting for transfers between devices, to_col(): return lax.ppermute(v, 'col', [(i, i ^ k) for i in range(4)])  71.8 us
    ppermute x47, starting transfers between devices, to_col(): return lax.ppermute(v, 'col', [(i, i ^ k) for i in range(4)])  54.9 us
    pallas_call x10, Pallas kernels, whole_call(): pl.pallas_call(body, out_shape=[jax.ShapeDtypeStruct(s, t) for s, t in ou...  45.8 us
    unnamed x141, local copies, waits for them, and re-layouts  28.5 us
    pallas_call x4, Pallas kernels, run_ffn(): pl.pallas_call(functools.partial(ffn_kernel, k), grid_spec=pltpu.Prefetch...  22.4 us
    ppermute x3, waiting for transfers between devices, scatter_dp(): lax.ppermute(piece(k), 'dp', [(i, i ^ k) for i in range(4)]).astype(F32)  11.9 us
    dot_general x7, matrix products, mm(): return lax.dot_general(a, b, dims, preferred_element_type=F32)  11.2 us
  transfers between devices with their start and end apart: 64, of which 26 were waited for; matrix products, arithmetic and copies ran while one was open for 10% of the time, Pallas kernels for 24%

profile of v3, /device:TPU:0, one launch (start us, length us, event | category | flops | bytes accessed | tf_op | source)
XLA Modules:
  0.0 345.1 jit_solution(7465104050301628075)
XLA Ops:
  7.2 3.0 collective-permute-start
  10.2 1.5 collective-permute-start.1
  16.6 2.9 collective-permute-start.6
  21.3 3.7 %fusion.5.table.table_from = f32[2048,128]{1,0:T(8,128)S(1)} fusion(f32[128]{0:T(128)S(1)} %fusion.33, f32[2048]{0:T(1024)S(1)} %fusion.26, pred[128]{0:T(512)(128)(4,1)S(1)} %broadcast_compare_fusion), kind=kLoop, calls=%fused_computation.19 | loop fusion | flops 524288 | bytes 1057408 | tf_op jit(solution)/shard_map/jit(_where)/select_n | solution.py:759
  28.3 2.9 fusion.2
  32.5 8.5 %collective-permute-done.2.x3a = bf16[512,256]{1,0:T(8,128)(2,1)S(1)} collective-permute-done((bf16[512,256]{1,0:T(8,128)(2,1)}, bf16[512,256]{1,0:T(8,128)(2,1)S(1)}, u32[]{:S(2)}, u32[]{:S(2)}) %collective-permute-start.2) | collective-permute-done | bytes 262176 | tf_op jit(solution)/shard_map/ppermute | solution.py:72
  42.1 1.7 collective-permute-start.20
  43.8 1.4 collective-permute-start.21
  47.7 4.2 %shard_map.381 = (bf16[1024,384]{1,0:T(8,128)(2,1)S(1)}, bf16[1024,1024]{1,0:T(8,128)(2,1)S(1)}, f32[1024,128]{1,0:T(8,128)S(1)}, bf16[256,1024]{1,0:T(8,128)(2,1)S(1)}) custom-call(s32[2]{0:T(128)S(1)} %pad_add_fusion.index, bf16[1024,256]{1,0:T(8,128)(2,1)S(1)} %copy-done.31, bf16[1024,256]{1,0:T(8,128)(2,1)S(1)} %collective-permute-done.x1, ...), custom_call_target="tpu_custom_call" | custom-call | flops 1024 | bytes 1024 | tf_op jit(solution)/shard_map/pallas_call | solution.py:201
  57.4 1.5 collective-permute-start.10
  58.9 1.5 collective-permute-start.8
  61.5 1.5 collective-permute-done.7.h
  64.2 4.5 %shard_map.382.recv = bf16[1024,384]{1,0:T(8,128)(2,1)S(1)} custom-call(s32[2]{0:T(128)S(1)} %pad_add_fusion.index, bf16[1024,1024]{1,0:T(8,128)(2,1)} %collective-permute-done.7.h, bf16[4,528,256]{2,1,0:T(8,128)(2,1)S(1)} %pad_maximum_fusion.2.w_own.refs_1_.refs_2_, f32[2048,128]{1,0:T(8,128)S(1)} %copy-done.5), custom_call_target="tpu_custom_call" | custom-call | flops 1024 | bytes 1024 | tf_op jit(solution)/shard_map/pallas_call | solution.py:230
  68.7 18.1 %shard_map.383 = (bf16[1024,128]{1,0:T(8,128)(2,1)S(1)}, bf16[1024,128]{1,0:T(8,128)(2,1)S(1)}, f32[2,2048]{1,0:T(2,128)S(1)}) custom-call(s32[5,8]{1,0:T(8,128)S(1)} %stack.115.info, f32[1,2048]{1,0:T(1,128)S(1)} %convert_element_type.146.seg, bf16[1024,384]{1,0:T(8,128)(2,1)S(1)} %copy-done.17, bf16[1024,384]{1,0:T(8,128)(2,1)S(1)} %shard_map.382.recv), custom_call_target="tpu_custom_call" | custom-call | flops 1024 | bytes 1024 | tf_op jit(solution)/shard_map/pallas_call | solution.py:58
  87.1 1.4 collective-permute-done.12.mix_oth
  89.5 1.6 collective-permute-start.15
  92.7 10.8 %collective-permute-done.15.got = bf16[256,1024]{1,0:T(8,128)(2,1)S(1)} collective-permute-done((bf16[256,1024]{1,0:T(8,128)(2,1)S(1)}, bf16[256,1024]{1,0:T(8,128)(2,1)S(1)}, u32[]{:S(2)}, u32[]{:S(2)}) %collective-permute-start.15) | collective-permute-done | bytes 524320 | tf_op jit(solution)/shard_map/ppermute | solution.py:72
  106.8 4.6 %collective-permute-done.16.got_b = bf16[128,1024]{1,0:T(8,128)(2,1)S(1)} collective-permute-done((bf16[128,1024]{1,0:T(8,128)(2,1)S(1)}, bf16[128,1024]{1,0:T(8,128)(2,1)S(1)}, u32[]{:S(2)}, u32[]{:S(2)}) %collective-permute-start.16) | collective-permute-done | bytes 262176 | tf_op jit(solution)/shard_map/ppermute | solution.py:72
  111.4 1.7 collective-permute-done.14.got_a
  118.0 1.5 collective-permute-start.18
  119.6 1.7 copy-done
  121.2 5.5 %shard_map.389 = (bf16[1024,256]{1,0:T(8,128)(2,1)S(1)}, bf16[1024,256]{1,0:T(8,128)(2,1)}, bf16[1024,256]{1,0:T(8,128)(2,1)}, bf16[1024,256]{1,0:T(8,128)(2,1)}...) custom-call(s32[2]{0:T(128)S(1)} %pad_add_fusion.index, ...), custom_call_target="tpu_custom_call" | custom-call | flops 1024 | bytes 1024 | tf_op jit(solution)/shard_map/pallas_call | solution.py:563
  126.7 4.6 %collective-permute-done.17.refs_0_ = bf16[256,1024]{1,0:T(8,128)(2,1)S(1)} collective-permute-done((bf16[256,1024]{1,0:T(8,128)(2,1)S(1)}, bf16[256,1024]{1,0:T(8,128)(2,1)S(1)}, u32[]{:S(2)}, u32[]{:S(2)}) %collective-permute-start.17) | collective-permute-done | bytes 524320 | tf_op jit(solution)/shard_map/ppermute | solution.py:72
  132.1 1.6 collective-permute-start.23
  134.6 5.5 %shard_map.390 = (bf16[1024,256]{1,0:T(8,128)(2,1)S(1)}, bf16[1024,256]{1,0:T(8,128)(2,1)}, bf16[1024,256]{1,0:T(8,128)(2,1)}, bf16[1024,256]{1,0:T(8,128)(2,1)}...) custom-call(s32[2]{0:T(128)S(1)} %pad_add_fusion.index, ...), custom_call_target="tpu_custom_call", output_to_operand_aliasing={{0}: (9, {}), {1}: (10, {}), {2}: (11, {}), {3}: (12, {}), ... | custom-call | flops 1024 | bytes 1024 | tf_op jit(solution)/shard_map/pallas_call | solution.py:563
  141.1 5.5 %shard_map.391 = (bf16[1024,256]{1,0:T(8,128)(2,1)S(1)}, bf16[1024,256]{1,0:T(8,128)(2,1)}, bf16[1024,256]{1,0:T(8,128)(2,1)}, bf16[1024,256]{1,0:T(8,128)(2,1)}...) custom-call(s32[2]{0:T(128)S(1)} %pad_add_fusion.index, ...), custom_call_target="tpu_custom_call", output_to_operand_aliasing={{0}: (9, {}), {1}: (10, {}), {2}: (11, {}), {3}: (12, {}), ... | custom-call | flops 1024 | bytes 1024 | tf_op jit(solution)/shard_map/pallas_call | solution.py:563
  148.1 6.0 %shard_map.392 = (bf16[1024,256]{1,0:T(8,128)(2,1)S(1)}, bf16[1024,256]{1,0:T(8,128)(2,1)}, bf16[1024,256]{1,0:T(8,128)(2,1)}, bf16[1024,256]{1,0:T(8,128)(2,1)}...) custom-call(s32[2]{0:T(128)S(1)} %pad_add_fusion.index, ...), custom_call_target="tpu_custom_call", output_to_operand_aliasing={{0}: (10, {}), {1}: (11, {}), {2}: (12, {}), {3}: (13, {}),... | custom-call | flops 1024 | bytes 1024 | tf_op jit(solution)/shard_map/pallas_call | solution.py:563
  154.1 2.0 collective-permute-start.27
  157.0 11.3 %collective-permute-done.27.p3a = bf16[128,1024]{1,0:T(8,128)(2,1)S(1)} collective-permute-done((bf16[128,1024]{1,0:T(8,128)(2,1)S(1)}, bf16[128,1024]{1,0:T(8,128)(2,1)S(1)}, u32[]{:S(2)}, u32[]{:S(2)}) %collective-permute-start.27) | collective-permute-done | bytes 262176 | tf_op jit(solution)/shard_map/ppermute | solution.py:72
  168.3 2.8 collective-permute-done.28.p3b
  171.1 3.4 shard_map.393
  178.4 7.0 %collective-permute-done.29.refs_0_ = bf16[256,1024]{1,0:T(8,128)(2,1)S(1)} collective-permute-done((bf16[256,1024]{1,0:T(8,128)(2,1)S(1)}, bf16[256,1024]{1,0:T(8,128)(2,1)S(1)}, u32[]{:S(2)}, u32[]{:S(2)}) %collective-permute-start.29) | collective-permute-done | bytes 524320 | tf_op jit(solution)/shard_map/ppermute | solution.py:72
  185.9 1.9 convolution_convert_fusion.1
  192.5 1.9 convolution_convert_fusion
  194.6 3.6 %collective-permute-done.32.refs_0_ = bf16[128,1024]{1,0:T(8,128)(2,1)S(1)} collective-permute-done((bf16[128,1024]{1,0:T(8,128)(2,1)S(1)}, bf16[128,1024]{1,0:T(8,128)(2,1)S(1)}, u32[]{:S(2)}, u32[]{:S(2)}) %collective-permute-start.32) | collective-permute-done | bytes 262176 | tf_op jit(solution)/shard_map/ppermute | solution.py:72
  200.1 1.4 copy-done.7
  202.6 1.5 shard_map.394
  204.1 1.5 shard_map.395
  205.6 1.5 shard_map.396
  207.1 1.5 shard_map.397
  213.5 1.9 collective-permute-done.34.dm_recv
  219.6 21.3 %shard_map.398 = (bf16[1024,384]{1,0:T(8,128)(2,1)S(1)}, bf16[1024,384]{1,0:T(8,128)(2,1)S(1)}) custom-call(s32[5,8]{1,0:T(8,128)S(1)} %stack.115.info, f32[1,2048]{1,0:T(1,128)S(1)} %convert_element_type.146.seg, f32[2,2048]{1,0:T(2,128)S(1)} %get-tuple-element.242.lse, bf16[1024,128]{1,0:T(8,128)(2,1)S(1)} %get-tuple-element.266.dm_own, ...), custom_call_target="tpu_custom_call" | custom-call | flops 1024 | bytes 1024 | tf_op jit(solution)/shard_map/pallas_call | solution.py:58
  242.3 2.9 fusion.58
  246.8 6.5 %shard_map.399 = (bf16[1024,256]{1,0:T(8,128)(2,1)S(1)}, bf16[1024,256]{1,0:T(8,128)(2,1)S(1)}, bf16[1024,256]{1,0:T(8,128)(2,1)S(1)}, bf16[1024,256]{1,0:T(8,12...) custom-call(bf16[1024,384]{1,0:T(8,128)(2,1)S(1)} %get-tuple-element.283.d_own, ...), custom_call_target="tpu_custom_call" | custom-call | flops 1024 | bytes 1024 | tf_op jit(solution)/shard_map/pallas_call | solution.py:697
  254.7 5.6 %collective-permute-start.47 = (bf16[4,64,512]{2,1,0:T(8,128)(2,1)S(1)}, bf16[4,64,512]{2,1,0:T(8,128)(2,1)S(1)}, u32[]{:S(2)}, u32[]{:S(2)}) collective-permute-start(bf16[4,64,512]{2,1,0:T(8,128)(2,1)S(1)} %get-tuple-element.444), channel_id=1, source_target_pairs={{0,16},{8,24},{16,0},{24,8},{1,17},{9,25},{17,1},{25,9},{2,18},{10... | collective-permute-start | bytes 786440 | tf_op jit(solution)/shard_map/ppermute | solution.py:112
  262.4 3.7 %collective-permute-done.46 = bf16[4,64,512]{2,1,0:T(8,128)(2,1)S(1)} collective-permute-done((bf16[4,64,512]{2,1,0:T(8,128)(2,1)S(1)}, bf16[4,64,512]{2,1,0:T(8,128)(2,1)S(1)}, u32[]{:S(2)}, u32[]{:S(2)}) %collective-permute-start.46) | collective-permute-done | bytes 262176 | tf_op jit(solution)/shard_map/ppermute | solution.py:112
  266.1 2.0 collective-permute-start.42
  268.1 2.5 add_convert_fusion.1
  270.6 8.2 %collective-permute-done.47 = bf16[4,64,512]{2,1,0:T(8,128)(2,1)S(1)} collective-permute-done((bf16[4,64,512]{2,1,0:T(8,128)(2,1)S(1)}, bf16[4,64,512]{2,1,0:T(8,128)(2,1)S(1)}, u32[]{:S(2)}, u32[]{:S(2)}) %collective-permute-start.47) | collective-permute-done | bytes 262176 | tf_op jit(solution)/shard_map/ppermute | solution.py:112
  281.2 4.4 %collective-permute-done.42.p3 = bf16[1024,256]{1,0:T(8,128)(2,1)S(1)} collective-permute-done((bf16[1024,256]{1,0:T(8,128)(2,1)S(1)}, bf16[1024,256]{1,0:T(8,128)(2,1)S(1)}, u32[]{:S(2)}, u32[]{:S(2)}) %collective-permute-start.42) | collective-permute-done | bytes 524320 | tf_op jit(solution)/shard_map/ppermute | solution.py:72
  286.3 1.5 collective-permute-start.59
  290.0 2.3 shard_map.400
  292.3 1.9 collective-permute-done.61
  294.2 2.0 multiply_reduce_fusion
  297.8 3.9 %collective-permute-start.50 = (f32[8,256]{1,0:T(8,128)S(1)}, f32[8,256]{1,0:T(8,128)S(1)}, u32[]{:S(2)}, u32[]{:S(2)}) collective-permute-start(f32[8,256]{1,0:T(8,128)S(1)} %concatenate.86), channel_id=1, source_target_pairs={{0,16},{8,24},{16,0},{24,8},{1,17},{9,25},{17,1},{25,9},{2,18},{10... | collective-permute-start | bytes 24584 | tf_op jit(solution)/shard_map/ppermute | solution.py:100
  303.4 3.8 %collective-permute-done.51 = f32[8,256]{1,0:T(8,128)S(1)} collective-permute-done((f32[8,256]{1,0:T(8,128)S(1)}, f32[8,256]{1,0:T(8,128)S(1)}, u32[]{:S(2)}, u32[]{:S(2)}) %collective-permute-start.51) | collective-permute-done | bytes 8224 | tf_op jit(solution)/shard_map/ppermute | solution.py:100
  308.8 2.0 collective-permute-start.55
  312.1 1.9 collective-permute-done.53
  314.0 3.2 collective-permute-done.54
  322.4 1.7 collective-permute-done.58
  326.0 1.7 fusion.41
  327.7 1.4 copy.201
  329.2 1.4 copy.202
  334.5 2.4 fusion.44
  (343 shorter events, 85.6 us)
Async XLA Ops:
  7.2 106.6 %all-gather.3.cloned.1.call-start = ((), (), s32[]{:S(2)}) async-start(), calls=%async_computation.2 | async-start | bytes 2949120 | tf_op jit(solution)/shard_map/all_gather | solution.py:829
  7.2 17.8 %collective-permute-start = (bf16[1024,256]{1,0:T(8,128)(2,1)}, bf16[1024,256]{1,0:T(8,128)(2,1)S(1)}, u32[]{:S(2)}, u32[]{:S(2)}) collective-permute-start(bf16[1024,256]{1,0:T(8,128)(2,1)} %x0.1), channel_id=1, source_target_pairs={{0,1},{1,0},{2,3},{3,2},{4,5},{5,4},{6,7},{7,6},{8,9},{9,8},{10,11... | collective-permute-start | bytes 1572872 | tf_op jit(solution)/shard_map/ppermute | solution.py:72
  10.2 16.1 %collective-permute-start.1 = (bf16[1024,256]{1,0:T(8,128)(2,1)}, bf16[1024,256]{1,0:T(8,128)(2,1)S(1)}, u32[]{:S(2)}, u32[]{:S(2)}) collective-permute-start(bf16[1024,256]{1,0:T(8,128)(2,1)} %x0.1), channel_id=1, source_target_pairs={{0,2},{1,3},{2,0},{3,1},{4,6},{5,7},{6,4},{7,5},{8,10},{9,11},{10,... | collective-permute-start | bytes 1572872 | tf_op jit(solution)/shard_map/ppermute | solution.py:72
  16.0 27.8 %collective-permute-start.4 = (bf16[528,256]{1,0:T(8,128)(2,1)}, bf16[528,256]{1,0:T(8,128)(2,1)}, u32[]{:S(2)}, u32[]{:S(2)}) collective-permute-start(bf16[528,256]{1,0:T(8,128)(2,1)} %get-tuple-element.490), channel_id=1, source_target_pairs={{0,1},{1,0},{2,3},{3,2},{4,5},{5,4},{6,7},{7,6},{8,9},{9,8},{10,11... | collective-permute-start | bytes 811016 | tf_op jit(solution)/shard_map/ppermute | solution.py:72
  16.5 28.7 %collective-permute-start.5 = (bf16[528,256]{1,0:T(8,128)(2,1)}, bf16[528,256]{1,0:T(8,128)(2,1)}, u32[]{:S(2)}, u32[]{:S(2)}) collective-permute-start(bf16[528,256]{1,0:T(8,128)(2,1)} %get-tuple-element.491), channel_id=1, source_target_pairs={{0,2},{1,3},{2,0},{3,1},{4,6},{5,7},{6,4},{7,5},{8,10},{9,11},{10,... | collective-permute-start | bytes 811016 | tf_op jit(solution)/shard_map/ppermute | solution.py:72
  16.6 28.7 %collective-permute-start.6 = (bf16[528,256]{1,0:T(8,128)(2,1)}, bf16[528,256]{1,0:T(8,128)(2,1)}, u32[]{:S(2)}, u32[]{:S(2)}) collective-permute-start(bf16[528,256]{1,0:T(8,128)(2,1)} %get-tuple-element.489), channel_id=1, source_target_pairs={{0,3},{1,2},{2,1},{3,0},{4,7},{5,6},{6,5},{7,4},{8,11},{9,10},{10,... | collective-permute-start | bytes 811016 | tf_op jit(solution)/shard_map/ppermute | solution.py:72
  25.8 15.2 %collective-permute-start.2 = (bf16[512,256]{1,0:T(8,128)(2,1)}, bf16[512,256]{1,0:T(8,128)(2,1)S(1)}, u32[]{:S(2)}, u32[]{:S(2)}) collective-permute-start(bf16[512,256]{1,0:T(8,128)(2,1)} %slice.285), channel_id=1, source_target_pairs={{0,2},{1,3},{2,0},{3,1},{4,6},{5,7},{6,4},{7,5},{8,10},{9,11},{10,... | collective-permute-start | bytes 786440 | tf_op jit(solution)/shard_map/ppermute | solution.py:72
  27.1 13.9 %collective-permute-start.3 = (bf16[512,256]{1,0:T(8,128)(2,1)}, bf16[512,256]{1,0:T(8,128)(2,1)S(1)}, u32[]{:S(2)}, u32[]{:S(2)}) collective-permute-start(bf16[512,256]{1,0:T(8,128)(2,1)} %slice.286), channel_id=1, source_target_pairs={{0,1},{1,0},{2,3},{3,2},{4,5},{5,4},{6,7},{7,6},{8,9},{9,8},{10,11... | collective-permute-start | bytes 786440 | tf_op jit(solution)/shard_map/ppermute | solution.py:72
  41.7 14.1 %collective-permute-start.19 = (bf16[3,96,256]{2,1,0:T(8,128)(2,1)S(1)}, bf16[3,96,256]{2,1,0:T(8,128)(2,1)S(1)}, u32[]{:S(2)}, u32[]{:S(2)}) collective-permute-start(bf16[3,96,256]{2,1,0:T(8,128)(2,1)S(1)} %get-tuple-element.205), channel_id=1, source_target_pairs={{0,1},{1,0},{2,3},{3,2},{4,5},{5,4},{6,7},{7,6},{8,9},{9,8},{10,11... | collective-permute-start | bytes 442376 | tf_op jit(solution)/shard_map/ppermute | solution.py:72
  42.1 13.7 %collective-permute-start.20 = (bf16[3,96,256]{2,1,0:T(8,128)(2,1)S(1)}, bf16[3,96,256]{2,1,0:T(8,128)(2,1)S(1)}, u32[]{:S(2)}, u32[]{:S(2)}) collective-permute-start(bf16[3,96,256]{2,1,0:T(8,128)(2,1)S(1)} %get-tuple-element.206), channel_id=1, source_target_pairs={{0,2},{1,3},{2,0},{3,1},{4,6},{5,7},{6,4},{7,5},{8,10},{9,11},{10,... | collective-permute-start | bytes 442376 | tf_op jit(solution)/shard_map/ppermute | solution.py:72
  43.8 12.0 %collective-permute-start.21 = (bf16[3,96,256]{2,1,0:T(8,128)(2,1)S(1)}, bf16[3,96,256]{2,1,0:T(8,128)(2,1)S(1)}, u32[]{:S(2)}, u32[]{:S(2)}) collective-permute-start(bf16[3,96,256]{2,1,0:T(8,128)(2,1)S(1)} %get-tuple-element.207), channel_id=1, source_target_pairs={{0,3},{1,2},{2,1},{3,0},{4,7},{5,6},{6,5},{7,4},{8,11},{9,10},{10,... | collective-permute-start | bytes 442376 | tf_op jit(solution)/shard_map/ppermute | solution.py:72
  56.8 237.4 %reduce-scatter.2.cloned.1.call-start = ((), (), s32[]{:S(2)}) async-start(), calls=%async_computation.1 | async-start | bytes 2949120 | tf_op jit(solution)/shard_map/reduce_scatter | solution.py:893
  56.8 6.1 %collective-permute-start.7 = (bf16[1024,1024]{1,0:T(8,128)(2,1)}, bf16[1024,1024]{1,0:T(8,128)(2,1)}, u32[]{:S(2)}, u32[]{:S(2)}) collective-permute-start(bf16[1024,1024]{1,0:T(8,128)(2,1)} %copy-done.12), channel_id=1, source_target_pairs={{0,4},{4,0},{1,5},{5,1},{2,6},{6,2},{3,7},{7,3},{8,12},{12,8},{9,1... | collective-permute-start | bytes 6291464 | tf_op jit(solution)/shard_map/ppermute | solution.py:76
  56.9 30.0 %collective-permute-start.11 = (bf16[4,528,256]{2,1,0:T(8,128)(2,1)S(1)}, bf16[4,528,256]{2,1,0:T(8,128)(2,1)S(1)}, u32[]{:S(2)}, u32[]{:S(2)}) collective-permute-start(bf16[4,528,256]{2,1,0:T(8,128)(2,1)S(1)} %pad_maximum_fusion.2.w_own.refs_1_.refs_2_), channel_id=1, source_target_pairs={{0,4},{4,0},{1,5},{5,1},{2,6},{6,2},{3,7},{7,3},{8,12},{12,8},{9,1... | collective-permute-start | bytes 3244040 | tf_op jit(solution)/shard_map/ppermute | solution.py:76
  57.4 29.4 %collective-permute-start.10 = (bf16[1024,256]{1,0:T(8,128)(2,1)S(1)}, bf16[1024,256]{1,0:T(8,128)(2,1)S(1)}, u32[]{:S(2)}, u32[]{:S(2)}) collective-permute-start(bf16[1024,256]{1,0:T(8,128)(2,1)S(1)} %copy-done.3), channel_id=1, source_target_pairs={{0,3},{1,2},{2,1},{3,0},{4,7},{5,6},{6,5},{7,4},{8,11},{9,10},{10,... | collective-permute-start | bytes 1572872 | tf_op jit(solution)/shard_map/ppermute | solution.py:72
  58.9 28.0 %collective-permute-start.8 = (bf16[1024,256]{1,0:T(8,128)(2,1)S(1)}, bf16[1024,256]{1,0:T(8,128)(2,1)}, u32[]{:S(2)}, u32[]{:S(2)}) collective-permute-start(bf16[1024,256]{1,0:T(8,128)(2,1)S(1)} %copy-done.3), channel_id=1, source_target_pairs={{0,1},{1,0},{2,3},{3,2},{4,5},{5,4},{6,7},{7,6},{8,9},{9,8},{10,11... | collective-permute-start | bytes 1572872 | tf_op jit(solution)/shard_map/ppermute | solution.py:72
  60.4 26.5 %collective-permute-start.9 = (bf16[1024,256]{1,0:T(8,128)(2,1)S(1)}, bf16[1024,256]{1,0:T(8,128)(2,1)}, u32[]{:S(2)}, u32[]{:S(2)}) collective-permute-start(bf16[1024,256]{1,0:T(8,128)(2,1)S(1)} %copy-done.3), channel_id=1, source_target_pairs={{0,2},{1,3},{2,0},{3,1},{4,6},{5,7},{6,4},{7,5},{8,10},{9,11},{10,... | collective-permute-start | bytes 1572872 | tf_op jit(solution)/shard_map/ppermute | solution.py:72
  86.9 1.6 collective-permute-start.12
  89.5 14.0 %collective-permute-start.15 = (bf16[256,1024]{1,0:T(8,128)(2,1)S(1)}, bf16[256,1024]{1,0:T(8,128)(2,1)S(1)}, u32[]{:S(2)}, u32[]{:S(2)}) collective-permute-start(bf16[256,1024]{1,0:T(8,128)(2,1)S(1)} %get-tuple-element.196), channel_id=1, source_target_pairs={{0,2},{1,3},{2,0},{3,1},{4,6},{5,7},{6,4},{7,5},{8,10},{9,11},{10,... | collective-permute-start | bytes 1572872 | tf_op jit(solution)/shard_map/ppermute | solution.py:72
  91.1 13.7 %collective-permute-start.13 = (bf16[256,1024]{1,0:T(8,128)(2,1)S(1)}, bf16[256,1024]{1,0:T(8,128)(2,1)S(1)}, u32[]{:S(2)}, u32[]{:S(2)}) collective-permute-start(bf16[256,1024]{1,0:T(8,128)(2,1)S(1)} %get-tuple-element.192), channel_id=1, source_target_pairs={{0,1},{1,0},{2,3},{3,2},{4,5},{5,4},{6,7},{7,6},{8,9},{9,8},{10,11... | collective-permute-start | bytes 1572872 | tf_op jit(solution)/shard_map/ppermute | solution.py:72
  103.7 7.7 %collective-permute-start.16 = (bf16[128,1024]{1,0:T(8,128)(2,1)S(1)}, bf16[128,1024]{1,0:T(8,128)(2,1)S(1)}, u32[]{:S(2)}, u32[]{:S(2)}) collective-permute-start(bf16[128,1024]{1,0:T(8,128)(2,1)S(1)} %get-tuple-element.199), channel_id=1, source_target_pairs={{0,1},{1,0},{2,3},{3,2},{4,5},{5,4},{6,7},{7,6},{8,9},{9,8},{10,11... | collective-permute-start | bytes 786440 | tf_op jit(solution)/shard_map/ppermute | solution.py:72
  105.8 7.3 %collective-permute-start.14 = (bf16[128,1024]{1,0:T(8,128)(2,1)S(1)}, bf16[128,1024]{1,0:T(8,128)(2,1)S(1)}, u32[]{:S(2)}, u32[]{:S(2)}) collective-permute-start(bf16[128,1024]{1,0:T(8,128)(2,1)S(1)} %get-tuple-element.195), channel_id=1, source_target_pairs={{0,2},{1,3},{2,0},{3,1},{4,6},{5,7},{6,4},{7,5},{8,10},{9,11},{10,... | collective-permute-start | bytes 786440 | tf_op jit(solution)/shard_map/ppermute | solution.py:72
  113.8 5.8 %collective-permute-start.22 = (bf16[4,1152,256]{2,1,0:T(8,128)(2,1)}, bf16[4,1152,256]{2,1,0:T(8,128)(2,1)S(1)}, u32[]{:S(2)}, u32[]{:S(2)}) collective-permute-start(bf16[4,1152,256]{2,1,0:T(8,128)(2,1)} %bitcast.155), channel_id=1, source_target_pairs={{0,4},{4,0},{1,5},{5,1},{2,6},{6,2},{3,7},{7,3},{8,12},{12,8},{9,1... | collective-permute-start | bytes 7077896 | tf_op jit(solution)/shard_map/ppermute | solution.py:76
  116.9 14.4 %collective-permute-start.17 = (bf16[256,1024]{1,0:T(8,128)(2,1)S(1)}, bf16[256,1024]{1,0:T(8,128)(2,1)S(1)}, u32[]{:S(2)}, u32[]{:S(2)}) collective-permute-start(bf16[256,1024]{1,0:T(8,128)(2,1)S(1)} %shard_map.388.refs_0_.mid), channel_id=1, source_target_pairs={{0,1},{1,0},{2,3},{3,2},{4,5},{5,4},{6,7},{7,6},{8,9},{9,8},{10,11... | collective-permute-start | bytes 1572872 | tf_op jit(solution)/shard_map/ppermute | solution.py:72
  118.0 14.1 %collective-permute-start.18 = (bf16[256,1024]{1,0:T(8,128)(2,1)S(1)}, bf16[256,1024]{1,0:T(8,128)(2,1)S(1)}, u32[]{:S(2)}, u32[]{:S(2)}) collective-permute-start(bf16[256,1024]{1,0:T(8,128)(2,1)S(1)} %shard_map.388.refs_0_.mid), channel_id=1, source_target_pairs={{0,2},{1,3},{2,0},{3,1},{4,6},{5,7},{6,4},{7,5},{8,10},{9,11},{10,... | collective-permute-start | bytes 1572872 | tf_op jit(solution)/shard_map/ppermute | solution.py:72
  132.1 8.0 %collective-permute-start.23 = (bf16[128,1024]{1,0:T(8,128)(2,1)S(1)}, bf16[128,1024]{1,0:T(8,128)(2,1)S(1)}, u32[]{:S(2)}, u32[]{:S(2)}) collective-permute-start(bf16[128,1024]{1,0:T(8,128)(2,1)S(1)} %slice.233), channel_id=1, source_target_pairs={{0,2},{1,3},{2,0},{3,1},{4,6},{5,7},{6,4},{7,5},{8,10},{9,11},{10,... | collective-permute-start | bytes 786440 | tf_op jit(solution)/shard_map/ppermute | solution.py:72
  133.7 7.4 %collective-permute-start.24 = (bf16[128,1024]{1,0:T(8,128)(2,1)S(1)}, bf16[128,1024]{1,0:T(8,128)(2,1)S(1)}, u32[]{:S(2)}, u32[]{:S(2)}) collective-permute-start(bf16[128,1024]{1,0:T(8,128)(2,1)S(1)} %slice.234), channel_id=1, source_target_pairs={{0,1},{1,0},{2,3},{3,2},{4,5},{5,4},{6,7},{7,6},{8,9},{9,8},{10,11... | collective-permute-start | bytes 786440 | tf_op jit(solution)/shard_map/ppermute | solution.py:72
  146.6 24.5 %collective-permute-start.26 = (bf16[256,1024]{1,0:T(8,128)(2,1)S(1)}, bf16[256,1024]{1,0:T(8,128)(2,1)S(1)}, u32[]{:S(2)}, u32[]{:S(2)}) collective-permute-start(bf16[256,1024]{1,0:T(8,128)(2,1)S(1)} %get-tuple-element.248), channel_id=1, source_target_pairs={{0,2},{1,3},{2,0},{3,1},{4,6},{5,7},{6,4},{7,5},{8,10},{9,11},{10,... | collective-permute-start | bytes 1572872 | tf_op jit(solution)/shard_map/ppermute | solution.py:72
  147.1 24.0 %collective-permute-start.25 = (bf16[256,1024]{1,0:T(8,128)(2,1)S(1)}, bf16[256,1024]{1,0:T(8,128)(2,1)S(1)}, u32[]{:S(2)}, u32[]{:S(2)}) collective-permute-start(bf16[256,1024]{1,0:T(8,128)(2,1)S(1)} %get-tuple-element.247), channel_id=1, source_target_pairs={{0,1},{1,0},{2,3},{3,2},{4,5},{5,4},{6,7},{7,6},{8,9},{9,8},{10,11... | collective-permute-start | bytes 1572872 | tf_op jit(solution)/shard_map/ppermute | solution.py:72
  154.1 14.2 %collective-permute-start.27 = (bf16[128,1024]{1,0:T(8,128)(2,1)S(1)}, bf16[128,1024]{1,0:T(8,128)(2,1)S(1)}, u32[]{:S(2)}, u32[]{:S(2)}) collective-permute-start(bf16[128,1024]{1,0:T(8,128)(2,1)S(1)} %get-tuple-element.249), channel_id=1, source_target_pairs={{0,3},{1,2},{2,1},{3,0},{4,7},{5,6},{6,5},{7,4},{8,11},{9,10},{10,... | collective-permute-start | bytes 786440 | tf_op jit(solution)/shard_map/ppermute | solution.py:72
  156.1 15.0 %collective-permute-start.28 = (bf16[128,1024]{1,0:T(8,128)(2,1)S(1)}, bf16[128,1024]{1,0:T(8,128)(2,1)S(1)}, u32[]{:S(2)}, u32[]{:S(2)}) collective-permute-start(bf16[128,1024]{1,0:T(8,128)(2,1)S(1)} %get-tuple-element.250), channel_id=1, source_target_pairs={{0,3},{1,2},{2,1},{3,0},{4,7},{5,6},{6,5},{7,4},{8,11},{9,10},{10,... | collective-permute-start | bytes 786440 | tf_op jit(solution)/shard_map/ppermute | solution.py:72
  174.5 10.9 %collective-permute-start.29 = (bf16[256,1024]{1,0:T(8,128)(2,1)S(1)}, bf16[256,1024]{1,0:T(8,128)(2,1)S(1)}, u32[]{:S(2)}, u32[]{:S(2)}) collective-permute-start(bf16[256,1024]{1,0:T(8,128)(2,1)S(1)} %get-tuple-element.251.refs_0_), channel_id=1, source_target_pairs={{0,1},{1,0},{2,3},{3,2},{4,5},{5,4},{6,7},{7,6},{8,9},{9,8},{10,11... | collective-permute-start | bytes 1572872 | tf_op jit(solution)/shard_map/ppermute | solution.py:72
  175.4 10.6 %collective-permute-start.30 = (bf16[256,1024]{1,0:T(8,128)(2,1)S(1)}, bf16[256,1024]{1,0:T(8,128)(2,1)S(1)}, u32[]{:S(2)}, u32[]{:S(2)}) collective-permute-start(bf16[256,1024]{1,0:T(8,128)(2,1)S(1)} %get-tuple-element.251.refs_0_), channel_id=1, source_target_pairs={{0,2},{1,3},{2,0},{3,1},{4,6},{5,7},{6,4},{7,5},{8,10},{9,11},{10,... | collective-permute-start | bytes 1572872 | tf_op jit(solution)/shard_map/ppermute | solution.py:72
  189.3 10.3 %collective-permute-start.31 = (bf16[1024,1152]{1,0:T(8,128)(2,1)S(1)}, bf16[1024,1152]{1,0:T(8,128)(2,1)S(1)}, u32[]{:S(2)}, u32[]{:S(2)}) collective-permute-start(bf16[1024,1152]{1,0:T(8,128)(2,1)S(1)} %pad_maximum_fusion), channel_id=1, source_target_pairs={{0,4},{4,0},{1,5},{5,1},{2,6},{6,2},{3,7},{7,3},{8,12},{12,8},{9,1... | collective-permute-start | bytes 7077896 | tf_op jit(solution)/shard_map/ppermute | solution.py:76
  189.4 8.8 %collective-permute-start.32 = (bf16[128,1024]{1,0:T(8,128)(2,1)S(1)}, bf16[128,1024]{1,0:T(8,128)(2,1)S(1)}, u32[]{:S(2)}, u32[]{:S(2)}) collective-permute-start(bf16[128,1024]{1,0:T(8,128)(2,1)S(1)} %slice.293), channel_id=1, source_target_pairs={{0,2},{1,3},{2,0},{3,1},{4,6},{5,7},{6,4},{7,5},{8,10},{9,11},{10,... | collective-permute-start | bytes 786440 | tf_op jit(solution)/shard_map/ppermute | solution.py:72
  190.1 8.7 %collective-permute-start.33 = (bf16[128,1024]{1,0:T(8,128)(2,1)S(1)}, bf16[128,1024]{1,0:T(8,128)(2,1)S(1)}, u32[]{:S(2)}, u32[]{:S(2)}) collective-permute-start(bf16[128,1024]{1,0:T(8,128)(2,1)S(1)} %slice.294), channel_id=1, source_target_pairs={{0,1},{1,0},{2,3},{3,2},{4,5},{5,4},{6,7},{7,6},{8,9},{9,8},{10,11... | collective-permute-start | bytes 786440 | tf_op jit(solution)/shard_map/ppermute | solution.py:72
  210.0 30.8 %collective-permute-start.35 = (bf16[1024,256]{1,0:T(8,128)(2,1)}, bf16[1024,256]{1,0:T(8,128)(2,1)}, u32[]{:S(2)}, u32[]{:S(2)}) collective-permute-start(bf16[1024,256]{1,0:T(8,128)(2,1)} %get-tuple-element.275), channel_id=1, source_target_pairs={{0,1},{1,0},{2,3},{3,2},{4,5},{5,4},{6,7},{7,6},{8,9},{9,8},{10,11... | collective-permute-start | bytes 1572872 | tf_op jit(solution)/shard_map/ppermute | solution.py:72
  211.2 29.7 %collective-permute-start.36 = (bf16[1024,256]{1,0:T(8,128)(2,1)}, bf16[1024,256]{1,0:T(8,128)(2,1)}, u32[]{:S(2)}, u32[]{:S(2)}) collective-permute-start(bf16[1024,256]{1,0:T(8,128)(2,1)} %get-tuple-element.276), channel_id=1, source_target_pairs={{0,2},{1,3},{2,0},{3,1},{4,6},{5,7},{6,4},{7,5},{8,10},{9,11},{10,... | collective-permute-start | bytes 1572872 | tf_op jit(solution)/shard_map/ppermute | solution.py:72
  212.3 28.5 %collective-permute-start.37 = (bf16[1024,256]{1,0:T(8,128)(2,1)}, bf16[1024,256]{1,0:T(8,128)(2,1)}, u32[]{:S(2)}, u32[]{:S(2)}) collective-permute-start(bf16[1024,256]{1,0:T(8,128)(2,1)} %get-tuple-element.277), channel_id=1, source_target_pairs={{0,3},{1,2},{2,1},{3,0},{4,7},{5,6},{6,5},{7,4},{8,11},{9,10},{10,... | collective-permute-start | bytes 1572872 | tf_op jit(solution)/shard_map/ppermute | solution.py:72
  213.5 1.9 collective-permute-start.34
  241.7 4.8 %collective-permute-start.45 = (bf16[1024,128]{1,0:T(8,128)(2,1)S(1)}, bf16[1024,128]{1,0:T(8,128)(2,1)S(1)}, u32[]{:S(2)}, u32[]{:S(2)}) collective-permute-start(bf16[1024,128]{1,0:T(8,128)(2,1)S(1)} %slice.347), channel_id=1, source_target_pairs={{0,4},{4,0},{1,5},{5,1},{2,6},{6,2},{3,7},{7,3},{8,12},{12,8},{9,1... | collective-permute-start | bytes 786440 | tf_op jit(solution)/shard_map/ppermute | solution.py:76
  241.9 4.9 %collective-permute-start.38 = (bf16[1024,384]{1,0:T(8,128)(2,1)S(1)}, bf16[1024,384]{1,0:T(8,128)(2,1)S(1)}, u32[]{:S(2)}, u32[]{:S(2)}) collective-permute-start(bf16[1024,384]{1,0:T(8,128)(2,1)S(1)} %get-tuple-element.284), channel_id=1, source_target_pairs={{0,4},{4,0},{1,5},{5,1},{2,6},{6,2},{3,7},{7,3},{8,12},{12,8},{9,1... | collective-permute-start | bytes 2359304 | tf_op jit(solution)/shard_map/ppermute | solution.py:76
  253.3 12.7 %collective-permute-start.46 = (bf16[4,64,512]{2,1,0:T(8,128)(2,1)S(1)}, bf16[4,64,512]{2,1,0:T(8,128)(2,1)S(1)}, u32[]{:S(2)}, u32[]{:S(2)}) collective-permute-start(bf16[4,64,512]{2,1,0:T(8,128)(2,1)S(1)} %get-tuple-element.442), channel_id=1, source_target_pairs={{0,8},{8,0},{16,24},{24,16},{1,9},{9,1},{17,25},{25,17},{2,10},{10... | collective-permute-start | bytes 786440 | tf_op jit(solution)/shard_map/ppermute | solution.py:112
  253.5 6.9 %collective-permute-start.39 = (f32[4,1024]{1,0:T(4,128)S(1)}, f32[4,1024]{1,0:T(4,128)S(1)}, u32[]{:S(2)}, u32[]{:S(2)}) collective-permute-start(f32[4,1024]{1,0:T(4,128)S(1)} %get-tuple-element.488), channel_id=1, source_target_pairs={{0,1},{1,0},{2,3},{3,2},{4,5},{5,4},{6,7},{7,6},{8,9},{9,8},{10,11... | collective-permute-start | bytes 49160 | tf_op jit(solution)/shard_map/ppermute | solution.py:72
  254.7 24.0 %collective-permute-start.47 = (bf16[4,64,512]{2,1,0:T(8,128)(2,1)S(1)}, bf16[4,64,512]{2,1,0:T(8,128)(2,1)S(1)}, u32[]{:S(2)}, u32[]{:S(2)}) collective-permute-start(bf16[4,64,512]{2,1,0:T(8,128)(2,1)S(1)} %get-tuple-element.444), channel_id=1, source_target_pairs={{0,16},{8,24},{16,0},{24,8},{1,17},{9,25},{17,1},{25,9},{2,18},{10... | collective-permute-start | bytes 786440 | tf_op jit(solution)/shard_map/ppermute | solution.py:112
  260.4 19.6 %collective-permute-start.48 = (bf16[4,64,512]{2,1,0:T(8,128)(2,1)S(1)}, bf16[4,64,512]{2,1,0:T(8,128)(2,1)S(1)}, u32[]{:S(2)}, u32[]{:S(2)}) collective-permute-start(bf16[4,64,512]{2,1,0:T(8,128)(2,1)S(1)} %get-tuple-element.443), channel_id=1, source_target_pairs={{0,24},{8,16},{16,8},{24,0},{1,25},{9,17},{17,9},{25,1},{2,26},{10... | collective-permute-start | bytes 786440 | tf_op jit(solution)/shard_map/ppermute | solution.py:112
  260.4 20.8 %collective-permute-start.40 = (bf16[1024,256]{1,0:T(8,128)(2,1)S(1)}, bf16[1024,256]{1,0:T(8,128)(2,1)S(1)}, u32[]{:S(2)}, u32[]{:S(2)}) collective-permute-start(bf16[1024,256]{1,0:T(8,128)(2,1)S(1)} %get-tuple-element.293), channel_id=1, source_target_pairs={{0,1},{1,0},{2,3},{3,2},{4,5},{5,4},{6,7},{7,6},{8,9},{9,8},{10,11... | collective-permute-start | bytes 1572872 | tf_op jit(solution)/shard_map/ppermute | solution.py:72
  261.2 20.0 %collective-permute-start.41 = (bf16[1024,256]{1,0:T(8,128)(2,1)S(1)}, bf16[1024,256]{1,0:T(8,128)(2,1)S(1)}, u32[]{:S(2)}, u32[]{:S(2)}) collective-permute-start(bf16[1024,256]{1,0:T(8,128)(2,1)S(1)} %get-tuple-element.294), channel_id=1, source_target_pairs={{0,2},{1,3},{2,0},{3,1},{4,6},{5,7},{6,4},{7,5},{8,10},{9,11},{10,... | collective-permute-start | bytes 1572872 | tf_op jit(solution)/shard_map/ppermute | solution.py:72
  266.1 19.5 %collective-permute-start.42 = (bf16[1024,256]{1,0:T(8,128)(2,1)S(1)}, bf16[1024,256]{1,0:T(8,128)(2,1)S(1)}, u32[]{:S(2)}, u32[]{:S(2)}) collective-permute-start(bf16[1024,256]{1,0:T(8,128)(2,1)S(1)} %get-tuple-element.295), channel_id=1, source_target_pairs={{0,3},{1,2},{2,1},{3,0},{4,7},{5,6},{6,5},{7,4},{8,11},{9,10},{10,... | collective-permute-start | bytes 1572872 | tf_op jit(solution)/shard_map/ppermute | solution.py:72
  278.8 11.1 %collective-permute-start.43 = (f32[4,1024]{1,0:T(4,128)S(1)}, f32[4,1024]{1,0:T(4,128)S(1)}, u32[]{:S(2)}, u32[]{:S(2)}) collective-permute-start(f32[4,1024]{1,0:T(4,128)S(1)} %get-tuple-element.486), channel_id=1, source_target_pairs={{0,2},{1,3},{2,0},{3,1},{4,6},{5,7},{6,4},{7,5},{8,10},{9,11},{10,... | collective-permute-start | bytes 49160 | tf_op jit(solution)/shard_map/ppermute | solution.py:72
  279.9 10.0 %collective-permute-start.44 = (f32[4,1024]{1,0:T(4,128)S(1)}, f32[4,1024]{1,0:T(4,128)S(1)}, u32[]{:S(2)}, u32[]{:S(2)}) collective-permute-start(f32[4,1024]{1,0:T(4,128)S(1)} %get-tuple-element.487), channel_id=1, source_target_pairs={{0,3},{1,2},{2,1},{3,0},{4,7},{5,6},{6,5},{7,4},{8,11},{9,10},{10,... | collective-permute-start | bytes 49160 | tf_op jit(solution)/shard_map/ppermute | solution.py:72
  286.3 5.9 %collective-permute-start.59 = (bf16[64,512]{1,0:T(8,128)(2,1)S(1)}, bf16[64,512]{1,0:T(8,128)(2,1)S(1)}, u32[]{:S(2)}, u32[]{:S(2)}) collective-permute-start(bf16[64,512]{1,0:T(8,128)(2,1)S(1)} %get-tuple-element.466), channel_id=1, source_target_pairs={{0,1},{1,0},{2,3},{3,2},{4,5},{5,4},{6,7},{7,6},{8,9},{9,8},{10,11... | collective-permute-start | bytes 196616 | tf_op jit(solution)/shard_map/ppermute | solution.py:72
  287.8 4.4 %collective-permute-start.60 = (bf16[64,512]{1,0:T(8,128)(2,1)S(1)}, bf16[64,512]{1,0:T(8,128)(2,1)S(1)}, u32[]{:S(2)}, u32[]{:S(2)}) collective-permute-start(bf16[64,512]{1,0:T(8,128)(2,1)S(1)} %get-tuple-element.465), channel_id=1, source_target_pairs={{0,2},{1,3},{2,0},{3,1},{4,6},{5,7},{6,4},{7,5},{8,10},{9,11},{10,... | collective-permute-start | bytes 196616 | tf_op jit(solution)/shard_map/ppermute | solution.py:72
  289.0 5.2 %collective-permute-start.61 = (bf16[64,512]{1,0:T(8,128)(2,1)S(1)}, bf16[64,512]{1,0:T(8,128)(2,1)S(1)}, u32[]{:S(2)}, u32[]{:S(2)}) collective-permute-start(bf16[64,512]{1,0:T(8,128)(2,1)S(1)} %get-tuple-element.464), channel_id=1, source_target_pairs={{0,3},{1,2},{2,1},{3,0},{4,7},{5,6},{6,5},{7,4},{8,11},{9,10},{10,... | collective-permute-start | bytes 196616 | tf_op jit(solution)/shard_map/ppermute | solution.py:72
  297.6 5.2 %collective-permute-start.49 = (f32[8,256]{1,0:T(8,128)S(1)}, f32[8,256]{1,0:T(8,128)S(1)}, u32[]{:S(2)}, u32[]{:S(2)}) collective-permute-start(f32[8,256]{1,0:T(8,128)S(1)} %concatenate.86), channel_id=1, source_target_pairs={{0,8},{8,0},{16,24},{24,16},{1,9},{9,1},{17,25},{25,17},{2,10},{10... | collective-permute-start | bytes 24584 | tf_op jit(solution)/shard_map/ppermute | solution.py:100
  297.8 5.5 %collective-permute-start.50 = (f32[8,256]{1,0:T(8,128)S(1)}, f32[8,256]{1,0:T(8,128)S(1)}, u32[]{:S(2)}, u32[]{:S(2)}) collective-permute-start(f32[8,256]{1,0:T(8,128)S(1)} %concatenate.86), channel_id=1, source_target_pairs={{0,16},{8,24},{16,0},{24,8},{1,17},{9,25},{17,1},{25,9},{2,18},{10... | collective-permute-start | bytes 24584 | tf_op jit(solution)/shard_map/ppermute | solution.py:100
  301.7 5.4 %collective-permute-start.51 = (f32[8,256]{1,0:T(8,128)S(1)}, f32[8,256]{1,0:T(8,128)S(1)}, u32[]{:S(2)}, u32[]{:S(2)}) collective-permute-start(f32[8,256]{1,0:T(8,128)S(1)} %concatenate.86), channel_id=1, source_target_pairs={{0,24},{8,16},{16,8},{24,0},{1,25},{9,17},{17,9},{25,1},{2,26},{10... | collective-permute-start | bytes 24584 | tf_op jit(solution)/shard_map/ppermute | solution.py:100
  307.2 3.6 %collective-permute-start.52 = (f32[8,256]{1,0:T(8,128)S(1)}, f32[8,256]{1,0:T(8,128)S(1)}, u32[]{:S(2)}, u32[]{:S(2)}) collective-permute-start(f32[8,256]{1,0:T(8,128)S(1)} %add_add_fusion), channel_id=1, source_target_pairs={{0,4},{4,0},{1,5},{5,1},{2,6},{6,2},{3,7},{7,3},{8,12},{12,8},{9,1... | collective-permute-start | bytes 24584 | tf_op jit(solution)/shard_map/ppermute | solution.py:76
  307.3 6.7 %collective-permute-start.53 = (bf16[64,1152]{1,0:T(8,128)(2,1)S(1)}, bf16[64,1152]{1,0:T(8,128)(2,1)S(1)}, u32[]{:S(2)}, u32[]{:S(2)}) collective-permute-start(bf16[64,1152]{1,0:T(8,128)(2,1)S(1)} %get-tuple-element.456), channel_id=1, source_target_pairs={{0,1},{1,0},{2,3},{3,2},{4,5},{5,4},{6,7},{7,6},{8,9},{9,8},{10,11... | collective-permute-start | bytes 442376 | tf_op jit(solution)/shard_map/ppermute | solution.py:72
  308.1 9.1 %collective-permute-start.54 = (bf16[64,1152]{1,0:T(8,128)(2,1)S(1)}, bf16[64,1152]{1,0:T(8,128)(2,1)S(1)}, u32[]{:S(2)}, u32[]{:S(2)}) collective-permute-start(bf16[64,1152]{1,0:T(8,128)(2,1)S(1)} %get-tuple-element.455), channel_id=1, source_target_pairs={{0,2},{1,3},{2,0},{3,1},{4,6},{5,7},{6,4},{7,5},{8,10},{9,11},{10,... | collective-permute-start | bytes 442376 | tf_op jit(solution)/shard_map/ppermute | solution.py:72
  308.8 8.4 %collective-permute-start.55 = (bf16[64,1152]{1,0:T(8,128)(2,1)S(1)}, bf16[64,1152]{1,0:T(8,128)(2,1)S(1)}, u32[]{:S(2)}, u32[]{:S(2)}) collective-permute-start(bf16[64,1152]{1,0:T(8,128)(2,1)S(1)} %get-tuple-element.454), channel_id=1, source_target_pairs={{0,3},{1,2},{2,1},{3,0},{4,7},{5,6},{6,5},{7,4},{8,11},{9,10},{10,... | collective-permute-start | bytes 442376 | tf_op jit(solution)/shard_map/ppermute | solution.py:72
  317.4 4.2 %collective-permute-start.56 = (f32[8,128]{1,0:T(8,128)S(1)}, f32[8,128]{1,0:T(8,128)S(1)}, u32[]{:S(2)}, u32[]{:S(2)}) collective-permute-start(f32[8,128]{1,0:T(8,128)S(1)} %broadcast_in_dim.31), channel_id=1, source_target_pairs={{0,1},{1,0},{2,3},{3,2},{4,5},{5,4},{6,7},{7,6},{8,9},{9,8},{10,11... | collective-permute-start | bytes 12296 | tf_op jit(solution)/shard_map/ppermute | solution.py:72
  318.7 3.6 %collective-permute-start.57 = (f32[8,128]{1,0:T(8,128)S(1)}, f32[8,128]{1,0:T(8,128)S(1)}, u32[]{:S(2)}, u32[]{:S(2)}) collective-permute-start(f32[8,128]{1,0:T(8,128)S(1)} %broadcast_in_dim.31), channel_id=1, source_target_pairs={{0,2},{1,3},{2,0},{3,1},{4,6},{5,7},{6,4},{7,5},{8,10},{9,11},{10,... | collective-permute-start | bytes 12296 | tf_op jit(solution)/shard_map/ppermute | solution.py:72
  319.6 4.5 %collective-permute-start.58 = (f32[8,128]{1,0:T(8,128)S(1)}, f32[8,128]{1,0:T(8,128)S(1)}, u32[]{:S(2)}, u32[]{:S(2)}) collective-permute-start(f32[8,128]{1,0:T(8,128)S(1)} %broadcast_in_dim.31), channel_id=1, source_target_pairs={{0,3},{1,2},{2,1},{3,0},{4,7},{5,6},{6,5},{7,4},{8,11},{9,10},{10,... | collective-permute-start | bytes 12296 | tf_op jit(solution)/shard_map/ppermute | solution.py:72
  (68 other events, 413.7 us)
Sparse Core Ops, SparseCore 0:
  56.9 50.7 all-gather.2
  201.7 49.3 reduce-scatter.1
